TPU v7x, 32 devices: a whole 2x2x4 slice. The times are simulated.
32 devices in a mesh: dp: 2 (over x), row: 4 (over y, core), col: 4 (over z).
Axes of the slice: x: 2, y: 2, z: 4, core: 2. Of those that a mesh axis runs over, the one named last changes fastest.
Arguments:
- tokens: bfloat16 [512, 8192], P(('dp', 'col'), 'row'), may hold values from -6 to 6
- cotangent: bfloat16 [512, 8192], P(('dp', 'col'), 'row'), may hold values from -6 to 6
- gate_blocks: bfloat16 [4, 4, 336, 128, 128], P('row', 'col'), may hold values from -0.09375 to 0.09375
- gate_index: int32 [4, 4, 336, 2], P('row', 'col'), may hold values from -1 to 27, as said below
- up_blocks: bfloat16 [4, 4, 336, 128, 128], P('row', 'col'), may hold values from -0.09375 to 0.09375
- up_index: int32 [4, 4, 336, 2], P('row', 'col'), may hold values from -1 to 27, as said below
- down_blocks: bfloat16 [4, 4, 336, 128, 128], P('row', 'col'), may hold values from -0.0625 to 0.0625
- down_index: int32 [4, 4, 336, 2], P('row', 'col'), may hold values from -1 to 27, as said below
Outputs:
- output: bfloat16 [512, 8192], P(('dp', 'col'), 'row')
- input_grad: bfloat16 [512, 8192], P(('dp', 'col'), 'row')
- gate_grad: bfloat16 [4, 4, 336, 128, 128], P('row', 'col')
- up_grad: bfloat16 [4, 4, 336, 128, 128], P('row', 'col')
- down_grad: bfloat16 [4, 4, 336, 128, 128], P('row', 'col')
Inputs may be any that keep to these rules, and one draw needn't show every extreme that they name: `gate_index`: in each tile the listed slots come first and name distinct positions, with a first entry below 16 and a second below 28; every slot after them holds -1 in both entries. A tile lists 112 to 336 blocks, and some tile lists exactly 336. `up_index`: as for gate_index, with a pattern of its own. `down_index`: as for gate_index with the entries' roles swapped: the first is below 28, the second below 16. A tile lists 112 to 336 blocks, and some tile lists exactly 336.
All inputs are finite; a program needn't handle non-finite values.
Results may differ from a plain program's by a relative error of at most 0.0059.
Values may be sent and summed in bfloat16 or wider, within the bound.
No kernel may reach another device: no remote copies, remote signals or barrier semaphores. Data moves between devices by JAX's collectives and lax.ppermute only.
A program may use at most 256 MiB of HBM per device.

v0:
```python
import math

import jax
import jax.numpy as jnp
from jax import lax
from jax.sharding import PartitionSpec as P

FF = 14336
BLK = 128


def one_hots(index_list, row_count, col_count):
    row_hot = (index_list[:, 0:1] == jnp.arange(row_count, dtype=jnp.int32)[None, :]).astype(
        jnp.bfloat16
    )
    col_hot = (index_list[:, 1:2] == jnp.arange(col_count, dtype=jnp.int32)[None, :]).astype(
        jnp.bfloat16
    )
    return (row_hot, col_hot)


def dense_tools(blocks, index_list, row_count, col_count):
    blocks = blocks[0, 0]
    listing = index_list[0, 0]
    row_hot, col_hot = one_hots(listing, row_count, col_count)
    listed = listing[:, 0] >= 0
    row_ids = jnp.maximum(listing[:, 0], 0)
    col_ids = jnp.maximum(listing[:, 1], 0)
    width = blocks.shape[1]
    dense = jnp.einsum(
        "kr,kc,kab->racb", row_hot, col_hot, blocks, preferred_element_type=jnp.float32
    )
    dense = dense.astype(jnp.bfloat16).reshape(row_count * width, col_count * width)

    def apply_tile(panel):
        return jnp.dot(panel, dense, preferred_element_type=jnp.float32)

    def apply_back(panel):
        return lax.dot_general(
            panel, dense, (((1,), (1,)), ((), ())), preferred_element_type=jnp.float32
        )

    def block_grads(left, right):
        full = lax.dot_general(
            left, right, (((0,), (0,)), ((), ())), preferred_element_type=jnp.float32
        )
        shaped = full.reshape(row_count, width, col_count, width).transpose(0, 2, 1, 3)
        picked = shaped[row_ids, col_ids]
        return jnp.where(listed[:, None, None], picked, jnp.float32(0.0))

    return (apply_tile, apply_back, block_grads)


def on_device(
    tokens, cotangent, gate_blocks, gate_index, up_blocks, up_index, down_blocks, down_index
):
    feat_count = tokens.shape[1] // BLK
    unit_count = FF // BLK // lax.axis_size("col")
    unit_width = unit_count * BLK
    panel_x, panel_d = (
        lax.all_gather(tokens, "col", axis=0, tiled=True),
        lax.all_gather(cotangent, "col", axis=0, tiled=True),
    )
    group_rows = panel_x.shape[0]
    scale = 1.0 / math.sqrt(group_rows * lax.axis_size("dp"))
    gate_fwd, gate_back, gate_grads = dense_tools(gate_blocks, gate_index, feat_count, unit_count)
    up_fwd, up_back, up_grads = dense_tools(up_blocks, up_index, feat_count, unit_count)
    down_fwd, down_back, down_grads = dense_tools(down_blocks, down_index, unit_count, feat_count)
    both = lax.psum_scatter(
        jnp.concatenate([gate_fwd(panel_x), up_fwd(panel_x)], axis=1),
        "row",
        scatter_dimension=0,
        tiled=True,
    )
    gate_part = both[:, :unit_width]
    up_part = both[:, unit_width:]
    hidden_part = (gate_part * jax.nn.sigmoid(gate_part) * up_part).astype(jnp.bfloat16)
    hidden_all = lax.all_gather(hidden_part, "row", axis=0, tiled=True)
    output = lax.psum_scatter(down_fwd(hidden_all), "col", scatter_dimension=0, tiled=True).astype(
        jnp.bfloat16
    )
    grad_hidden = lax.psum_scatter(down_back(panel_d), "row", scatter_dimension=0, tiled=True)
    sigma = jax.nn.sigmoid(gate_part)
    grad_gate = (grad_hidden * up_part * sigma * (1.0 + gate_part * (1.0 - sigma))).astype(
        jnp.bfloat16
    )
    grad_up = (grad_hidden * gate_part * sigma).astype(jnp.bfloat16)
    gate_grad_all, up_grad_all = (
        lax.all_gather(grad_gate, "row", axis=0, tiled=True),
        lax.all_gather(grad_up, "row", axis=0, tiled=True),
    )
    input_grad = lax.psum_scatter(
        gate_back(gate_grad_all) + up_back(up_grad_all), "col", scatter_dimension=0, tiled=True
    ).astype(jnp.bfloat16)
    gate_local = gate_grads(panel_x, gate_grad_all) * scale
    up_local = up_grads(panel_x, up_grad_all) * scale
    down_local = down_grads(hidden_all, panel_d) * scale
    gate_sum, up_sum, down_sum = (
        lax.psum(gate_local.astype(jnp.bfloat16), "dp").astype(jnp.float32),
        lax.psum(up_local.astype(jnp.bfloat16), "dp").astype(jnp.float32),
        lax.psum(down_local.astype(jnp.bfloat16), "dp").astype(jnp.float32),
    )
    gate_grad = gate_sum.astype(jnp.bfloat16).reshape(gate_blocks.shape)
    up_grad = up_sum.astype(jnp.bfloat16).reshape(up_blocks.shape)
    down_grad = down_sum.astype(jnp.bfloat16).reshape(down_blocks.shape)
    return (output, input_grad, gate_grad, up_grad, down_grad)


def solution(mesh):
    return jax.shard_map(
        on_device,
        mesh=mesh,
        in_specs=(
            P(("dp", "col"), "row"),
            P(("dp", "col"), "row"),
            P("row", "col", None, None, None),
            P("row", "col", None, None),
            P("row", "col", None, None, None),
            P("row", "col", None, None),
            P("row", "col", None, None, None),
            P("row", "col", None, None),
        ),
        out_specs=(
            P(("dp", "col"), "row"),
            P(("dp", "col"), "row"),
            P("row", "col", None, None, None),
            P("row", "col", None, None, None),
            P("row", "col", None, None, None),
        ),
        check_vma=False,
    )
```

profile of v0, /device:TPU:0, one launch (start us, length us, event | category | flops | bytes accessed | tf_op | source)
XLA Modules:
  0.0 1419.6 jit_solution(11388300764999956086)
XLA Ops:
  7.2 0.7 all-gather.10.cloned.1.call-update
  7.9 0.7 all-gather.6.cloned.1.call-update
  8.7 1.4 or_reduce_fusion
  10.1 1.4 or_reduce_fusion.1
  11.4 23.6 %convert_bitcast_fusion = bf16[28,128,16,128]{3,0,1,2:T(8,128)(2,1)} fusion(bf16[336,128,128]{2,1,0:T(8,128)(2,1)} %bitcast.141, f32[336,28]{0,1:T(8,128)S(1)} %fusion.62, f32[336,16]{0,1:T(8,128)S(1)} %fusion.65), kind=kOutput, calls=%fused_computation.7 | convolution fusion | flops 4939992064 | bytes 25749248 | tf_op jit(solution)/shard_map/kr,kc,kab->racb/dot_general | solution.py:30
  35.1 14.9 %copy.44 = bf16[28,128,16,128]{3,2,1,0:T(8,128)(2,1)} copy(bf16[28,128,16,128]{3,0,1,2:T(8,128)(2,1)} %convert_bitcast_fusion) | data formatting | bytes 29360128 | tf_op jit(solution)/shard_map/convert_element_type | solution.py:33
  50.0 11.5 fusion.42
  61.5 5.1 copy.55
  66.7 23.0 %convert_bitcast_fusion.1 = bf16[16,128,28,128]{3,0,1,2:T(8,128)(2,1)} fusion(bf16[336,128,128]{2,1,0:T(8,128)(2,1)} %bitcast.142, f32[336,16]{0,1:T(8,128)S(1)} %fusion.64, f32[336,28]{0,1:T(8,128)S(1)} %fusion.61), kind=kOutput, calls=%fused_computation.20 | convolution fusion | flops 4939992064 | bytes 25749248 | tf_op jit(solution)/shard_map/kr,kc,kab->racb/dot_general | solution.py:30
  89.7 21.8 %copy.40 = bf16[16,128,28,128]{1,0,3,2:T(8,128)(2,1)} copy(bf16[16,128,28,128]{3,0,1,2:T(8,128)(2,1)} %convert_bitcast_fusion.1) | data formatting | bytes 29360128 | tf_op jit(solution)/shard_map/convert_element_type | solution.py:33
  111.6 0.6 or_reduce_fusion.2
  112.2 23.4 %convert_bitcast_fusion.2 = bf16[16,128,28,128]{3,0,1,2:T(8,128)(2,1)} fusion(bf16[336,128,128]{2,1,0:T(8,128)(2,1)} %bitcast.143, f32[336,16]{0,1:T(8,128)S(1)} %fusion.63, f32[336,28]{0,1:T(8,128)S(1)} %fusion.60), kind=kOutput, calls=%fused_computation.21 | convolution fusion | flops 4939992064 | bytes 25749248 | tf_op jit(solution)/shard_map/kr,kc,kab->racb/dot_general | solution.py:30
  135.6 21.8 %copy.38 = bf16[16,128,28,128]{1,0,3,2:T(8,128)(2,1)} copy(bf16[16,128,28,128]{3,0,1,2:T(8,128)(2,1)} %convert_bitcast_fusion.2) | data formatting | bytes 29360128 | tf_op jit(solution)/shard_map/convert_element_type | solution.py:33
  157.4 11.7 fusion.39
  169.1 6.1 fusion.36
  175.2 6.7 pad_maximum_fusion
  181.9 8.4 copy.53
  190.3 68.1 %reduce-scatter.13.cloned.1.call-done = f32[64,7168]{1,0:T(8,128)} async-done(((f32[256,7168]{1,0:T(8,128)}), f32[64,7168]{1,0:T(8,128)}) %reduce-scatter.13.cloned.1.call-update) | async-done | bytes 1835024 | tf_op jit(solution)/shard_map/reduce_scatter | solution.py:69
  258.5 3.2 multiply_convert_fusion.4
  262.3 0.7 all-gather.12.cloned.1.call-update
  263.5 19.5 %all-gather.8.cloned.1.call-done = bf16[256,3584]{1,0:T(8,128)(2,1)} async-done(((bf16[64,3584]{1,0:T(8,128)(2,1)}), bf16[256,3584]{1,0:T(8,128)(2,1)}) %all-gather.8.cloned.1.call-update) | async-done | bytes 1835024 | tf_op jit(solution)/shard_map/all_gather | solution.py:78
  283.0 11.0 fusion.2
  295.8 10.3 all-gather.14.cloned.1.call-done
  306.2 7.8 fusion.4
  314.0 15.4 %all-gather.12.cloned.1.call-done = bf16[256,3584]{1,0:T(8,128)(2,1)} async-done(((bf16[64,3584]{1,0:T(8,128)(2,1)}), bf16[256,3584]{1,0:T(8,128)(2,1)}) %all-gather.12.cloned.1.call-update) | async-done | bytes 1835024 | tf_op jit(solution)/shard_map/all_gather | solution.py:89
  329.5 11.0 fusion.45
  340.7 13.5 convolution_bitcast_fusion.2
  354.3 11.7 convolution_bitcast_fusion.1
  365.9 11.7 convolution_bitcast_fusion
  377.7 26.0 %copy.60 = f32[448,8,16,128]{3,2,1,0:T(8,128)} copy(f32[448,8,16,128]{3,1,2,0:T(8,128)} %convolution_bitcast_fusion.2) | data formatting | bytes 58720256
  403.7 30.3 %copy.47 = f32[16,128,28,128]{3,1,2,0:T(8,128)} copy(f32[16,128,28,128]{1,0,3,2:T(8,128)} %bitcast.124) | data formatting | bytes 58720256 | tf_op jit(solution)/shard_map/reshape | solution.py:47
  434.0 25.9 %copy.61 = f32[448,8,16,128]{3,2,1,0:T(8,128)} copy(f32[448,8,16,128]{3,1,2,0:T(8,128)} %convolution_bitcast_fusion.1) | data formatting | bytes 58720256
  459.9 30.2 %copy.48 = f32[16,128,28,128]{3,1,2,0:T(8,128)} copy(f32[16,128,28,128]{1,0,3,2:T(8,128)} %bitcast.125) | data formatting | bytes 58720256 | tf_op jit(solution)/shard_map/reshape | solution.py:47
  490.1 15.3 %copy.62 = f32[448,8,16,128]{3,2,1,0:T(8,128)S(1)} copy(f32[448,8,16,128]{3,1,2,0:T(8,128)} %convolution_bitcast_fusion) | data formatting | bytes 58720256
  505.4 13.3 copy.114
  518.7 30.3 %gather_fusion = f32[336,128,128]{2,1,0:T(8,128)} fusion(f32[16,28,128,128]{3,2,1,0:T(8,128)} %bitcast.127, s32[336]{0:T(512)S(1)} %copy-done.3), kind=kCustom, calls=%fused_computation | custom fusion | bytes 44042880 | tf_op jit(solution)/shard_map/gather | solution.py:48
  549.0 30.4 %gather_fusion.1 = f32[336,128,128]{2,1,0:T(8,128)} fusion(f32[16,28,128,128]{3,2,1,0:T(8,128)} %bitcast.128, s32[336]{0:T(512)S(1)} %copy-done.2), kind=kCustom, calls=%fused_computation.1 | custom fusion | bytes 44042880 | tf_op jit(solution)/shard_map/gather | solution.py:48
  579.4 32.9 %gather_fusion.2 = f32[336,128,128]{2,1,0:T(8,128)} fusion(f32[28,16,128,128]{3,2,1,0:T(8,128)} %bitcast.129, s32[336]{0:T(512)S(1)} %copy-done.1), kind=kCustom, calls=%fused_computation.2 | custom fusion | bytes 44042880 | tf_op jit(solution)/shard_map/gather | solution.py:48
  612.4 14.8 %fusion.20 = bf16[1,1,336,128,128]{4,3,2,1,0:T(8,128)(2,1)} fusion(f32[336,128,128]{2,1,0:T(8,128)} %gather_fusion.2, pred[336]{0:T(512)(128)(4,1)S(1)} %copy-done.11), kind=kLoop, calls=%fused_computation.33 | loop fusion | flops 16515072 | bytes 33030480 | tf_op jit(solution)/shard_map/reshape | solution.py:105
  627.1 2.8 copy-done
  629.9 17.6 %fusion.18 = (bf16[1,1,336,128,128]{4,3,2,1,0:T(8,128)(2,1)}, bf16[1,1,336,128,128]{4,3,2,1,0:T(8,128)(2,1)}) fusion(f32[336,128,128]{2,1,0:T(8,128)} %gather_fusion, pred[336]{0:T(512)(128)(4,1)S(1)} %copy-done.12, f32[336,128,128]{2,1,0:T(8,128)S(1)} %copy-done, pred[336]{0:T(512)(128)(4,1)S(1)} %copy-done.13), kind=kLoop, calls=%fused_computation.31 | loop fusion | flops 33030144 | bytes 66060960 | tf_op jit(solution)/shard_map/reshape | solution.py:103
  647.5 1.8 convert_element_type.61
  649.3 1.8 convert_element_type.64
  651.1 738.8 %all-reduce.3.cloned.1.call-done = (bf16[1,1,336,128,128]{4,3,2,1,0:T(8,128)(2,1)}, bf16[1,1,336,128,128]{4,3,2,1,0:T(8,128)(2,1)}, bf16[1,1,336,128,128]{4,3,2,1,0:T(8,128)(2,1)}) async-done(((bf16[1,1,336,128,128]{4,3,2,1,0:T(8,128)(2,1)}, bf16[1,1,336,128,128]{4,3,2,1,0:T(8,128)(2,1)}, bf16[1,1,336,128,128]{4,3,2,1,0:T(8,128)(2,1)}), (bf16[1,1,336,128,128]{4,3,2,1,0:T(8,128)(2,1)}, ...) | async-done | bytes 33030160 | tf_op jit(solution)/shard_map/psum | solution.py:99
  1389.9 12.1 copy.118
  1402.0 5.4 copy.119
  1407.4 0.7 slice-done.2
  1408.1 4.3 copy.120
  (64 shorter events, 3.5 us)
Async XLA Ops:
  7.2 42.8 %all-gather.10.cloned.1.call-start = ((), (), s32[]{:S(2)}) async-start(), calls=%async_computation.7 | async-start | bytes 1310720 | tf_op jit(solution)/shard_map/all_gather | solution.py:62
  7.9 149.5 %all-gather.6.cloned.1.call-start = ((), (), s32[]{:S(2)}) async-start(), calls=%async_computation.4 | async-start | bytes 1310720 | tf_op jit(solution)/shard_map/all_gather | solution.py:61
  8.6 181.7 %reduce-scatter.15.cloned.1.call-start = ((), (), s32[]{:S(2)}) async-start(), calls=%async_computation.12 | async-start | bytes 4587520 | tf_op jit(solution)/shard_map/reduce_scatter | solution.py:82
  66.7 191.8 %reduce-scatter.13.cloned.1.call-start = ((), (), s32[]{:S(2)}) async-start(), calls=%async_computation.11 | async-start | bytes 9175040 | tf_op jit(solution)/shard_map/reduce_scatter | solution.py:69
  89.7 21.9 %copy-start.10 = (s32[1,1,336,2]{2,3,1,0:T(2,128)S(1)}, s32[1,1,336,2]{2,3,1,0:T(2,128)}, u32[]{:S(2)}) copy-start(s32[1,1,336,2]{2,3,1,0:T(2,128)} %param.11) | copy-start | bytes 8068
  157.4 11.7 copy-start.4
  157.4 11.7 copy-start.6
  190.3 92.7 %all-gather.8.cloned.1.call-start = ((), (), s32[]{:S(2)}) async-start(), calls=%async_computation.5 | async-start | bytes 2293760 | tf_op jit(solution)/shard_map/all_gather | solution.py:78
  261.7 44.4 %all-gather.14.cloned.1.call-start = ((), (), s32[]{:S(2)}) async-start(), calls=%async_computation.9 | async-start | bytes 2293760 | tf_op jit(solution)/shard_map/all_gather | solution.py:90
  262.3 67.2 %all-gather.12.cloned.1.call-start = ((), (), s32[]{:S(2)}) async-start(), calls=%async_computation.8 | async-start | bytes 2293760 | tf_op jit(solution)/shard_map/all_gather | solution.py:89
  263.1 384.5 %reduce-scatter.9.cloned.1.call-start = ((), (), s32[]{:S(2)}) async-start(), calls=%async_computation.6 | async-start | bytes 2621440 | tf_op jit(solution)/shard_map/reduce_scatter | solution.py:79
  294.1 355.2 %reduce-scatter.11.cloned.1.call-start = ((), (), s32[]{:S(2)}) async-start(), calls=%async_computation.10 | async-start | bytes 2621440 | tf_op jit(solution)/shard_map/reduce_scatter | solution.py:92
  340.5 13.7 copy-start.8
  340.5 1049.4 %all-reduce.3.cloned.1.call-start = ((), (), s32[]{:S(2)}) async-start(), calls=%async_computation.13 | async-start | bytes 66060288 | tf_op jit(solution)/shard_map/psum | solution.py:99
  354.3 11.7 copy-start.7
  354.3 11.7 copy-start.9
  505.4 13.3 copy-start.3
  518.7 30.3 %copy-start.2 = (s32[336]{0:T(512)S(1)}, s32[336]{0:T(512)}, u32[]{:S(2)}) copy-start(s32[336]{0:T(512)} %get-tuple-element.8) | copy-start | bytes 4036
  549.0 30.4 %copy-start.1 = (s32[336]{0:T(512)S(1)}, s32[336]{0:T(512)}, u32[]{:S(2)}) copy-start(s32[336]{0:T(512)} %get-tuple-element.5) | copy-start | bytes 4036
  579.4 32.9 %copy-start.11 = (pred[336]{0:T(512)(128)(4,1)S(1)}, pred[336]{0:T(512)(128)(4,1)}, u32[]{:S(2)}) copy-start(pred[336]{0:T(512)(128)(4,1)} %broadcast_compare_fusion) | copy-start | bytes 1012
  612.3 17.6 %copy-start = (f32[336,128,128]{2,1,0:T(8,128)S(1)}, f32[336,128,128]{2,1,0:T(8,128)}, u32[]{:S(2)}) copy-start(f32[336,128,128]{2,1,0:T(8,128)} %gather_fusion.1) | copy-start | bytes 66060292
  612.3 17.6 %copy-start.12 = (pred[336]{0:T(512)(128)(4,1)S(1)}, pred[336]{0:T(512)(128)(4,1)}, u32[]{:S(2)}) copy-start(pred[336]{0:T(512)(128)(4,1)} %broadcast_compare_fusion.2) | copy-start | bytes 1012
  612.3 17.6 %copy-start.13 = (pred[336]{0:T(512)(128)(4,1)S(1)}, pred[336]{0:T(512)(128)(4,1)}, u32[]{:S(2)}) copy-start(pred[336]{0:T(512)(128)(4,1)} %broadcast_compare_fusion.1) | copy-start | bytes 1012
  1389.9 12.1 copy-start.5
  1389.9 17.5 %slice-start = ((s8[11010048]{0:T(1024)(128)(4,1)}), s8[4194304]{0:T(1024)(128)(4,1)S(1)}, s32[]{:S(2)}) async-start(s8[11010048]{0:T(1024)(128)(4,1)} %bitcast.136), calls=%async_computation.14 | async-start | bytes 8388608
  1389.9 17.5 %slice-start.1 = ((s8[11010048]{0:T(1024)(128)(4,1)}), s8[4194304]{0:T(1024)(128)(4,1)S(1)}, s32[]{:S(2)}) async-start(s8[11010048]{0:T(1024)(128)(4,1)} %bitcast.136), calls=%async_computation.15 | async-start | bytes 8388608
  1402.0 6.1 slice-start.2
Sparse Core Ops, SparseCore 0:
  9.6 30.6 all-gather.9
  41.8 27.4 all-gather.5
  72.4 40.7 reduce-scatter.14
  190.4 68.0 reduce-scatter.12
  261.8 21.1 all-gather.7
  285.0 21.1 all-gather.13
  308.3 21.1 all-gather.11
  331.7 43.8 reduce-scatter.8
  378.0 43.1 reduce-scatter.10
  647.6 742.2 all-reduce.2
where the time goes:
time: 1430 us; the launch traced here: 1420 us
  waiting for transfers between devices  855 us (60%)
  local copies, waits for them, and re-layouts  332 us (23%)
  matrix products  166 us (12%)
  other arithmetic  50.9 us (4%)
  between operations  14.8 us (1%)
    psum x1, waiting for transfers between devices, on_device(): lax.psum(gate_local.astype(jnp.bfloat16), 'dp').astype(jnp.float32)  739 us
    unnamed x42, local copies, waits for them, and re-layouts  106 us
    gather x3, local copies, waits for them, and re-layouts, block_grads(): picked = shaped[row_ids, col_ids]  93.6 us
    reshape x3, local copies, waits for them, and re-layouts, block_grads(): full.reshape(row_count, width, col_count, width).transpose(0, 2, 1, 3)  73.8 us
    dot_general x3, matrix products, dense_tools(): jnp.einsum('kr,kc,kab->racb', row_hot, col_hot, blocks, preferred_element...  70 us
    reduce_scatter x1, waiting for transfers between devices, on_device(): lax.psum_scatter(jnp.concatenate([gate_fwd(panel_x), up_fwd(panel_x)], ax...  68.1 us
    convert_element_type x3, local copies, waits for them, and re-layouts, dense_tools(): dense.astype(jnp.bfloat16).reshape(row_count * width, col_count * width)  58.5 us
    dot_general x3, matrix products, block_grads(): lax.dot_general(left, right, (((0,), (0,)), ((), ())), preferred_element_...  36.9 us
  transfers between devices with their start and end apart: 10, of which 5 were waited for; matrix products, arithmetic and copies ran while one was open for 37% of the time, Pallas kernels for 0%

commit v1 on v0

v1 whole, which is shorter than its diff:
```python
import functools
import math

import jax
import jax.numpy as jnp
from jax import lax
from jax.experimental import pallas as pl
from jax.experimental.pallas import tpu as pltpu
from jax.sharding import PartitionSpec as P

BLK = 128
VMEM_LIMIT = 56 * 1024 * 1024
VM = pltpu.VMEM
SM = pltpu.SMEM


def params():
    return pltpu.CompilerParams(vmem_limit_bytes=VMEM_LIMIT)


def cost(flops, nbytes):
    return pl.CostEstimate(flops=int(flops), bytes_accessed=int(nbytes), transcendentals=0)


def tile_of(size, largest):
    tile = largest
    while size % tile:
        tile //= 2
    return tile


def nat_rows(core, half, rows):
    start = core * rows if half == 0 else (1 - core) * rows
    return pl.ds(pl.multiple_of(start, rows), rows)


def slot_table(index_list, first_count, second_count):
    listing = index_list[0, 0]
    flat = jnp.where(listing[:, 0] >= 0, listing[:, 0] * second_count + listing[:, 1], -1)
    slots = jnp.arange(1, flat.shape[0] + 1, dtype=jnp.int32)
    positions = jnp.arange(first_count * second_count, dtype=jnp.int32)
    hits = flat[None, :] == positions[:, None]
    table = jnp.sum(jnp.where(hits, slots[None, :], 0), axis=1) - 1
    count = jnp.sum((flat >= 0).astype(jnp.int32))
    return table, count.reshape(1)


def densify_kernel(cols, table_ref, blocks_ref, out_ref):
    row = pl.program_id(0)
    for j in range(cols):
        slot = table_ref[row * cols + j]
        block = blocks_ref[jnp.maximum(slot, 0)]
        out_ref[:, j * BLK : (j + 1) * BLK] = jnp.where(slot >= 0, block, jnp.zeros_like(block))


def densify(blocks, table, rows, cols):
    slots = blocks.shape[0]
    return pl.pallas_call(
        functools.partial(densify_kernel, cols),
        out_shape=jax.ShapeDtypeStruct((rows * BLK, cols * BLK), blocks.dtype),
        grid_spec=pltpu.PrefetchScalarGridSpec(
            num_scalar_prefetch=1,
            grid=(rows,),
            in_specs=[
                pl.BlockSpec(
                    (slots, BLK, BLK), lambda i, t: (0, 0, 0), pipeline_mode=pl.Buffered(1)
                )
            ],
            out_specs=pl.BlockSpec((BLK, cols * BLK), lambda i, t: (i, 0)),
        ),
        compiler_params=params(),
        cost_estimate=cost(0, (slots + rows * cols) * BLK * BLK * 2),
    )(table, blocks)


def project_kernel(transposed, core_ref, x_ref, w_ref, mine_ref, other_ref):
    half = x_ref.shape[0] // 2
    dims = (((1,), (1 if transposed else 0,)), ((), ()))
    full = lax.dot_general(x_ref[...], w_ref[...], dims, preferred_element_type=jnp.float32)
    first, second = full[:half], full[half:]
    is_first = core_ref[0] == 0
    mine_ref[...] = jnp.where(is_first, first, second)
    other_ref[...] = jnp.where(is_first, second, first).astype(jnp.bfloat16)


def project(core, x, dense, transposed):
    tokens, depth = x.shape
    width = dense.shape[0] if transposed else dense.shape[1]
    tile = tile_of(width, 512)
    if transposed:
        w_spec = pl.BlockSpec((tile, depth), lambda i, c: (i, 0))
    else:
        w_spec = pl.BlockSpec((depth, tile), lambda i, c: (0, i))
    out_spec = pl.BlockSpec((tokens // 2, tile), lambda i, c: (0, i))
    shape = (tokens // 2, width)
    return pl.pallas_call(
        functools.partial(project_kernel, transposed),
        out_shape=(
            jax.ShapeDtypeStruct(shape, jnp.float32),
            jax.ShapeDtypeStruct(shape, jnp.bfloat16),
        ),
        grid_spec=pltpu.PrefetchScalarGridSpec(
            num_scalar_prefetch=1,
            grid=(width // tile,),
            in_specs=[
                pl.BlockSpec((tokens, depth), lambda i, c: (0, 0), pipeline_mode=pl.Buffered(1)),
                w_spec,
            ],
            out_specs=(out_spec, out_spec),
        ),
        compiler_params=params(),
        cost_estimate=cost(2 * tokens * depth * width, 2 * depth * width),
    )(core, x, dense)


def back_kernel(transposed, pairs, chunks, core_ref, *refs):
    pieces = refs[: 2 * pairs]
    weights = refs[2 * pairs : 3 * pairs]
    outs = refs[3 * pairs :]
    half = pieces[0].shape[0]
    dims = (((1,), (1 if transposed else 0,)), ((), ()))
    total = None
    for p in range(pairs):
        panel = jnp.concatenate([pieces[2 * p][...], pieces[2 * p + 1][...]], axis=0)
        part = lax.dot_general(panel, weights[p][...], dims, preferred_element_type=jnp.float32)
        total = part if total is None else total + part
    is_first = core_ref[0] == 0
    first = jnp.where(is_first, total[:half], total[half:])
    second = jnp.where(is_first, total[half:], total[:half])
    rows = 2 * half // chunks
    for d in range(chunks):
        part, at = (first, d * rows) if d < chunks // 2 else (second, d * rows - half)
        outs[d][...] = part[at : at + rows].astype(outs[d].dtype)


def back(core, operands, chunks, transposed):
    pairs = len(operands)
    half, depth = operands[0][0].shape
    dense = operands[0][2]
    width = dense.shape[0] if transposed else dense.shape[1]
    tile = tile_of(width, 256)
    if transposed:
        w_spec = pl.BlockSpec((tile, depth), lambda i, c: (i, 0))
    else:
        w_spec = pl.BlockSpec((depth, tile), lambda i, c: (0, i))
    piece_spec = pl.BlockSpec((half, depth), lambda i, c: (0, 0), pipeline_mode=pl.Buffered(1))
    rows = 2 * half // chunks
    shapes = tuple(
        jax.ShapeDtypeStruct((rows, width), jnp.bfloat16 if d else jnp.float32)
        for d in range(chunks)
    )
    out_spec = pl.BlockSpec((rows, tile), lambda i, c: (0, i))
    args = [a for mine, other, _ in operands for a in (mine, other)]
    args += [dense for _, _, dense in operands]
    return pl.pallas_call(
        functools.partial(back_kernel, transposed, pairs, chunks),
        out_shape=shapes,
        grid_spec=pltpu.PrefetchScalarGridSpec(
            num_scalar_prefetch=1,
            grid=(width // tile,),
            in_specs=[piece_spec] * (2 * pairs) + [w_spec] * pairs,
            out_specs=(out_spec,) * chunks,
        ),
        compiler_params=params(),
        cost_estimate=cost(4 * half * depth * width * pairs, 2 * depth * width * pairs),
    )(core, *args)


def both_halves(core, ref, columns=slice(None)):
    half = ref.shape[0] // 2
    return [ref[nat_rows(core, h, half), columns] for h in (0, 1)]


def block_grad_kernel(groups, left_whole, scale, cols, table_ref, count_ref, core_ref, *refs):
    core = core_ref[0]
    n_left = groups if left_whole else 2 * groups
    lefts = refs[:n_left]
    rights = refs[n_left : 3 * groups]
    out_ref, store, turned, sem = refs[3 * groups :]
    slots = out_ref.shape[0]
    step = pl.program_id(0)
    height = lefts[0].shape[1]
    width = rights[0].shape[1]
    wide = tile_of(width, 256)
    if left_whole:
        pieces = [piece for ref in lefts for piece in both_halves(core, ref)]
    else:
        pieces = [ref[...] for ref in lefts]
    turned[...] = jnp.concatenate(pieces, axis=0).T
    for b in range(width // wide):
        span = slice(b * wide, (b + 1) * wide)
        if left_whole:
            panel = [ref[:, span] for ref in rights]
        else:
            panel = [piece for ref in rights for piece in both_halves(core, ref, span)]
        full = jnp.dot(
            turned[...], jnp.concatenate(panel, axis=0), preferred_element_type=jnp.float32
        )
        full = (full * scale).astype(jnp.bfloat16)
        for di in range(height // BLK):
            for dj in range(wide // BLK):
                position = (step * (height // BLK) + di) * cols + b * (wide // BLK) + dj
                slot = table_ref[position]
                block = full[di * BLK : (di + 1) * BLK, dj * BLK : (dj + 1) * BLK]
                store[jnp.where(slot < 0, slots, slot)] = block

    @pl.when(step == pl.num_programs(0) - 1)
    def _():
        def clear(slot, carry):
            store[slot] = jnp.zeros((BLK, BLK), jnp.bfloat16)
            return carry

        lax.fori_loop(count_ref[0], slots, clear, 0)
        copy = pltpu.make_async_copy(store.at[pl.ds(0, slots)], out_ref, sem)
        copy.start()
        copy.wait()


def block_grads(core, table, count, lefts, rights, left_whole, slots, scale):
    groups = len(lefts) if left_whole else len(rights)
    tokens = (lefts if left_whole else rights)[0].shape[0] * groups
    length, width = lefts[0].shape[1], rights[0].shape[1]
    tile = tile_of(length, 256)
    left_specs = [pl.BlockSpec((a.shape[0], tile), lambda i, *_: (0, i)) for a in lefts]
    right_specs = [
        pl.BlockSpec(a.shape, lambda i, *_: (0, 0), pipeline_mode=pl.Buffered(1)) for a in rights
    ]
    return pl.pallas_call(
        functools.partial(block_grad_kernel, groups, left_whole, scale, width // BLK),
        out_shape=jax.ShapeDtypeStruct((slots, BLK, BLK), jnp.bfloat16),
        grid_spec=pltpu.PrefetchScalarGridSpec(
            num_scalar_prefetch=3,
            grid=(length // tile,),
            in_specs=left_specs + right_specs,
            out_specs=pl.BlockSpec(memory_space=pl.ANY),
            scratch_shapes=[
                VM((slots + 1, BLK, BLK), jnp.bfloat16),
                VM((tile, tokens), jnp.bfloat16),
                pltpu.SemaphoreType.DMA,
            ],
        ),
        compiler_params=params(),
        cost_estimate=cost(2 * tokens * length * width, slots * BLK * BLK * 2),
    )(table, count, core, *lefts, *rights)


def shift(x, axis, by):
    n = lax.axis_size(axis)
    return lax.ppermute(x, axis, [(i, (i + by) % n) for i in range(n)])


def swap_cores(x):
    n = lax.axis_size("row")
    return lax.ppermute(x, "row", [(i, i ^ 1) for i in range(n)])


def add_up(parts):
    total = parts[0].astype(jnp.float32)
    for part in parts[1:]:
        total = total + part.astype(jnp.float32)
    return total


def gather_chunks(x):
    return jnp.concatenate(
        [x] + [shift(x, "col", d) for d in range(1, lax.axis_size("col"))], axis=0
    )


def scatter_chunks(chunks):
    parts = [chunks[0]] + [shift(chunk, "col", -d) for d, chunk in enumerate(chunks) if d]
    return add_up(parts).astype(jnp.bfloat16)


def row_sum(mine, other):
    pair = add_up([mine, swap_cores(other)])
    sent = pair.astype(jnp.bfloat16)
    n = lax.axis_size("row")
    return add_up([pair] + [shift(sent, "row", 2 * s) for s in range(1, n // 2)])


def other_groups(x):
    return [shift(x, "dp", s) for s in range(1, lax.axis_size("dp"))]


def halves_of_groups(mine, other):
    out = [mine, other]
    for far in other_groups(mine):
        out += [far, swap_cores(far)]
    return out


def on_device(
    tokens, cotangent, gate_blocks, gate_index, up_blocks, up_index, down_blocks, down_index
):
    n_col = lax.axis_size("col")
    core = lax.rem(lax.axis_index("row"), 2).astype(jnp.int32).reshape(1)
    feats = tokens.shape[1] // BLK
    units = 14336 // BLK // n_col
    slots = gate_blocks.shape[2]
    group_rows = tokens.shape[0] * n_col
    scale = 1.0 / math.sqrt(group_rows * lax.axis_size("dp"))

    gate_table, gate_count = slot_table(gate_index, feats, units)
    up_table, up_count = slot_table(up_index, feats, units)
    down_table, down_count = slot_table(down_index, units, feats)

    x_all = gather_chunks(tokens)
    c_all = gather_chunks(cotangent)
    w_gate = densify(gate_blocks[0, 0], gate_table, feats, units)
    w_up = densify(up_blocks[0, 0], up_table, feats, units)
    w_down = densify(down_blocks[0, 0], down_table, units, feats)

    gate = row_sum(*project(core, x_all, w_gate, False))
    up = row_sum(*project(core, x_all, w_up, False))
    grad_hidden = row_sum(*project(core, c_all, w_down, True))
    x_groups = [x_all] + other_groups(x_all)
    c_groups = [c_all] + other_groups(c_all)

    sigma = jax.nn.sigmoid(gate)
    hidden = (gate * sigma * up).astype(jnp.bfloat16)
    grad_gate = (grad_hidden * up * sigma * (1.0 + gate * (1.0 - sigma))).astype(jnp.bfloat16)
    grad_up = (grad_hidden * gate * sigma).astype(jnp.bfloat16)

    hidden_other = swap_cores(hidden)
    output = scatter_chunks(back(core, [(hidden, hidden_other, w_down)], n_col, False))
    gate_other, up_other = swap_cores(grad_gate), swap_cores(grad_up)
    input_grad = scatter_chunks(
        back(
            core,
            [(grad_gate, gate_other, w_gate), (grad_up, up_other, w_up)],
            n_col,
            True,
        )
    )
    down_grad = block_grads(
        core,
        down_table,
        down_count,
        halves_of_groups(hidden, hidden_other),
        c_groups,
        False,
        slots,
        scale,
    )
    gate_grad = block_grads(
        core,
        gate_table,
        gate_count,
        x_groups,
        halves_of_groups(grad_gate, gate_other),
        True,
        slots,
        scale,
    )
    up_grad = block_grads(
        core,
        up_table,
        up_count,
        x_groups,
        halves_of_groups(grad_up, up_other),
        True,
        slots,
        scale,
    )
    shape = gate_blocks.shape
    return (
        output,
        input_grad,
        gate_grad.reshape(shape),
        up_grad.reshape(shape),
        down_grad.reshape(shape),
    )


def solution(mesh):
    return jax.shard_map(
        on_device,
        mesh=mesh,
        in_specs=(
            P(("dp", "col"), "row"),
            P(("dp", "col"), "row"),
            P("row", "col", None, None, None),
            P("row", "col", None, None),
            P("row", "col", None, None, None),
            P("row", "col", None, None),
            P("row", "col", None, None, None),
            P("row", "col", None, None),
        ),
        out_specs=(
            P(("dp", "col"), "row"),
            P(("dp", "col"), "row"),
            P("row", "col", None, None, None),
            P("row", "col", None, None, None),
            P("row", "col", None, None, None),
        ),
        check_vma=False,
    )
```

time: 1430 us -> 313 us (0.22)
  waiting for transfers between devices: 855 us -> 95.2 us
  local copies, waits for them, and re-layouts: 332 us -> 8.08 us
  matrix products: 166 us -> 0 us
  Pallas kernels: 0 us -> 164 us
  other arithmetic: 50.9 us -> 9.34 us
  starting transfers between devices: 0.98 us -> 31.7 us
    psum x1 -> x0, waiting for transfers between devices: 739 us -> none  [on_device(): lax.psum(gate_local.astype(jnp.bfloat16), 'dp').astype(jnp.float32)]
    dot_general x12 -> x0, matrix products: 166 us -> none  [the longest x3 70 us: dense_tools(): jnp.einsum('kr,kc,kab->racb', row_hot, col_hot, blocks, preferred_element...]
    pallas_call x0 -> x11, Pallas kernels: none -> 164 us  [the longest x3 55.7 us: block_grads(): pl.pallas_call(functools.partial(block_grad_kernel, groups, left_whole, s...]
    unnamed x42 -> x48, local copies, waits for them, and re-layouts: 106 us -> 8.04 us
    ppermute x0 -> x29, waiting for transfers between devices: none -> 95.2 us  [the longest x20 95.1 us: shift(): return lax.ppermute(x, axis, [(i, (i + by) % n) for i in range(n)])]
    gather x3 -> x0, local copies, waits for them, and re-layouts: 93.6 us -> none  [block_grads(): picked = shaped[row_ids, col_ids]]
    reshape x3 -> x0, local copies, waits for them, and re-layouts: 73.8 us -> none  [block_grads(): full.reshape(row_count, width, col_count, width).transpose(0, 2, 1, 3)]
    reduce_scatter x4 -> x0, waiting for transfers between devices: 68.2 us -> none  [the longest x1 68.1 us: on_device(): lax.psum_scatter(jnp.concatenate([gate_fwd(panel_x), up_fwd(panel_x)], ax...]
  transfers between devices with their start and end apart: 10 -> 29, of which waited for: 5 -> 9; matrix products, arithmetic and copies ran while one was open for 37% -> 3% of each run, Pallas kernels for 0% -> 47%
where the time goes in v1:
time: 313 us; the launch traced here: 309 us
  Pallas kernels  164 us (52%)
  waiting for transfers between devices  95.2 us (30%)
  starting transfers between devices  31.7 us (10%)
  other arithmetic  9.34 us (3%)
  local copies, waits for them, and re-layouts  8.08 us (3%)
    ppermute x20, waiting for transfers between devices, shift(): return lax.ppermute(x, axis, [(i, (i + by) % n) for i in range(n)])  95.1 us
    pallas_call x3, Pallas kernels, block_grads(): pl.pallas_call(functools.partial(block_grad_kernel, groups, left_whole, s...  55.7 us
    pallas_call x3, Pallas kernels, densify(): pl.pallas_call(functools.partial(densify_kernel, cols), out_shape=jax.Sha...  48 us
    pallas_call x3, Pallas kernels, project(): pl.pallas_call(functools.partial(project_kernel, transposed), out_shape=(...  32.9 us
    ppermute x20, starting transfers between devices, shift(): return lax.ppermute(x, axis, [(i, (i + by) % n) for i in range(n)])  29.9 us
    pallas_call x2, Pallas kernels, back(): pl.pallas_call(functools.partial(back_kernel, transposed, pairs, chunks),...  27.4 us
    unnamed x48, local copies, waits for them, and re-layouts  8.04 us
  transfers between devices with their start and end apart: 29, of which 9 were waited for; matrix products, arithmetic and copies ran while one was open for 3% of the time, Pallas kernels for 47%

profile of v1, /device:TPU:0, one launch (start us, length us, event | category | flops | bytes accessed | tf_op | source)
XLA Modules:
  0.0 309.3 jit_solution(12281639255376415614)
XLA Ops:
  0.6 3.1 collective-permute-start.11
  3.7 2.6 collective-permute-start.12
  6.3 1.3 collective-permute-start.13
  8.7 1.0 constant_dynamic-update-slice_fusion.7
  9.6 1.0 constant_dynamic-update-slice_fusion.3
  10.6 0.8 fusion.5
  11.4 0.8 fusion.3
  14.2 18.6 %shard_map.123.refs_2_.w_ref = bf16[3584,2048]{1,0:T(8,128)(2,1)} custom-call(s32[448]{0:T(512)} %broadcast_add_fusion.table_ref, bf16[336,128,128]{2,1,0:T(8,128)(2,1)} %bitcast.13), custom_call_target="tpu_custom_call" | custom-call | bytes 25690112 | tf_op jit(solution)/shard_map/pallas_call | solution.py:58
  32.7 14.6 %shard_map.119.w_ref.refs_4_ = bf16[2048,3584]{1,0:T(8,128)(2,1)} custom-call(s32[448]{0:T(512)} %broadcast_add_fusion.2.table_ref, bf16[336,128,128]{2,1,0:T(8,128)(2,1)} %bitcast.14), custom_call_target="tpu_custom_call" | custom-call | bytes 25690112 | tf_op jit(solution)/shard_map/pallas_call | solution.py:58
  47.4 14.8 %shard_map.121.w_ref.refs_5_ = bf16[2048,3584]{1,0:T(8,128)(2,1)} custom-call(s32[448]{0:T(512)} %broadcast_add_fusion.1.table_ref, bf16[336,128,128]{2,1,0:T(8,128)(2,1)} %bitcast.15), custom_call_target="tpu_custom_call" | custom-call | bytes 25690112 | tf_op jit(solution)/shard_map/pallas_call | solution.py:58
  62.2 2.8 collective-permute-start.2
  65.0 1.0 constant_dynamic-update-slice_fusion.6
  66.0 0.9 copy-done.8
  67.0 10.9 %shard_map.125 = (f32[128,3584]{1,0:T(8,128)}, bf16[128,3584]{1,0:T(8,128)(2,1)}) custom-call(s32[1]{0:T(128)} %bitcast.core_ref, bf16[256,2048]{1,0:T(8,128)(2,1)} %copy-done.8, bf16[3584,2048]{1,0:T(8,128)(2,1)} %shard_map.123.refs_2_.w_ref), custom_call_target="tpu_custom_call" | custom-call | flops 3758096384 | bytes 14680064 | tf_op jit(solution)/shard_map/pallas_call | solution.py:96
  78.0 1.0 copy-done.3
  79.0 10.9 %shard_map.120 = (f32[128,3584]{1,0:T(8,128)}, bf16[128,3584]{1,0:T(8,128)(2,1)}) custom-call(s32[1]{0:T(128)} %bitcast.core_ref, bf16[256,2048]{1,0:T(8,128)(2,1)} %copy-done.3, bf16[2048,3584]{1,0:T(8,128)(2,1)} %shard_map.119.w_ref.refs_4_), custom_call_target="tpu_custom_call" | custom-call | flops 3758096384 | bytes 14680064 | tf_op jit(solution)/shard_map/pallas_call | solution.py:96
  90.4 11.0 %shard_map.122 = (f32[128,3584]{1,0:T(8,128)}, bf16[128,3584]{1,0:T(8,128)(2,1)}) custom-call(s32[1]{0:T(128)} %bitcast.core_ref, bf16[256,2048]{1,0:T(8,128)(2,1)} %copy-done.3, bf16[2048,3584]{1,0:T(8,128)(2,1)} %shard_map.121.w_ref.refs_5_), custom_call_target="tpu_custom_call" | custom-call | flops 3758096384 | bytes 14680064 | tf_op jit(solution)/shard_map/pallas_call | solution.py:96
  101.7 1.6 collective-permute-start.15
  103.4 1.3 collective-permute-start.4
  104.9 1.3 collective-permute-start.6
  106.3 18.6 %collective-permute-done.15 = bf16[128,3584]{1,0:T(8,128)(2,1)S(1)} collective-permute-done((bf16[128,3584]{1,0:T(8,128)(2,1)S(1)}, bf16[128,3584]{1,0:T(8,128)(2,1)S(1)}, u32[]{:S(2)}, u32[]{:S(2)}) %collective-permute-start.15) | collective-permute-done | bytes 917536 | tf_op jit(solution)/shard_map/ppermute | solution.py:249
  124.9 19.7 %collective-permute-done.4 = bf16[128,3584]{1,0:T(8,128)(2,1)S(1)} collective-permute-done((bf16[128,3584]{1,0:T(8,128)(2,1)S(1)}, bf16[128,3584]{1,0:T(8,128)(2,1)S(1)}, u32[]{:S(2)}, u32[]{:S(2)}) %collective-permute-start.4) | collective-permute-done | bytes 917536 | tf_op jit(solution)/shard_map/ppermute | solution.py:249
  144.6 19.2 %collective-permute-done.6 = bf16[128,3584]{1,0:T(8,128)(2,1)S(1)} collective-permute-done((bf16[128,3584]{1,0:T(8,128)(2,1)S(1)}, bf16[128,3584]{1,0:T(8,128)(2,1)S(1)}, u32[]{:S(2)}, u32[]{:S(2)}) %collective-permute-start.6) | collective-permute-done | bytes 917536 | tf_op jit(solution)/shard_map/ppermute | solution.py:249
  163.8 1.7 multiply_convert_fusion
  166.1 1.5 collective-permute-start.22
  168.2 0.7 convert_reduce_fusion.2
  170.2 1.5 collective-permute-start.26
  171.7 11.0 %shard_map.124 = (f32[64,2048]{1,0:T(8,128)}, bf16[64,2048]{1,0:T(8,128)(2,1)}, bf16[64,2048]{1,0:T(8,128)(2,1)}, bf16[64,2048]{1,0:T(8,128)(2,1)}) custom-call(s32[1]{0:T(128)} %bitcast.core_ref, bf16[128,3584]{1,0:T(8,128)(2,1)} %copy-done.5, bf16[128,3584]{1,0:T(8,128)(2,1)} %copy-done.10, bf16[3584,2048]{1,0:T(8,128)(2,1)} %shard_map.123.refs_2_.w_ref), custom_call_target="tpu_custom_call" | custom-call | flops 3758096384 | bytes 14680064 | tf_op jit(solution)/shard_map/pallas_call | solution.py:155
  182.7 1.0 collective-permute-start.21
  184.3 5.1 %collective-permute-done.22.refs_4_ = bf16[128,3584]{1,0:T(8,128)(2,1)} collective-permute-done((bf16[128,3584]{1,0:T(8,128)(2,1)S(1)}, bf16[128,3584]{1,0:T(8,128)(2,1)}, u32[]{:S(2)}, u32[]{:S(2)}) %collective-permute-start.22) | collective-permute-done | bytes 917536 | tf_op jit(solution)/shard_map/ppermute | solution.py:249
  189.4 2.0 collective-permute-start.9
  191.4 17.5 %collective-permute-done.24.refs_4_ = bf16[128,3584]{1,0:T(8,128)(2,1)S(1)} collective-permute-done((bf16[128,3584]{1,0:T(8,128)(2,1)S(1)}, bf16[128,3584]{1,0:T(8,128)(2,1)S(1)}, u32[]{:S(2)}, u32[]{:S(2)}) %collective-permute-start.24) | collective-permute-done | bytes 917536 | tf_op jit(solution)/shard_map/ppermute | solution.py:249
  209.0 0.9 copy-done.17
  209.9 1.2 collective-permute-start.8
  211.1 16.4 %shard_map.126 = (f32[64,2048]{1,0:T(8,128)}, bf16[64,2048]{1,0:T(8,128)(2,1)}, bf16[64,2048]{1,0:T(8,128)(2,1)}, bf16[64,2048]{1,0:T(8,128)(2,1)}) custom-call(s32[1]{0:T(128)} %bitcast.core_ref, bf16[128,3584]{1,0:T(8,128)(2,1)} %copy-done.7, bf16[128,3584]{1,0:T(8,128)(2,1)} %copy-done.12, bf16[128,3584]{1,0:T(8,128)(2,1)} %copy-done.6, ...), custom_call_target="tpu_custom_call" | custom-call | flops 7516192768 | bytes 29360128 | tf_op jit(solution)/shard_map/pallas_call | solution.py:155
  227.6 1.1 collective-permute-done.26.refs_2_
  229.3 1.5 collective-permute-start.19
  230.8 2.9 collective-permute-start.18
  233.7 0.8 add_convert_fusion.1
  234.5 5.6 %collective-permute-done.20 = bf16[64,2048]{1,0:T(8,128)(2,1)S(1)} collective-permute-done((bf16[64,2048]{1,0:T(8,128)(2,1)}, bf16[64,2048]{1,0:T(8,128)(2,1)S(1)}, u32[]{:S(2)}, u32[]{:S(2)}) %collective-permute-start.20) | collective-permute-done | bytes 262176 | tf_op jit(solution)/shard_map/ppermute | solution.py:249
  240.1 1.5 collective-permute-start.28
  241.6 8.0 %collective-permute-done.19 = bf16[64,2048]{1,0:T(8,128)(2,1)S(1)} collective-permute-done((bf16[64,2048]{1,0:T(8,128)(2,1)}, bf16[64,2048]{1,0:T(8,128)(2,1)S(1)}, u32[]{:S(2)}, u32[]{:S(2)}) %collective-permute-start.19) | collective-permute-done | bytes 262176 | tf_op jit(solution)/shard_map/ppermute | solution.py:249
  250.1 0.8 add_convert_fusion
  251.2 0.9 copy-done.19
  252.1 18.3 %shard_map.127 = bf16[336,128,128]{2,1,0:T(8,128)(2,1)} custom-call(s32[448]{0:T(512)} %broadcast_add_fusion.2.table_ref, s32[1]{0:T(128)} %bitcast.7.count_ref, s32[1]{0:T(128)} %bitcast.core_ref, bf16[256,2048]{1,0:T(8,128)(2,1)} %copy-done.3, bf16[256,2048]{1,0:T(8,128)(2,1)} %collective-permute-done.21.refs_1_, bf16[128,3584]{1,0:T(8,128)(2,1)} %copy-done.7, ...), custom_call_target="tpu_custom_call" | custom-call | flops 7516192768 | bytes 11010048 | tf_op jit(solution)/shard_map/pallas_call | solution.py:228
  270.4 18.0 %shard_map.128 = bf16[336,128,128]{2,1,0:T(8,128)(2,1)} custom-call(s32[448]{0:T(512)} %broadcast_add_fusion.1.table_ref, s32[1]{0:T(128)} %bitcast.9.count_ref, s32[1]{0:T(128)} %bitcast.core_ref, bf16[256,2048]{1,0:T(8,128)(2,1)} %copy-done.3, bf16[256,2048]{1,0:T(8,128)(2,1)} %collective-permute-done.21.refs_1_, bf16[128,3584]{1,0:T(8,128)(2,1)} %copy-done.6, ...), custom_call_target="tpu_custom_call" | custom-call | flops 7516192768 | bytes 11010048 | tf_op jit(solution)/shard_map/pallas_call | solution.py:228
  288.5 1.0 copy-done.16
  289.7 19.4 %shard_map.129 = bf16[336,128,128]{2,1,0:T(8,128)(2,1)} custom-call(s32[448]{0:T(512)} %broadcast_add_fusion.table_ref, s32[1]{0:T(128)} %bitcast.11.count_ref, s32[1]{0:T(128)} %bitcast.core_ref, bf16[128,3584]{1,0:T(8,128)(2,1)} %copy-done.5, bf16[128,3584]{1,0:T(8,128)(2,1)} %copy-done.10, bf16[128,3584]{1,0:T(8,128)(2,1)} %collective-permute-done.26.refs_2_, ...), custom_call_target="tpu_custom_call" | custom-call | flops 7516192768 | bytes 11010048 | tf_op jit(solution)/shard_map/pallas_call | solution.py:228
  (87 shorter events, 9.0 us)
Async XLA Ops:
  0.6 61.5 %collective-permute-start.11 = (bf16[64,2048]{1,0:T(8,128)(2,1)}, bf16[64,2048]{1,0:T(8,128)(2,1)}, u32[]{:S(2)}, u32[]{:S(2)}) collective-permute-start(bf16[64,2048]{1,0:T(8,128)(2,1)} %param.9), channel_id=1, source_target_pairs={{0,1},{1,2},{2,3},{3,0},{4,5},{5,6},{6,7},{7,4},{8,9},{9,10},{10,1... | collective-permute-start | bytes 786440 | tf_op jit(solution)/shard_map/ppermute | solution.py:249
  3.7 62.2 %collective-permute-start.12 = (bf16[64,2048]{1,0:T(8,128)(2,1)}, bf16[64,2048]{1,0:T(8,128)(2,1)S(1)}, u32[]{:S(2)}, u32[]{:S(2)}) collective-permute-start(bf16[64,2048]{1,0:T(8,128)(2,1)} %param.9), channel_id=1, source_target_pairs={{0,2},{1,3},{2,0},{3,1},{4,6},{5,7},{6,4},{7,5},{8,10},{9,11},{10,... | collective-permute-start | bytes 786440 | tf_op jit(solution)/shard_map/ppermute | solution.py:249
  6.3 59.7 %collective-permute-start.13 = (bf16[64,2048]{1,0:T(8,128)(2,1)}, bf16[64,2048]{1,0:T(8,128)(2,1)S(1)}, u32[]{:S(2)}, u32[]{:S(2)}) collective-permute-start(bf16[64,2048]{1,0:T(8,128)(2,1)} %param.9), channel_id=1, source_target_pairs={{0,3},{1,0},{2,1},{3,2},{4,7},{5,4},{6,5},{7,6},{8,11},{9,8},{10,9... | collective-permute-start | bytes 786440 | tf_op jit(solution)/shard_map/ppermute | solution.py:249
  7.6 70.2 %collective-permute-start = (bf16[64,2048]{1,0:T(8,128)(2,1)}, bf16[64,2048]{1,0:T(8,128)(2,1)S(1)}, u32[]{:S(2)}, u32[]{:S(2)}) collective-permute-start(bf16[64,2048]{1,0:T(8,128)(2,1)} %param.8), channel_id=1, source_target_pairs={{0,1},{1,2},{2,3},{3,0},{4,5},{5,6},{6,7},{7,4},{8,9},{9,10},{10,1... | collective-permute-start | bytes 786440 | tf_op jit(solution)/shard_map/ppermute | solution.py:249
  8.3 69.6 %collective-permute-start.1 = (bf16[64,2048]{1,0:T(8,128)(2,1)}, bf16[64,2048]{1,0:T(8,128)(2,1)S(1)}, u32[]{:S(2)}, u32[]{:S(2)}) collective-permute-start(bf16[64,2048]{1,0:T(8,128)(2,1)} %param.8), channel_id=1, source_target_pairs={{0,2},{1,3},{2,0},{3,1},{4,6},{5,7},{6,4},{7,5},{8,10},{9,11},{10,... | collective-permute-start | bytes 786440 | tf_op jit(solution)/shard_map/ppermute | solution.py:249
  47.4 14.8 %copy-start.15 = (bf16[64,2048]{1,0:T(8,128)(2,1)S(1)}, bf16[64,2048]{1,0:T(8,128)(2,1)}, u32[]{:S(2)}) copy-start(bf16[64,2048]{1,0:T(8,128)(2,1)} %param.8) | copy-start | bytes 786436
  62.2 15.8 %collective-permute-start.2 = (bf16[64,2048]{1,0:T(8,128)(2,1)S(1)}, bf16[64,2048]{1,0:T(8,128)(2,1)S(1)}, u32[]{:S(2)}, u32[]{:S(2)}) collective-permute-start(bf16[64,2048]{1,0:T(8,128)(2,1)S(1)} %copy-done.15), channel_id=1, source_target_pairs={{0,3},{1,0},{2,1},{3,2},{4,7},{5,4},{6,5},{7,6},{8,11},{9,8},{10,9... | collective-permute-start | bytes 786440 | tf_op jit(solution)/shard_map/ppermute | solution.py:249
  66.0 1.0 copy-start.8
  77.9 23.6 %collective-permute-start.14 = (bf16[128,3584]{1,0:T(8,128)(2,1)}, bf16[128,3584]{1,0:T(8,128)(2,1)S(1)}, u32[]{:S(2)}, u32[]{:S(2)}) collective-permute-start(bf16[128,3584]{1,0:T(8,128)(2,1)} %get-tuple-element.28), channel_id=1, source_target_pairs={{0,4},{4,0},{8,12},{12,8},{1,5},{5,1},{9,13},{13,9},{2,6},{6,2},{1... | collective-permute-start | bytes 2752520 | tf_op jit(solution)/shard_map/ppermute | solution.py:254
  78.0 1.0 copy-start.3
  89.9 11.6 %copy-start = (f32[128,3584]{1,0:T(8,128)S(1)}, f32[128,3584]{1,0:T(8,128)}, u32[]{:S(2)}) copy-start(f32[128,3584]{1,0:T(8,128)} %get-tuple-element.27) | copy-start | bytes 5505028
  89.9 13.4 %collective-permute-start.3 = (bf16[128,3584]{1,0:T(8,128)(2,1)}, bf16[128,3584]{1,0:T(8,128)(2,1)S(1)}, u32[]{:S(2)}, u32[]{:S(2)}) collective-permute-start(bf16[128,3584]{1,0:T(8,128)(2,1)} %get-tuple-element.20), channel_id=1, source_target_pairs={{0,4},{4,0},{8,12},{12,8},{1,5},{5,1},{9,13},{13,9},{2,6},{6,2},{1... | collective-permute-start | bytes 2752520 | tf_op jit(solution)/shard_map/ppermute | solution.py:254
  101.4 3.4 %collective-permute-start.5 = (bf16[128,3584]{1,0:T(8,128)(2,1)}, bf16[128,3584]{1,0:T(8,128)(2,1)S(1)}, u32[]{:S(2)}, u32[]{:S(2)}) collective-permute-start(bf16[128,3584]{1,0:T(8,128)(2,1)} %get-tuple-element.22), channel_id=1, source_target_pairs={{0,4},{4,0},{8,12},{12,8},{1,5},{5,1},{9,13},{13,9},{2,6},{6,2},{1... | collective-permute-start | bytes 2752520 | tf_op jit(solution)/shard_map/ppermute | solution.py:254
  101.5 1.7 copy-start.1
  101.7 23.2 %collective-permute-start.15 = (bf16[128,3584]{1,0:T(8,128)(2,1)S(1)}, bf16[128,3584]{1,0:T(8,128)(2,1)S(1)}, u32[]{:S(2)}, u32[]{:S(2)}) collective-permute-start(bf16[128,3584]{1,0:T(8,128)(2,1)S(1)} %fusion.2), channel_id=1, source_target_pairs={{0,8},{4,12},{8,0},{12,4},{1,9},{5,13},{9,1},{13,5},{2,10},{6,14},... | collective-permute-start | bytes 2752520 | tf_op jit(solution)/shard_map/ppermute | solution.py:249
  103.3 1.5 copy-start.2
  103.4 41.1 %collective-permute-start.4 = (bf16[128,3584]{1,0:T(8,128)(2,1)S(1)}, bf16[128,3584]{1,0:T(8,128)(2,1)S(1)}, u32[]{:S(2)}, u32[]{:S(2)}) collective-permute-start(bf16[128,3584]{1,0:T(8,128)(2,1)S(1)} %fusion), channel_id=1, source_target_pairs={{0,8},{4,12},{8,0},{12,4},{1,9},{5,13},{9,1},{13,5},{2,10},{6,14},... | collective-permute-start | bytes 2752520 | tf_op jit(solution)/shard_map/ppermute | solution.py:249
  104.9 58.8 %collective-permute-start.6 = (bf16[128,3584]{1,0:T(8,128)(2,1)S(1)}, bf16[128,3584]{1,0:T(8,128)(2,1)S(1)}, u32[]{:S(2)}, u32[]{:S(2)}) collective-permute-start(bf16[128,3584]{1,0:T(8,128)(2,1)S(1)} %fusion.1), channel_id=1, source_target_pairs={{0,8},{4,12},{8,0},{12,4},{1,9},{5,13},{9,1},{13,5},{2,10},{6,14},... | collective-permute-start | bytes 2752520 | tf_op jit(solution)/shard_map/ppermute | solution.py:249
  165.5 6.2 %copy-start.5 = (bf16[128,3584]{1,0:T(8,128)(2,1)}, bf16[128,3584]{1,0:T(8,128)(2,1)S(1)}, u32[]{:S(2)}) copy-start(bf16[128,3584]{1,0:T(8,128)(2,1)S(1)} %get-tuple-element.38.refs_0_) | copy-start | bytes 2752516
  165.5 17.2 %copy-start.6 = (bf16[128,3584]{1,0:T(8,128)(2,1)}, bf16[128,3584]{1,0:T(8,128)(2,1)S(1)}, u32[]{:S(2)}) copy-start(bf16[128,3584]{1,0:T(8,128)(2,1)S(1)} %get-tuple-element.36.refs_2_) | copy-start | bytes 2752516
  165.5 17.2 %copy-start.7 = (bf16[128,3584]{1,0:T(8,128)(2,1)}, bf16[128,3584]{1,0:T(8,128)(2,1)S(1)}, u32[]{:S(2)}) copy-start(bf16[128,3584]{1,0:T(8,128)(2,1)S(1)} %get-tuple-element.37.refs_0_.refs_2_) | copy-start | bytes 2752516
  165.5 4.7 %collective-permute-start.7 = (bf16[128,3584]{1,0:T(8,128)(2,1)S(1)}, bf16[128,3584]{1,0:T(8,128)(2,1)S(1)}, u32[]{:S(2)}, u32[]{:S(2)}) collective-permute-start(bf16[128,3584]{1,0:T(8,128)(2,1)S(1)} %get-tuple-element.38.refs_0_), channel_id=1, source_target_pairs={{0,4},{4,0},{8,12},{12,8},{1,5},{5,1},{9,13},{13,9},{2,6},{6,2},{1... | collective-permute-start | bytes 2752520 | tf_op jit(solution)/shard_map/ppermute | solution.py:254
  165.6 17.1 %collective-permute-start.16 = (bf16[128,3584]{1,0:T(8,128)(2,1)S(1)}, bf16[128,3584]{1,0:T(8,128)(2,1)S(1)}, u32[]{:S(2)}, u32[]{:S(2)}) collective-permute-start(bf16[128,3584]{1,0:T(8,128)(2,1)S(1)} %get-tuple-element.37.refs_0_.refs_2_), channel_id=1, source_target_pairs={{0,4},{4,0},{8,12},{12,8},{1,5},{5,1},{9,13},{13,9},{2,6},{6,2},{1... | collective-permute-start | bytes 2752520 | tf_op jit(solution)/shard_map/ppermute | solution.py:254
  166.1 17.7 %collective-permute-start.17 = (bf16[128,3584]{1,0:T(8,128)(2,1)S(1)}, bf16[128,3584]{1,0:T(8,128)(2,1)S(1)}, u32[]{:S(2)}, u32[]{:S(2)}) collective-permute-start(bf16[128,3584]{1,0:T(8,128)(2,1)S(1)} %get-tuple-element.36.refs_2_), channel_id=1, source_target_pairs={{0,4},{4,0},{8,12},{12,8},{1,5},{5,1},{9,13},{13,9},{2,6},{6,2},{1... | collective-permute-start | bytes 2752520 | tf_op jit(solution)/shard_map/ppermute | solution.py:254
  166.1 23.3 %collective-permute-start.22 = (bf16[128,3584]{1,0:T(8,128)(2,1)S(1)}, bf16[128,3584]{1,0:T(8,128)(2,1)}, u32[]{:S(2)}, u32[]{:S(2)}) collective-permute-start(bf16[128,3584]{1,0:T(8,128)(2,1)S(1)} %get-tuple-element.37.refs_0_.refs_2_), channel_id=1, source_target_pairs={{0,16},{16,0},{1,17},{17,1},{2,18},{18,2},{3,19},{19,3},{4,20},{20... | collective-permute-start | bytes 2752520 | tf_op jit(solution)/shard_map/ppermute | solution.py:249
  167.6 41.3 %collective-permute-start.24 = (bf16[128,3584]{1,0:T(8,128)(2,1)S(1)}, bf16[128,3584]{1,0:T(8,128)(2,1)S(1)}, u32[]{:S(2)}, u32[]{:S(2)}) collective-permute-start(bf16[128,3584]{1,0:T(8,128)(2,1)S(1)} %get-tuple-element.36.refs_2_), channel_id=1, source_target_pairs={{0,16},{16,0},{1,17},{17,1},{2,18},{18,2},{3,19},{19,3},{4,20},{20... | collective-permute-start | bytes 2752520 | tf_op jit(solution)/shard_map/ppermute | solution.py:249
  170.2 12.5 %copy-start.4 = (bf16[256,2048]{1,0:T(8,128)(2,1)S(1)}, bf16[256,2048]{1,0:T(8,128)(2,1)}, u32[]{:S(2)}) copy-start(bf16[256,2048]{1,0:T(8,128)(2,1)} %copy-done.3) | copy-start | bytes 3145732
  170.2 1.5 copy-start.10
  170.2 58.6 %collective-permute-start.26 = (bf16[128,3584]{1,0:T(8,128)(2,1)S(1)}, bf16[128,3584]{1,0:T(8,128)(2,1)}, u32[]{:S(2)}, u32[]{:S(2)}) collective-permute-start(bf16[128,3584]{1,0:T(8,128)(2,1)S(1)} %get-tuple-element.38.refs_0_), channel_id=1, source_target_pairs={{0,16},{16,0},{1,17},{17,1},{2,18},{18,2},{3,19},{19,3},{4,20},{20... | collective-permute-start | bytes 2752520 | tf_op jit(solution)/shard_map/ppermute | solution.py:249
  182.7 28.4 %copy-start.12 = (bf16[128,3584]{1,0:T(8,128)(2,1)}, bf16[128,3584]{1,0:T(8,128)(2,1)S(1)}, u32[]{:S(2)}) copy-start(bf16[128,3584]{1,0:T(8,128)(2,1)S(1)} %collective-permute-done.16.refs_1_.refs_3_) | copy-start | bytes 2752516
  182.7 68.5 %collective-permute-start.21 = (bf16[256,2048]{1,0:T(8,128)(2,1)S(1)}, bf16[256,2048]{1,0:T(8,128)(2,1)}, u32[]{:S(2)}, u32[]{:S(2)}) collective-permute-start(bf16[256,2048]{1,0:T(8,128)(2,1)S(1)} %copy-done.4), channel_id=1, source_target_pairs={{0,16},{16,0},{1,17},{17,1},{2,18},{18,2},{3,19},{19,3},{4,20},{20... | collective-permute-start | bytes 3145736 | tf_op jit(solution)/shard_map/ppermute | solution.py:249
  183.7 27.4 %copy-start.11 = (bf16[128,3584]{1,0:T(8,128)(2,1)}, bf16[128,3584]{1,0:T(8,128)(2,1)S(1)}, u32[]{:S(2)}) copy-start(bf16[128,3584]{1,0:T(8,128)(2,1)S(1)} %collective-permute-done.17.refs_3_) | copy-start | bytes 2752516
  183.7 45.6 %collective-permute-start.10 = (bf16[64,2048]{1,0:T(8,128)(2,1)}, bf16[64,2048]{1,0:T(8,128)(2,1)S(1)}, u32[]{:S(2)}, u32[]{:S(2)}) collective-permute-start(bf16[64,2048]{1,0:T(8,128)(2,1)} %get-tuple-element.26), channel_id=1, source_target_pairs={{0,1},{1,2},{2,3},{3,0},{4,5},{5,6},{6,7},{7,4},{8,9},{9,10},{10,1... | collective-permute-start | bytes 786440 | tf_op jit(solution)/shard_map/ppermute | solution.py:249
  189.4 41.4 %collective-permute-start.9 = (bf16[64,2048]{1,0:T(8,128)(2,1)}, bf16[64,2048]{1,0:T(8,128)(2,1)S(1)}, u32[]{:S(2)}, u32[]{:S(2)}) collective-permute-start(bf16[64,2048]{1,0:T(8,128)(2,1)} %get-tuple-element.25), channel_id=1, source_target_pairs={{0,2},{1,3},{2,0},{3,1},{4,6},{5,7},{6,4},{7,5},{8,10},{9,11},{10,... | collective-permute-start | bytes 786440 | tf_op jit(solution)/shard_map/ppermute | solution.py:249
  209.9 23.8 %copy-start.13 = (f32[64,2048]{1,0:T(8,128)S(1)}, f32[64,2048]{1,0:T(8,128)}, u32[]{:S(2)}) copy-start(f32[64,2048]{1,0:T(8,128)} %get-tuple-element.23) | copy-start | bytes 1572868
  209.9 30.2 %copy-start.9 = (bf16[256,2048]{1,0:T(8,128)(2,1)S(1)}, bf16[256,2048]{1,0:T(8,128)(2,1)}, u32[]{:S(2)}) copy-start(bf16[256,2048]{1,0:T(8,128)(2,1)} %copy-done.8) | copy-start | bytes 3145732
  209.9 39.7 %copy-start.18 = (bf16[128,3584]{1,0:T(8,128)(2,1)S(1)}, bf16[128,3584]{1,0:T(8,128)(2,1)}, u32[]{:S(2)}) copy-start(bf16[128,3584]{1,0:T(8,128)(2,1)} %copy-done.17) | copy-start | bytes 2752516
  209.9 23.8 %collective-permute-start.8 = (bf16[64,2048]{1,0:T(8,128)(2,1)}, bf16[64,2048]{1,0:T(8,128)(2,1)S(1)}, u32[]{:S(2)}, u32[]{:S(2)}) collective-permute-start(bf16[64,2048]{1,0:T(8,128)(2,1)} %get-tuple-element.24), channel_id=1, source_target_pairs={{0,3},{1,0},{2,1},{3,2},{4,7},{5,4},{6,5},{7,6},{8,11},{9,8},{10,9... | collective-permute-start | bytes 786440 | tf_op jit(solution)/shard_map/ppermute | solution.py:249
  227.6 22.5 %copy-start.14 = (f32[64,2048]{1,0:T(8,128)S(1)}, f32[64,2048]{1,0:T(8,128)}, u32[]{:S(2)}) copy-start(f32[64,2048]{1,0:T(8,128)} %get-tuple-element.29) | copy-start | bytes 1572868
  228.7 11.4 %collective-permute-start.20 = (bf16[64,2048]{1,0:T(8,128)(2,1)}, bf16[64,2048]{1,0:T(8,128)(2,1)S(1)}, u32[]{:S(2)}, u32[]{:S(2)}) collective-permute-start(bf16[64,2048]{1,0:T(8,128)(2,1)} %get-tuple-element.32), channel_id=1, source_target_pairs={{0,1},{1,2},{2,3},{3,0},{4,5},{5,6},{6,7},{7,4},{8,9},{9,10},{10,1... | collective-permute-start | bytes 786440 | tf_op jit(solution)/shard_map/ppermute | solution.py:249
  229.3 20.3 %collective-permute-start.19 = (bf16[64,2048]{1,0:T(8,128)(2,1)}, bf16[64,2048]{1,0:T(8,128)(2,1)S(1)}, u32[]{:S(2)}, u32[]{:S(2)}) collective-permute-start(bf16[64,2048]{1,0:T(8,128)(2,1)} %get-tuple-element.31), channel_id=1, source_target_pairs={{0,2},{1,3},{2,0},{3,1},{4,6},{5,7},{6,4},{7,5},{8,10},{9,11},{10,... | collective-permute-start | bytes 786440 | tf_op jit(solution)/shard_map/ppermute | solution.py:249
  230.8 18.8 %collective-permute-start.18 = (bf16[64,2048]{1,0:T(8,128)(2,1)}, bf16[64,2048]{1,0:T(8,128)(2,1)S(1)}, u32[]{:S(2)}, u32[]{:S(2)}) collective-permute-start(bf16[64,2048]{1,0:T(8,128)(2,1)} %get-tuple-element.30), channel_id=1, source_target_pairs={{0,3},{1,0},{2,1},{3,2},{4,7},{5,4},{6,5},{7,6},{8,11},{9,8},{10,9... | collective-permute-start | bytes 786440 | tf_op jit(solution)/shard_map/ppermute | solution.py:249
  233.7 17.5 %collective-permute-start.23 = (bf16[128,3584]{1,0:T(8,128)(2,1)}, bf16[128,3584]{1,0:T(8,128)(2,1)S(1)}, u32[]{:S(2)}, u32[]{:S(2)}) collective-permute-start(bf16[128,3584]{1,0:T(8,128)(2,1)} %collective-permute-done.22.refs_4_), channel_id=1, source_target_pairs={{0,4},{4,0},{8,12},{12,8},{1,5},{5,1},{9,13},{13,9},{2,6},{6,2},{1... | collective-permute-start | bytes 2752520 | tf_op jit(solution)/shard_map/ppermute | solution.py:254
  240.1 48.4 %collective-permute-start.28 = (bf16[256,2048]{1,0:T(8,128)(2,1)S(1)}, bf16[256,2048]{1,0:T(8,128)(2,1)S(1)}, u32[]{:S(2)}, u32[]{:S(2)}) collective-permute-start(bf16[256,2048]{1,0:T(8,128)(2,1)S(1)} %copy-done.9), channel_id=1, source_target_pairs={{0,16},{16,0},{1,17},{17,1},{2,18},{18,2},{3,19},{19,3},{4,20},{20... | collective-permute-start | bytes 3145736 | tf_op jit(solution)/shard_map/ppermute | solution.py:249
  249.6 20.8 %collective-permute-start.25 = (bf16[128,3584]{1,0:T(8,128)(2,1)S(1)}, bf16[128,3584]{1,0:T(8,128)(2,1)}, u32[]{:S(2)}, u32[]{:S(2)}) collective-permute-start(bf16[128,3584]{1,0:T(8,128)(2,1)S(1)} %copy-done.18), channel_id=1, source_target_pairs={{0,4},{4,0},{8,12},{12,8},{1,5},{5,1},{9,13},{13,9},{2,6},{6,2},{1... | collective-permute-start | bytes 2752520 | tf_op jit(solution)/shard_map/ppermute | solution.py:254
  249.6 38.9 %collective-permute-start.27 = (bf16[128,3584]{1,0:T(8,128)(2,1)}, bf16[128,3584]{1,0:T(8,128)(2,1)S(1)}, u32[]{:S(2)}, u32[]{:S(2)}) collective-permute-start(bf16[128,3584]{1,0:T(8,128)(2,1)} %collective-permute-done.26.refs_2_), channel_id=1, source_target_pairs={{0,4},{4,0},{8,12},{12,8},{1,5},{5,1},{9,13},{13,9},{2,6},{6,2},{1... | collective-permute-start | bytes 2752520 | tf_op jit(solution)/shard_map/ppermute | solution.py:254
  288.5 1.0 copy-start.16
  288.5 1.2 copy-start.20
  (2 other events, 1.9 us)

commit v2 on v0

v2 whole, which is shorter than its diff:
```python
import functools
import math

import jax
import jax.numpy as jnp
from jax import lax
from jax.experimental import pallas as pl
from jax.experimental.pallas import tpu as pltpu
from jax.sharding import PartitionSpec as P

BLK = 128
AHEAD = 3
COST = 0.000001
MARK = 200000
WIDE = 1792
FF = 14336
VMEM_LIMIT = 56 * 1024 * 1024
VM = pltpu.VMEM
SM = pltpu.SMEM


def params():
    return pltpu.CompilerParams(vmem_limit_bytes=VMEM_LIMIT)


def cost(flops, nbytes):
    return pl.CostEstimate(
        flops=int(flops * COST), bytes_accessed=int(nbytes * COST), transcendentals=0
    )


def tile_of(size, largest):
    return max(t for t in range(BLK, largest + 1, BLK) if size % t == 0)


def rows_at(start, rows):
    return pl.ds(pl.multiple_of(start, rows), rows)


def whole(memory_space):
    return pl.BlockSpec(memory_space=memory_space)


def natural_to_own(core, parts, ref, columns=slice(None)):
    rows = ref.shape[0] // (2 * parts)
    pieces = []
    for p in range(parts):
        pieces.append(ref[rows_at((2 * p + core) * rows, rows), columns])
        pieces.append(ref[rows_at((2 * p + 1 - core) * rows, rows), columns])
    return pieces


def after(x, *earlier):
    return lax.optimization_barrier((x, *earlier))[0]


def slot_table(index_list, first_count, second_count):
    listing = index_list[0, 0]
    slots = listing.shape[0]
    flat = jnp.where(listing[:, 0] >= 0, listing[:, 0] * second_count + listing[:, 1], -1)
    positions = jnp.arange(first_count * second_count, dtype=jnp.int32)
    hits = flat[None, :] == positions[:, None]
    back_from = slots - jnp.arange(slots, dtype=jnp.int32)
    table = slots - jnp.sum(jnp.where(hits, back_from[None, :], 0), axis=1)
    count = jnp.sum((flat >= 0).astype(jnp.int32))
    return table, count.reshape(1)


def densify_kernel(mats, rows, cols, panels, *refs):
    tables, blocks = refs[:mats], refs[mats : 2 * mats]
    outs = refs[-4 - mats : -4]
    store, stage, in_sem, out_sem = refs[-4:]
    slots = blocks[0].shape[0]
    loads = [
        pltpu.make_async_copy(blocks[m], store.at[m, pl.ds(0, slots)], in_sem.at[m])
        for m in range(mats)
    ]
    for load in loads:
        load.start()
    high = rows // panels
    writes = []
    for m in range(mats):
        store[m, slots] = jnp.zeros((BLK, BLK), jnp.bfloat16)
        loads[m].wait()
        for g in range(panels):
            if m:
                writes[(m - 1) * panels + g].wait()

            def fill(r, carry, m=m, g=g):
                for j in range(cols):
                    slot = tables[m][(g * high + r) * cols + j]
                    stage[g, rows_at(r * BLK, BLK), j * BLK : (j + 1) * BLK] = store[m, slot]
                return carry

            lax.fori_loop(0, high, fill, 0)
            write = pltpu.make_async_copy(
                stage.at[g], outs[m].at[pl.ds(g * high * BLK, high * BLK)], out_sem.at[g]
            )
            write.start()
            writes.append(write)
    for write in writes[-panels:]:
        write.wait()


def densify(tables, blocks, rows, cols, *earlier):
    mats = len(blocks)
    slots = blocks[0].shape[0]
    panels = 4 if rows % 4 == 0 else 1
    shape = jax.ShapeDtypeStruct((rows * BLK, cols * BLK), jnp.bfloat16)
    return pl.pallas_call(
        functools.partial(densify_kernel, mats, rows, cols, panels),
        out_shape=(shape,) * mats,
        in_specs=[whole(SM)] * mats + [whole(pl.ANY)] * (mats + len(earlier)),
        out_specs=(whole(pl.ANY),) * mats,
        scratch_shapes=[
            VM((mats, slots + 1, BLK, BLK), jnp.bfloat16),
            VM((panels, rows // panels * BLK, cols * BLK), jnp.bfloat16),
            pltpu.SemaphoreType.DMA((mats,)),
            pltpu.SemaphoreType.DMA((panels,)),
        ],
        compiler_params=params(),
        cost_estimate=cost(0, mats * (slots + rows * cols) * BLK * BLK * 2),
    )(*tables, *blocks, *earlier)


def stream(weights, stores, sem, tile, transposed, by_tile, ahead):
    length = weights[0].shape[0] if transposed else weights[0].shape[1]
    order = [(i, w) for i in range(length // tile) for w in range(len(weights))]
    if not by_tile:
        order.sort(key=lambda pair: pair[1])

    def copy(i, w):
        at = (pl.ds(i * tile, tile),) if transposed else (slice(None), pl.ds(i * tile, tile))
        return pltpu.make_async_copy(weights[w].at[at], stores[w].at[at], sem.at[w, i])

    for pair in order[:ahead]:
        copy(*pair).start()
    for n, (i, w) in enumerate(order):
        copy(i, w).wait()
        if n + ahead < len(order):
            copy(*order[n + ahead]).start()
        place = pl.ds(i * tile, tile)
        yield i, w, (stores[w].at[place] if transposed else stores[w].at[:, place])


def product(panel, held, transposed):
    dims = (((1,), (1 if transposed else 0,)), ((), ()))
    return lax.dot_general(panel, held[...], dims, preferred_element_type=jnp.float32)


def project_kernel(transposed, parts, mats, tile, core_ref, *refs):
    panels, weights = refs[:parts], refs[parts : parts + mats]
    outs = refs[-1 - mats - 2 * parts : -1 - mats]
    stores, sem = refs[-1 - mats : -1], refs[-1]
    is_first = core_ref[0] == 0
    half = panels[0].shape[0] // 2
    width = outs[0].shape[1] // mats
    panel = jnp.concatenate([ref[...] for ref in panels], axis=0)
    for i, w, held in stream(weights, stores, sem, tile, transposed, False, AHEAD):
        full = product(panel, held, transposed)
        span = slice(w * width + i * tile, w * width + (i + 1) * tile)
        for p in range(parts):
            first = full[2 * p * half : (2 * p + 1) * half]
            second = full[(2 * p + 1) * half : (2 * p + 2) * half]
            outs[2 * p][:, span] = jnp.where(is_first, first, second)
            outs[2 * p + 1][:, span] = jnp.where(is_first, second, first).astype(jnp.bfloat16)


def project(core, panels, weights, transposed, *earlier):
    parts, mats = len(panels), len(weights)
    tokens, depth = panels[0].shape
    width = weights[0].shape[0] if transposed else weights[0].shape[1]
    tile = tile_of(width, 512)
    shapes = (
        jax.ShapeDtypeStruct((tokens // 2, mats * width), jnp.float32),
        jax.ShapeDtypeStruct((tokens // 2, mats * width), jnp.bfloat16),
    )
    return pl.pallas_call(
        functools.partial(project_kernel, transposed, parts, mats, tile),
        out_shape=shapes * parts,
        in_specs=[whole(SM)]
        + [whole(VM)] * parts
        + [whole(pl.ANY)] * (mats + len(earlier)),
        out_specs=(whole(VM),) * (2 * parts),
        scratch_shapes=[VM(w.shape, jnp.bfloat16) for w in weights]
        + [pltpu.SemaphoreType.DMA((mats, width // tile))],
        compiler_params=params(),
        cost_estimate=cost(
            2 * parts * tokens * depth * width * mats, 2 * depth * width * mats
        ),
    )(core, *panels, *weights, *earlier)


def project_blocks_kernel(transposed, rows, cols, high, ring, core_ref, table, panel_ref, blocks, *refs):
    mine_ref, other_ref, dense = refs[-7:-4]
    store, stage, in_sem, out_sem = refs[-4:]
    slots = blocks.shape[0]
    load = pltpu.make_async_copy(blocks, store.at[pl.ds(0, slots)], in_sem)
    load.start()
    store[slots] = jnp.zeros((BLK, BLK), jnp.bfloat16)
    is_first = core_ref[0] == 0
    half = panel_ref.shape[0] // 2
    load.wait()
    writes = []
    for i in range((rows if transposed else cols) // high):
        held = stage.at[i % ring]
        if i >= ring:
            writes[i - ring].wait()
        for far in range(cols if transposed else rows):
            for near in range(high):
                r, c = (i * high + near, far) if transposed else (far, i * high + near)
                r_at, c_at = (near, far) if transposed else (far, near)
                held[r_at * BLK : (r_at + 1) * BLK, c_at * BLK : (c_at + 1) * BLK] = store[
                    table[r * cols + c]
                ]
        at = pl.ds(i * high * BLK, high * BLK)
        write = pltpu.make_async_copy(
            held, dense.at[at] if transposed else dense.at[:, at], out_sem.at[i % ring]
        )
        write.start()
        writes.append(write)
        full = product(panel_ref[...], held, transposed)
        first, second = full[:half], full[half:]
        mine_ref[:, at] = jnp.where(is_first, first, second)
        other_ref[:, at] = jnp.where(is_first, second, first).astype(jnp.bfloat16)
    for write in writes[-ring:]:
        write.wait()


def project_blocks(core, panel, table, blocks, rows, cols, transposed, *earlier):
    tokens, _ = panel.shape
    slots = blocks.shape[0]
    cut, across = (rows, cols) if transposed else (cols, rows)
    high = tile_of(cut * BLK, 512) // BLK
    ring = min(3, cut // high)
    tile_shape = (high * BLK, across * BLK) if transposed else (across * BLK, high * BLK)
    shape = (tokens // 2, cut * BLK)
    return pl.pallas_call(
        functools.partial(project_blocks_kernel, transposed, rows, cols, high, ring),
        out_shape=(
            jax.ShapeDtypeStruct(shape, jnp.float32),
            jax.ShapeDtypeStruct(shape, jnp.bfloat16),
            jax.ShapeDtypeStruct((rows * BLK, cols * BLK), jnp.bfloat16),
        ),
        in_specs=[whole(SM)] * 2 + [whole(VM)] + [whole(pl.ANY)] * (1 + len(earlier)),
        out_specs=(whole(VM), whole(VM), whole(pl.ANY)),
        scratch_shapes=[
            VM((slots + 1, BLK, BLK), jnp.bfloat16),
            VM((ring, *tile_shape), jnp.bfloat16),
            pltpu.SemaphoreType.DMA,
            pltpu.SemaphoreType.DMA((ring,)),
        ],
        compiler_params=params(),
        cost_estimate=cost(2 * tokens * rows * cols * BLK * BLK, rows * cols * BLK * BLK * 4),
    )(core, table, panel, blocks, *earlier)


def back_kernel(transposed, n_pieces, mats, chunks, tile, core_ref, *refs):
    pieces, weights = refs[:n_pieces], refs[n_pieces : n_pieces + mats]
    outs = refs[-1 - mats - chunks : -1 - mats]
    stores, sem = refs[-1 - mats : -1], refs[-1]
    is_first = core_ref[0] == 0
    half = pieces[0].shape[1]
    rows = n_pieces * half // chunks
    panels = [jnp.concatenate([ref[w] for ref in pieces], axis=0) for w in range(mats)]
    total = None
    for i, w, held in stream(weights, stores, sem, tile, transposed, True, AHEAD):
        part = product(panels[w], held, transposed)
        total = part if w == 0 else total + part
        if w < mats - 1:
            continue
        span = slice(i * tile, (i + 1) * tile)
        for p in range(n_pieces // 2):
            mine = total[2 * p * half : (2 * p + 1) * half]
            other = total[(2 * p + 1) * half : (2 * p + 2) * half]
            ordered = (jnp.where(is_first, mine, other), jnp.where(is_first, other, mine))
            for d in range(2 * half // rows):
                ref = outs[p * (2 * half // rows) + d]
                which, at = divmod(d * rows, half)
                ref[:, span] = ordered[which][at : at + rows].astype(ref.dtype)


def back(core, pieces, weights, chunks, transposed, *earlier):
    n_pieces, mats = len(pieces), len(weights)
    half, depth = pieces[0].shape[1:]
    width = weights[0].shape[0] if transposed else weights[0].shape[1]
    tile = tile_of(width, 512)
    rows = n_pieces * half // chunks
    shapes = tuple(
        jax.ShapeDtypeStruct((rows, width), jnp.bfloat16 if d else jnp.float32)
        for d in range(chunks)
    )
    return pl.pallas_call(
        functools.partial(back_kernel, transposed, n_pieces, mats, chunks, tile),
        out_shape=shapes,
        in_specs=[whole(SM)]
        + [whole(VM)] * n_pieces
        + [whole(pl.ANY)] * (mats + len(earlier)),
        out_specs=(whole(VM),) * chunks,
        scratch_shapes=[VM(w.shape, jnp.bfloat16) for w in weights]
        + [pltpu.SemaphoreType.DMA((mats, width // tile))],
        compiler_params=params(),
        cost_estimate=cost(
            2 * n_pieces * half * depth * width * mats, 2 * depth * width * mats
        ),
    )(core, *pieces, *weights, *earlier)


def pair_kernel(mine_ref, other_ref, *refs):
    wide = tile_of(mine_ref.shape[1], 512)
    for i in range(mine_ref.shape[1] // wide):
        span = slice(i * wide, (i + 1) * wide)
        refs[-1][:, span] = add_up([mine_ref[:, span], other_ref[:, span]]).astype(jnp.bfloat16)


def pair_sum(mine, other, *earlier):
    return pl.pallas_call(
        pair_kernel,
        out_shape=jax.ShapeDtypeStruct(mine.shape, jnp.bfloat16),
        in_specs=[whole(VM)] * 2 + [whole(pl.ANY)] * len(earlier),
        out_specs=whole(VM),
        compiler_params=params(),
        cost_estimate=cost(0, mine.size * 8),
    )(mine, other, *earlier)


def hold_kernel(*refs):
    del refs


def hold(x, *earlier):
    return pl.pallas_call(
        hold_kernel,
        out_shape=jax.ShapeDtypeStruct(x.shape, x.dtype),
        in_specs=[whole(pl.ANY)] * (1 + len(earlier)),
        out_specs=whole(pl.ANY),
        input_output_aliases={0: 0},
        compiler_params=params(),
        cost_estimate=pl.CostEstimate(flops=0, bytes_accessed=MARK, transcendentals=0),
    )(x, *earlier)


def sum_kernel(n_sum, *refs):
    refs[-1][...] = add_up([ref[...] for ref in refs[:n_sum]]).astype(refs[-1].dtype)


def sum_chunks(kept, *earlier):
    return pl.pallas_call(
        functools.partial(sum_kernel, len(kept)),
        out_shape=jax.ShapeDtypeStruct(kept[0].shape, jnp.bfloat16),
        in_specs=[whole(VM)] * len(kept) + [whole(pl.ANY)] * len(earlier),
        out_specs=whole(VM),
        compiler_params=params(),
        cost_estimate=cost(0, kept[0].size * 10),
    )(*kept, *earlier)


def mark_kernel(*refs):
    refs[-1][...] = jnp.zeros_like(refs[-1])


def mark(*earlier):
    return pl.pallas_call(
        mark_kernel,
        out_shape=jax.ShapeDtypeStruct((8, BLK), jnp.float32),
        in_specs=[whole(pl.ANY)] * len(earlier),
        out_specs=whole(VM),
        compiler_params=params(),
        cost_estimate=pl.CostEstimate(flops=0, bytes_accessed=MARK, transcendentals=0),
    )(*earlier)


def act_kernel(n_sum, *refs):
    gates, ups = refs[:n_sum], refs[n_sum : 2 * n_sum]
    hidden_ref, by_gate_ref, by_up_ref = refs[-3:]
    wide = tile_of(gates[0].shape[1], 512)
    for i in range(gates[0].shape[1] // wide):
        span = slice(i * wide, (i + 1) * wide)
        gate = add_up([ref[:, span] for ref in gates])
        up = add_up([ref[:, span] for ref in ups])
        sigma = jax.nn.sigmoid(gate)
        active = gate * sigma
        hidden_ref[0, :, span] = (active * up).astype(jnp.bfloat16)
        by_gate_ref[:, span] = up * sigma * (1.0 + gate * (1.0 - sigma))
        by_up_ref[:, span] = active


def act(gates, ups, *earlier):
    rows, width = gates[0].shape
    wide = jax.ShapeDtypeStruct((rows, width), jnp.float32)
    return pl.pallas_call(
        functools.partial(act_kernel, len(gates)),
        out_shape=(jax.ShapeDtypeStruct((1, rows, width), jnp.bfloat16), wide, wide),
        in_specs=[whole(VM)] * (2 * len(gates)) + [whole(pl.ANY)] * len(earlier),
        out_specs=(whole(VM),) * 3,
        compiler_params=params(),
        cost_estimate=cost(0, rows * width * 30),
    )(*gates, *ups, *earlier)


def grads_kernel(n_sum, *refs):
    sums, (by_gate_ref, by_up_ref) = refs[:n_sum], refs[n_sum : n_sum + 2]
    both_ref = refs[-1]
    wide = tile_of(sums[0].shape[1], 512)
    for i in range(sums[0].shape[1] // wide):
        span = slice(i * wide, (i + 1) * wide)
        grad_hidden = add_up([ref[:, span] for ref in sums])
        both_ref[0, :, span] = (grad_hidden * by_gate_ref[:, span]).astype(jnp.bfloat16)
        both_ref[1, :, span] = (grad_hidden * by_up_ref[:, span]).astype(jnp.bfloat16)


def act_grads(sums, by_gate, by_up, *earlier):
    return pl.pallas_call(
        functools.partial(grads_kernel, len(sums)),
        out_shape=jax.ShapeDtypeStruct((2, *by_gate.shape), jnp.bfloat16),
        in_specs=[whole(VM)] * (len(sums) + 2) + [whole(pl.ANY)] * len(earlier),
        out_specs=whole(VM),
        compiler_params=params(),
        cost_estimate=cost(0, by_gate.size * 20),
    )(*sums, by_gate, by_up, *earlier)


def block_grad_kernel(parts, mats, n_left, n_right, left_whole, scale, cols, wide, *refs):
    core_ref, tables, counts = refs[0], refs[1 : 1 + mats], refs[1 + mats : 1 + 2 * mats]
    rest = refs[1 + 2 * mats :]
    lefts, rights = rest[:n_left], rest[n_left : n_left + n_right]
    outs, stores = rest[-2 - 2 * mats : -2 - mats], rest[-2 - mats : -2]
    turned, sem = rest[-2:]
    core = core_ref[0]
    slots = outs[0].shape[0]
    length, width = turned.shape[0], rights[0].shape[-1]
    tall = tile_of(length, 512)

    for a in range(length // tall):
        span = slice(a * tall, (a + 1) * tall)
        if left_whole:
            pieces = [q for ref in lefts for q in natural_to_own(core, parts, ref, span)]
        else:
            pieces = [ref[0, :, span] for ref in lefts]
        turned[span, :] = jnp.concatenate(pieces, axis=0).T

    copies = []
    for m in range(mats):

        def clear(slot, carry, m=m):
            stores[m][slot] = jnp.zeros((BLK, BLK), jnp.bfloat16)
            return carry

        def column(at, carry, m=m):
            span = pl.ds(pl.multiple_of(at * wide, wide), wide)
            if left_whole:
                panel = [ref[m, :, span] for ref in rights]
            else:
                panel = [q for ref in rights for q in natural_to_own(core, parts, ref, span)]
            panel = jnp.concatenate(panel, axis=0)
            for a in range(length // tall):
                full = jnp.dot(
                    turned[a * tall : (a + 1) * tall, :], panel, preferred_element_type=jnp.float32
                )
                full = (full * scale).astype(jnp.bfloat16)
                for di in range(tall // BLK):
                    for dj in range(wide // BLK):
                        row = a * (tall // BLK) + di
                        slot = tables[m][row * cols + at * (wide // BLK) + dj]
                        stores[m][slot] = full[
                            di * BLK : (di + 1) * BLK, dj * BLK : (dj + 1) * BLK
                        ]
            return carry

        lax.fori_loop(counts[m][0], slots, clear, 0)
        lax.fori_loop(0, width // wide, column, 0)
        copies.append(
            pltpu.make_async_copy(stores[m].at[pl.ds(0, slots)], outs[m], sem.at[m])
        )
        copies[m].start()
    for copy in copies:
        copy.wait()


def block_grads(core, tables, counts, lefts, rights, left_whole, parts, slots, scale, *earlier):
    mats = len(tables)
    tokens = sum(a.shape[0] for a in (lefts if left_whole else rights))
    length, width = lefts[0].shape[-1], rights[0].shape[-1]
    wide = tile_of(width, 512)
    return pl.pallas_call(
        functools.partial(
            block_grad_kernel,
            parts,
            mats,
            len(lefts),
            len(rights),
            left_whole,
            scale,
            width // BLK,
            wide,
        ),
        out_shape=(jax.ShapeDtypeStruct((slots, BLK, BLK), jnp.bfloat16),) * mats,
        in_specs=[whole(SM)] * (1 + 2 * mats)
        + [whole(VM)] * (len(lefts) + len(rights))
        + [whole(pl.ANY)] * len(earlier),
        out_specs=(whole(pl.ANY),) * mats,
        scratch_shapes=[VM((slots + 1, BLK, BLK), jnp.bfloat16)] * mats
        + [VM((length, tokens), jnp.bfloat16), pltpu.SemaphoreType.DMA((mats,))],
        compiler_params=params(),
        cost_estimate=cost(2 * tokens * length * width * mats, slots * BLK * BLK * 2 * mats),
    )(core, *tables, *counts, *lefts, *rights, *earlier)


def shift(x, axis, by):
    n = lax.axis_size(axis)
    return lax.ppermute(x, axis, [(i, (i + by) % n) for i in range(n)])


def swap_cores(x):
    n = lax.axis_size("row")
    return lax.ppermute(x, "row", [(i, i ^ 1) for i in range(n)])


def add_up(parts):
    total = parts[0].astype(jnp.float32)
    for part in parts[1:]:
        total = total + part.astype(jnp.float32)
    return total


def z_order(n):
    return sorted(range(1, n), key=lambda d: (min(d, n - d), d))


def other_chips(sent):
    n = lax.axis_size("row")
    return [shift(sent, "row", 2 * s) for s in range(1, n // 2)]


def other_groups(x):
    return [shift(x, "dp", s) for s in range(1, lax.axis_size("dp"))]


def on_device(
    tokens, cotangent, gate_blocks, gate_index, up_blocks, up_index, down_blocks, down_index
):
    n_col = lax.axis_size("col")
    parts = 1
    chunks = n_col // parts
    core = lax.rem(lax.axis_index("row"), 2).astype(jnp.int32).reshape(1)
    feats = tokens.shape[1] // BLK
    units = FF // BLK // n_col
    width = units * BLK
    slots = gate_blocks.shape[2]
    group_rows = tokens.shape[0] * n_col
    scale = 1.0 / math.sqrt(group_rows * lax.axis_size("dp"))

    def gather(x):
        got = {0: x}
        for d in z_order(n_col):
            got[d] = shift(x, "col", d)
        return [
            jnp.concatenate([got[d] for d in range(p * chunks, (p + 1) * chunks)], axis=0)
            for p in range(parts)
        ]

    def scatter(cut, *earlier):
        kept = [cut[0]] + [shift(cut[d], "col", -d) for d in z_order(n_col)]
        return sum_chunks(kept, *earlier)

    def far_pieces(pairs):
        pieces = []
        for s in range(lax.axis_size("dp") - 1):
            for far in pairs:
                pieces += [far[s], swap_cores(far[s])]
        return pieces

    gate_table, gate_count = slot_table(gate_index, feats, units)
    up_table, up_count = slot_table(up_index, feats, units)
    down_table, down_count = slot_table(down_index, units, feats)

    x_parts = gather(tokens)
    x_whole = jnp.concatenate(x_parts, axis=0)
    (w_gate,) = densify((gate_table,), (gate_blocks[0, 0],), feats, units)
    gate_mine, gate_other = project(core, x_parts, [w_gate], False)
    gate_swapped = swap_cores(gate_other)
    gate_sent = pair_sum(gate_mine, gate_swapped)

    gate_got = other_chips(gate_sent)
    c_parts = gather(after(cotangent, x_whole))
    c_whole = jnp.concatenate(c_parts, axis=0)
    x_groups = [x_whole] + other_groups(x_whole)
    up_mine, up_other, w_up = project_blocks(
        core, x_whole, up_table, up_blocks[0, 0], feats, units, False, gate_sent
    )
    token = mark(up_other, *gate_got, c_whole, *x_groups[1:])
    up_swapped = swap_cores(up_other)
    up_sent = pair_sum(up_mine, up_swapped, token)

    up_got = other_chips(up_sent)
    c_groups = [c_whole] + other_groups(c_whole)
    back_mine, back_other, w_down = project_blocks(
        core, c_whole, down_table, down_blocks[0, 0], units, feats, True, up_sent
    )
    token = mark(back_other, *up_got, *c_groups[1:])
    hidden, by_gate, by_up = act(
        [gate_mine, gate_swapped] + gate_got, [up_mine, up_swapped] + up_got, token
    )
    back_swapped = swap_cores(back_other)
    back_sent = pair_sum(back_mine, back_swapped, hidden)

    back_got = other_chips(back_sent)
    hidden_far = other_groups(hidden)
    hidden_pieces = [hidden, swap_cores(hidden)]
    out_cut = back(core, hidden_pieces, [w_down], n_col, False, back_sent)
    hidden_far = [hold(far, out_cut[0]) for far in hidden_far]
    hidden_pieces += far_pieces([hidden_far])
    token = mark(out_cut[0], *back_got, *hidden_pieces[2:])
    grads = act_grads([back_mine, back_swapped] + back_got, by_gate, by_up, token)

    grads_far = other_groups(grads)
    grad_pieces = [grads, swap_cores(grads)]
    (down_grad,) = block_grads(
        core,
        (down_table,),
        (down_count,),
        hidden_pieces,
        c_groups,
        False,
        parts,
        slots,
        scale,
        grad_pieces[1],
    )
    in_cut = back(core, grad_pieces, [w_gate, w_up], n_col, True, down_grad)
    output = scatter(out_cut, in_cut[0])
    grads_far = [hold(far, output) for far in grads_far]
    gate_grad, up_grad = block_grads(
        core,
        (gate_table, up_table),
        (gate_count, up_count),
        x_groups,
        grad_pieces + far_pieces([grads_far]),
        True,
        parts,
        slots,
        scale,
    )
    input_grad = scatter(in_cut, gate_grad)
    shape = gate_blocks.shape
    return (
        output,
        input_grad,
        gate_grad.reshape(shape),
        up_grad.reshape(shape),
        down_grad.reshape(shape),
    )


def solution(mesh):
    return jax.shard_map(
        on_device,
        mesh=mesh,
        in_specs=(
            P(("dp", "col"), "row"),
            P(("dp", "col"), "row"),
            P("row", "col", None, None, None),
            P("row", "col", None, None),
            P("row", "col", None, None, None),
            P("row", "col", None, None),
            P("row", "col", None, None, None),
            P("row", "col", None, None),
        ),
        out_specs=(
            P(("dp", "col"), "row"),
            P(("dp", "col"), "row"),
            P("row", "col", None, None, None),
            P("row", "col", None, None, None),
            P("row", "col", None, None, None),
        ),
        check_vma=False,
    )
```

time: 1430 us -> 229 us (0.16)
  waiting for transfers between devices: 855 us -> 26.1 us
  local copies, waits for them, and re-layouts: 332 us -> 16.9 us
  matrix products: 166 us -> 0 us
  Pallas kernels: 0 us -> 144 us
  other arithmetic: 50.9 us -> 5.55 us
  starting transfers between devices: 0.98 us -> 34.4 us
    psum x1 -> x0, waiting for transfers between devices: 739 us -> none  [on_device(): lax.psum(gate_local.astype(jnp.bfloat16), 'dp').astype(jnp.float32)]
    dot_general x12 -> x0, matrix products: 166 us -> none  [the longest x3 70 us: dense_tools(): jnp.einsum('kr,kc,kab->racb', row_hot, col_hot, blocks, preferred_element...]
    pallas_call x0 -> x20, Pallas kernels: none -> 144 us  [the longest x2 47.6 us: block_grads(): pl.pallas_call(functools.partial(block_grad_kernel, parts, mats, len(left...]
    gather x3 -> x0, local copies, waits for them, and re-layouts: 93.6 us -> none  [block_grads(): picked = shaped[row_ids, col_ids]]
    unnamed x42 -> x64, local copies, waits for them, and re-layouts: 106 us -> 16.8 us
    reshape x3 -> x0, local copies, waits for them, and re-layouts: 73.8 us -> none  [block_grads(): full.reshape(row_count, width, col_count, width).transpose(0, 2, 1, 3)]
    reduce_scatter x4 -> x0, waiting for transfers between devices: 68.2 us -> none  [the longest x1 68.1 us: on_device(): lax.psum_scatter(jnp.concatenate([gate_fwd(panel_x), up_fwd(panel_x)], ax...]
    convert_element_type x3 -> x0, local copies, waits for them, and re-layouts: 58.5 us -> none  [dense_tools(): dense.astype(jnp.bfloat16).reshape(row_count * width, col_count * width)]
  transfers between devices with their start and end apart: 10 -> 26, of which waited for: 5 -> 7; matrix products, arithmetic and copies ran while one was open for 37% -> 3% of each run, Pallas kernels for 0% -> 56%
where the time goes in v2:
time: 229 us; the launch traced here: 228 us
  Pallas kernels  144 us (63%)
  starting transfers between devices  34.4 us (15%)
  waiting for transfers between devices  26.1 us (11%)
  local copies, waits for them, and re-layouts  16.9 us (7%)
  other arithmetic  5.55 us (2%)
    pallas_call x2, Pallas kernels, block_grads(): pl.pallas_call(functools.partial(block_grad_kernel, parts, mats, len(left...  47.6 us
    ppermute x19, starting transfers between devices, shift(): return lax.ppermute(x, axis, [(i, (i + by) % n) for i in range(n)])  34.2 us
    pallas_call x2, Pallas kernels, project_blocks(): pl.pallas_call(functools.partial(project_blocks_kernel, transposed, rows,...  26.2 us
    ppermute x19, waiting for transfers between devices, shift(): return lax.ppermute(x, axis, [(i, (i + by) % n) for i in range(n)])  26.1 us
    pallas_call x2, Pallas kernels, back(): pl.pallas_call(functools.partial(back_kernel, transposed, n_pieces, mats,...  24.9 us
    unnamed x64, local copies, waits for them, and re-layouts  16.8 us
    pallas_call x1, Pallas kernels, densify(): pl.pallas_call(functools.partial(densify_kernel, mats, rows, cols, panels...  10.8 us
    pallas_call x1, Pallas kernels, project(): pl.pallas_call(functools.partial(project_kernel, transposed, parts, mats,...  9.43 us
  transfers between devices with their start and end apart: 26, of which 7 were waited for; matrix products, arithmetic and copies ran while one was open for 3% of the time, Pallas kernels for 56%

profile of v2, /device:TPU:0, one launch (start us, length us, event | category | flops | bytes accessed | tf_op | source)
XLA Modules:
  0.0 228.2 jit_solution(4405122858079988082)
XLA Ops:
  0.6 4.1 %collective-permute-start.1 = (bf16[64,2048]{1,0:T(8,128)(2,1)}, bf16[64,2048]{1,0:T(8,128)(2,1)S(1)}, u32[]{:S(2)}, u32[]{:S(2)}) collective-permute-start(bf16[64,2048]{1,0:T(8,128)(2,1)} %param.8), channel_id=1, source_target_pairs={{0,2},{1,3},{2,0},{3,1},{4,6},{5,7},{6,4},{7,5},{8,10},{9,11},{10,... | collective-permute-start | bytes 786440 | tf_op jit(solution)/shard_map/ppermute | solution.py:511
  4.7 1.6 collective-permute-start
  6.3 2.2 collective-permute-start.2
  8.6 1.0 constant_dynamic-update-slice_fusion.3
  9.6 0.8 fusion.2
  10.3 0.8 fusion
  12.0 10.8 %shard_map.119.refs_1_.refs_2_ = bf16[2048,3584]{1,0:T(8,128)(2,1)} custom-call(s32[448]{0:T(512)} %broadcast_subtract_fusion.2.refs_0_.refs_1_, bf16[336,128,128]{2,1,0:T(8,128)(2,1)} %bitcast.14), custom_call_target="tpu_custom_call" | custom-call | bytes 25 | tf_op jit(solution)/shard_map/pallas_call | solution.py:110
  24.1 1.0 copy-done.1
  25.1 9.4 %shard_map.120 = (f32[128,3584]{1,0:T(8,128)}, bf16[128,3584]{1,0:T(8,128)(2,1)}) custom-call(s32[1]{0:T(128)} %bitcast.core_ref.refs_0_, bf16[256,2048]{1,0:T(8,128)(2,1)} %copy-done.1, bf16[2048,3584]{1,0:T(8,128)(2,1)} %shard_map.119.refs_1_.refs_2_), custom_call_target="tpu_custom_call" | custom-call | flops 3758 | bytes 14 | tf_op jit(solution)/shard_map/pallas_call | solution.py:178
  34.6 5.0 %collective-permute-start.6 = (bf16[64,2048]{1,0:T(8,128)(2,1)S(1)}, bf16[64,2048]{1,0:T(8,128)(2,1)S(1)}, u32[]{:S(2)}, u32[]{:S(2)}) collective-permute-start(bf16[64,2048]{1,0:T(8,128)(2,1)S(1)} %copy-done.19), channel_id=1, source_target_pairs={{0,1},{1,2},{2,3},{3,0},{4,5},{5,6},{6,7},{7,4},{8,9},{9,10},{10,1... | collective-permute-start | bytes 786440 | tf_op jit(solution)/shard_map/ppermute | solution.py:511
  40.2 1.8 collective-permute-start.7
  42.0 1.5 collective-permute-start.9
  43.5 1.0 copy-done.7
  44.4 2.8 %shard_map.121.refs_0_ = bf16[128,3584]{1,0:T(8,128)(2,1)} custom-call(f32[128,3584]{1,0:T(8,128)} %get-tuple-element.27.mine_ref.refs_0_, bf16[128,3584]{1,0:T(8,128)(2,1)} %copy-done.7), custom_call_target="tpu_custom_call" | custom-call | bytes 3 | tf_op jit(solution)/shard_map/pallas_call | solution.py:317
  47.2 1.5 collective-permute-start.4
  48.8 13.1 %shard_map.122 = (f32[128,3584]{1,0:T(8,128)}, bf16[128,3584]{1,0:T(8,128)(2,1)}, bf16[2048,3584]{1,0:T(8,128)(2,1)}) custom-call(s32[1]{0:T(128)} %bitcast.core_ref.refs_0_, s32[448]{0:T(512)} %broadcast_subtract_fusion.1.table.refs_2_, bf16[256,2048]{1,0:T(8,128)(2,1)} %copy-done.1, bf16[336,128,128]{2,1,0:T(8,128)(2,1)} %bitcast.16, ...), custom_call_target="tpu_custom_call" | custom-call | flops 3758 | bytes 29 | tf_op jit(solution)/shard_map/pallas_call | solution.py:238
  62.0 3.1 %collective-permute-start.8 = (bf16[64,2048]{1,0:T(8,128)(2,1)S(1)}, bf16[64,2048]{1,0:T(8,128)(2,1)S(1)}, u32[]{:S(2)}, u32[]{:S(2)}) collective-permute-start(bf16[64,2048]{1,0:T(8,128)(2,1)S(1)} %copy-done.19), channel_id=1, source_target_pairs={{0,3},{1,0},{2,1},{3,2},{4,7},{5,4},{6,5},{7,6},{8,11},{9,8},{10,9... | collective-permute-start | bytes 786440 | tf_op jit(solution)/shard_map/ppermute | solution.py:511
  65.2 6.2 %collective-permute-done.8 = bf16[64,2048]{1,0:T(8,128)(2,1)S(1)} collective-permute-done((bf16[64,2048]{1,0:T(8,128)(2,1)S(1)}, bf16[64,2048]{1,0:T(8,128)(2,1)S(1)}, u32[]{:S(2)}, u32[]{:S(2)}) %collective-permute-start.8) | collective-permute-done | bytes 262176 | tf_op jit(solution)/shard_map/ppermute | solution.py:511
  73.0 0.9 copy-done.8
  74.5 0.9 copy-done.9
  75.4 2.8 %shard_map.124.refs_0_ = bf16[128,3584]{1,0:T(8,128)(2,1)} custom-call(f32[128,3584]{1,0:T(8,128)} %get-tuple-element.29.mine_ref.refs_3_, bf16[128,3584]{1,0:T(8,128)(2,1)} %copy-done.9, f32[8,128]{1,0:T(8,128)} %shard_map.123.refs_0_), custom_call_target="tpu_custom_call" | custom-call | bytes 3 | tf_op jit(solution)/shard_map/pallas_call | solution.py:317
  79.3 13.1 %shard_map.125 = (f32[128,3584]{1,0:T(8,128)}, bf16[128,3584]{1,0:T(8,128)(2,1)}, bf16[3584,2048]{1,0:T(8,128)(2,1)}) custom-call(s32[1]{0:T(128)} %bitcast.core_ref.refs_0_, s32[448]{0:T(512)} %broadcast_subtract_fusion.table.refs_1_, bf16[256,2048]{1,0:T(8,128)(2,1)} %copy-done.2, bf16[336,128,128]{2,1,0:T(8,128)(2,1)} %bitcast.17, ...), custom_call_target="tpu_custom_call" | custom-call | flops 3758 | bytes 29 | tf_op jit(solution)/shard_map/pallas_call | solution.py:238
  92.5 3.7 %collective-permute-done.11.refs_2_.refs_8_ = bf16[256,2048]{1,0:T(8,128)(2,1)S(1)} collective-permute-done((bf16[256,2048]{1,0:T(8,128)(2,1)S(1)}, bf16[256,2048]{1,0:T(8,128)(2,1)S(1)}, u32[]{:S(2)}, u32[]{:S(2)}) %collective-permute-start.11) | collective-permute-done | bytes 1048608 | tf_op jit(solution)/shard_map/ppermute | solution.py:511
  96.2 3.9 %collective-permute-done.10.refs_1_.refs_5_ = bf16[128,3584]{1,0:T(8,128)(2,1)S(1)} collective-permute-done((bf16[128,3584]{1,0:T(8,128)(2,1)}, bf16[128,3584]{1,0:T(8,128)(2,1)S(1)}, u32[]{:S(2)}, u32[]{:S(2)}) %collective-permute-start.10) | collective-permute-done | bytes 917536 | tf_op jit(solution)/shard_map/ppermute | solution.py:511
  100.1 0.9 copy-done.10
  101.7 6.2 %shard_map.127 = (bf16[1,128,3584]{2,1,0:T(8,128)(2,1)}, f32[128,3584]{1,0:T(8,128)}, f32[128,3584]{1,0:T(8,128)}) custom-call(f32[128,3584]{1,0:T(8,128)} %get-tuple-element.27.mine_ref.refs_0_, bf16[128,3584]{1,0:T(8,128)(2,1)} %copy-done.7, bf16[128,3584]{1,0:T(8,128)(2,1)} %copy-done.8, f32[128,3584]{1,0:T(8,128)} %get-tuple-element.29.mine_ref.refs_3_, ...), custom_call_target="tpu_custom_call" | custom-call | bytes 13 | tf_op jit(solution)/shard_map/pallas_call | solution.py:391
  107.9 1.5 collective-permute-start.18
  109.4 0.9 copy-done.14
  110.3 2.8 %shard_map.128.refs_3_ = bf16[128,3584]{1,0:T(8,128)(2,1)} custom-call(f32[128,3584]{1,0:T(8,128)} %get-tuple-element.35.mine_ref.refs_0_, bf16[128,3584]{1,0:T(8,128)(2,1)} %copy-done.14, bf16[1,128,3584]{2,1,0:T(8,128)(2,1)} %get-tuple-element.33.refs_0_.refs_3_), custom_call_target="tpu_custom_call" | custom-call | bytes 3 | tf_op jit(solution)/shard_map/pallas_call | solution.py:317
  113.6 0.9 copy-done.13
  114.6 9.2 %shard_map.129 = (f32[64,2048]{1,0:T(8,128)}, bf16[64,2048]{1,0:T(8,128)(2,1)}, bf16[64,2048]{1,0:T(8,128)(2,1)}, bf16[64,2048]{1,0:T(8,128)(2,1)}) custom-call(s32[1]{0:T(128)} %bitcast.core_ref.refs_0_, bf16[1,128,3584]{2,1,0:T(8,128)(2,1)} %get-tuple-element.33.refs_0_.refs_3_, bf16[1,128,3584]{2,1,0:T(8,128)(2,1)} %copy-done.13, ...), custom_call_target="tpu_custom_call" | custom-call | flops 3758 | bytes 14 | tf_op jit(solution)/shard_map/pallas_call | solution.py:293
  123.8 7.0 %collective-permute-done.18.refs_0_ = bf16[1,128,3584]{2,1,0:T(8,128)(2,1)S(1)} collective-permute-done((bf16[1,128,3584]{2,1,0:T(8,128)(2,1)}, bf16[1,128,3584]{2,1,0:T(8,128)(2,1)S(1)}, u32[]{:S(2)}, u32[]{:S(2)}) %collective-permute-start.18) | collective-permute-done | bytes 917536 | tf_op jit(solution)/shard_map/ppermute | solution.py:511
  130.8 0.9 copy-done.3
  131.8 4.0 %collective-permute-done.17.refs_1_.refs_2_ = bf16[128,3584]{1,0:T(8,128)(2,1)S(1)} collective-permute-done((bf16[128,3584]{1,0:T(8,128)(2,1)}, bf16[128,3584]{1,0:T(8,128)(2,1)S(1)}, u32[]{:S(2)}, u32[]{:S(2)}) %collective-permute-start.17) | collective-permute-done | bytes 917536 | tf_op jit(solution)/shard_map/ppermute | solution.py:511
  135.8 0.9 copy-done.12
  136.8 0.9 copy-done.11
  138.3 4.9 %shard_map.132.refs_0_.refs_7_ = bf16[2,128,3584]{2,1,0:T(8,128)(2,1)} custom-call(f32[128,3584]{1,0:T(8,128)} %get-tuple-element.35.mine_ref.refs_0_, bf16[128,3584]{1,0:T(8,128)(2,1)} %copy-done.14, bf16[128,3584]{1,0:T(8,128)(2,1)} %copy-done.12, f32[128,3584]{1,0:T(8,128)} %get-tuple-element.40.refs_3_, f32[128,3584]{1,0:T(8,128)} %get-tuple-element.41.refs_4_, ...), custom_call_target="tpu_custom_call" | custom-call | bytes 9 | tf_op jit(solution)/shard_map/pallas_call | solution.py:413
  143.7 4.3 %collective-permute-start.14 = (bf16[64,2048]{1,0:T(8,128)(2,1)S(1)}, bf16[64,2048]{1,0:T(8,128)(2,1)S(1)}, u32[]{:S(2)}, u32[]{:S(2)}) collective-permute-start(bf16[64,2048]{1,0:T(8,128)(2,1)S(1)} %copy-done.25), channel_id=1, source_target_pairs={{0,3},{1,0},{2,1},{3,2},{4,7},{5,4},{6,5},{7,6},{8,11},{9,8},{10,9... | collective-permute-start | bytes 786440 | tf_op jit(solution)/shard_map/ppermute | solution.py:511
  149.2 1.2 copy-done
  150.5 18.0 %shard_map.133.refs_4_ = bf16[336,128,128]{2,1,0:T(8,128)(2,1)} custom-call(s32[1]{0:T(128)} %bitcast.core_ref.refs_0_, s32[448]{0:T(512)} %broadcast_subtract_fusion.table.refs_1_, s32[1]{0:T(128)} %bitcast.7.refs_2_, bf16[1,128,3584]{2,1,0:T(8,128)(2,1)} %get-tuple-element.33.refs_0_.refs_3_, bf16[1,128,3584]{2,1,0:T(8,128)(2,1)} %copy-done.13, ...), custom_call_target="tpu_custom_call" | custom-call | flops 7516 | bytes 11 | tf_op jit(solution)/shard_map/pallas_call | solution.py:485
  168.5 15.6 %shard_map.134 = (f32[64,2048]{1,0:T(8,128)}, bf16[64,2048]{1,0:T(8,128)(2,1)}, bf16[64,2048]{1,0:T(8,128)(2,1)}, bf16[64,2048]{1,0:T(8,128)(2,1)}) custom-call(s32[1]{0:T(128)} %bitcast.core_ref.refs_0_, bf16[2,128,3584]{2,1,0:T(8,128)(2,1)} %shard_map.132.refs_0_.refs_7_, bf16[2,128,3584]{2,1,0:T(8,128)(2,1)} %copy-done, ...), custom_call_target="tpu_custom_call" | custom-call | flops 7516 | bytes 29 | tf_op jit(solution)/shard_map/pallas_call | solution.py:293
  185.0 2.1 shard_map.135.refs_1_
  187.1 1.2 copy-done.4
  188.3 2.9 %collective-permute-start.21 = (bf16[64,2048]{1,0:T(8,128)(2,1)S(1)}, bf16[64,2048]{1,0:T(8,128)(2,1)S(1)}, u32[]{:S(2)}, u32[]{:S(2)}) collective-permute-start(bf16[64,2048]{1,0:T(8,128)(2,1)S(1)} %copy-done.28), channel_id=1, source_target_pairs={{0,3},{1,0},{2,1},{3,2},{4,7},{5,4},{6,5},{7,6},{8,11},{9,8},{10,9... | collective-permute-start | bytes 786440 | tf_op jit(solution)/shard_map/ppermute | solution.py:511
  191.7 1.4 collective-permute-start.23
  194.4 1.2 copy-done.15
  195.7 29.5 %shard_map.137 = (bf16[336,128,128]{2,1,0:T(8,128)(2,1)}, bf16[336,128,128]{2,1,0:T(8,128)(2,1)}) custom-call(s32[1]{0:T(128)} %bitcast.core_ref.refs_0_, s32[448]{0:T(512)} %broadcast_subtract_fusion.2.refs_0_.refs_1_, s32[448]{0:T(512)} %broadcast_subtract_fusion.1.table.refs_2_, s32[1]{0:T(128)} %bitcast.8.refs_3_, s32[1]{0:T(128)} %bitcast.9.refs_4_, ...), custom_call_target="tpu_custom_call" | custom-call | flops 15032 | bytes 22 | tf_op jit(solution)/shard_map/pallas_call | solution.py:485
  226.1 2.1 shard_map.138
  (100 shorter events, 13.2 us)
Async XLA Ops:
  0.6 22.7 %collective-permute-start.1 = (bf16[64,2048]{1,0:T(8,128)(2,1)}, bf16[64,2048]{1,0:T(8,128)(2,1)S(1)}, u32[]{:S(2)}, u32[]{:S(2)}) collective-permute-start(bf16[64,2048]{1,0:T(8,128)(2,1)} %param.8), channel_id=1, source_target_pairs={{0,2},{1,3},{2,0},{3,1},{4,6},{5,7},{6,4},{7,5},{8,10},{9,11},{10,... | collective-permute-start | bytes 786440 | tf_op jit(solution)/shard_map/ppermute | solution.py:511
  4.7 18.1 %collective-permute-start = (bf16[64,2048]{1,0:T(8,128)(2,1)}, bf16[64,2048]{1,0:T(8,128)(2,1)S(1)}, u32[]{:S(2)}, u32[]{:S(2)}) collective-permute-start(bf16[64,2048]{1,0:T(8,128)(2,1)} %param.8), channel_id=1, source_target_pairs={{0,1},{1,2},{2,3},{3,0},{4,5},{5,6},{6,7},{7,4},{8,9},{9,10},{10,1... | collective-permute-start | bytes 786440 | tf_op jit(solution)/shard_map/ppermute | solution.py:511
  6.3 17.8 %collective-permute-start.2 = (bf16[64,2048]{1,0:T(8,128)(2,1)}, bf16[64,2048]{1,0:T(8,128)(2,1)S(1)}, u32[]{:S(2)}, u32[]{:S(2)}) collective-permute-start(bf16[64,2048]{1,0:T(8,128)(2,1)} %param.8), channel_id=1, source_target_pairs={{0,3},{1,0},{2,1},{3,2},{4,7},{5,4},{6,5},{7,6},{8,11},{9,8},{10,9... | collective-permute-start | bytes 786440 | tf_op jit(solution)/shard_map/ppermute | solution.py:511
  24.1 1.0 copy-start.1
  25.1 9.5 %copy-start.19 = (bf16[64,2048]{1,0:T(8,128)(2,1)S(1)}, bf16[64,2048]{1,0:T(8,128)(2,1)}, u32[]{:S(2)}) copy-start(bf16[64,2048]{1,0:T(8,128)(2,1)} %param.9) | copy-start | bytes 786436
  34.5 8.9 %collective-permute-start.3 = (bf16[128,3584]{1,0:T(8,128)(2,1)}, bf16[128,3584]{1,0:T(8,128)(2,1)S(1)}, u32[]{:S(2)}, u32[]{:S(2)}) collective-permute-start(bf16[128,3584]{1,0:T(8,128)(2,1)} %get-tuple-element.28), channel_id=1, source_target_pairs={{0,4},{4,0},{8,12},{12,8},{1,5},{5,1},{9,13},{13,9},{2,6},{6,2},{1... | collective-permute-start | bytes 2752520 | tf_op jit(solution)/shard_map/ppermute | solution.py:516
  34.6 27.3 %collective-permute-start.6 = (bf16[64,2048]{1,0:T(8,128)(2,1)S(1)}, bf16[64,2048]{1,0:T(8,128)(2,1)S(1)}, u32[]{:S(2)}, u32[]{:S(2)}) collective-permute-start(bf16[64,2048]{1,0:T(8,128)(2,1)S(1)} %copy-done.19), channel_id=1, source_target_pairs={{0,1},{1,2},{2,3},{3,0},{4,5},{5,6},{6,7},{7,4},{8,9},{9,10},{10,1... | collective-permute-start | bytes 786440 | tf_op jit(solution)/shard_map/ppermute | solution.py:511
  40.2 25.0 %collective-permute-start.7 = (bf16[64,2048]{1,0:T(8,128)(2,1)S(1)}, bf16[64,2048]{1,0:T(8,128)(2,1)S(1)}, u32[]{:S(2)}, u32[]{:S(2)}) collective-permute-start(bf16[64,2048]{1,0:T(8,128)(2,1)S(1)} %copy-done.19), channel_id=1, source_target_pairs={{0,2},{1,3},{2,0},{3,1},{4,6},{5,7},{6,4},{7,5},{8,10},{9,11},{10,... | collective-permute-start | bytes 786440 | tf_op jit(solution)/shard_map/ppermute | solution.py:511
  42.0 30.0 %collective-permute-start.9 = (bf16[256,2048]{1,0:T(8,128)(2,1)}, bf16[256,2048]{1,0:T(8,128)(2,1)S(1)}, u32[]{:S(2)}, u32[]{:S(2)}) collective-permute-start(bf16[256,2048]{1,0:T(8,128)(2,1)} %copy-done.1), channel_id=1, source_target_pairs={{0,16},{16,0},{1,17},{17,1},{2,18},{18,2},{3,19},{19,3},{4,20},{20... | collective-permute-start | bytes 3145736 | tf_op jit(solution)/shard_map/ppermute | solution.py:511
  43.5 1.0 copy-start.7
  47.2 24.7 %collective-permute-start.4 = (bf16[128,3584]{1,0:T(8,128)(2,1)}, bf16[128,3584]{1,0:T(8,128)(2,1)S(1)}, u32[]{:S(2)}, u32[]{:S(2)}) collective-permute-start(bf16[128,3584]{1,0:T(8,128)(2,1)} %shard_map.121.refs_0_), channel_id=1, source_target_pairs={{0,8},{4,12},{8,0},{12,4},{1,9},{5,13},{9,1},{13,5},{2,10},{6,14},... | collective-permute-start | bytes 2752520 | tf_op jit(solution)/shard_map/ppermute | solution.py:511
  61.8 12.6 %collective-permute-start.5 = (bf16[128,3584]{1,0:T(8,128)(2,1)}, bf16[128,3584]{1,0:T(8,128)(2,1)S(1)}, u32[]{:S(2)}, u32[]{:S(2)}) collective-permute-start(bf16[128,3584]{1,0:T(8,128)(2,1)} %get-tuple-element.30.refs_0_), channel_id=1, source_target_pairs={{0,4},{4,0},{8,12},{12,8},{1,5},{5,1},{9,13},{13,9},{2,6},{6,2},{1... | collective-permute-start | bytes 2752520 | tf_op jit(solution)/shard_map/ppermute | solution.py:516
  62.0 9.4 %collective-permute-start.8 = (bf16[64,2048]{1,0:T(8,128)(2,1)S(1)}, bf16[64,2048]{1,0:T(8,128)(2,1)S(1)}, u32[]{:S(2)}, u32[]{:S(2)}) collective-permute-start(bf16[64,2048]{1,0:T(8,128)(2,1)S(1)} %copy-done.19), channel_id=1, source_target_pairs={{0,3},{1,0},{2,1},{3,2},{4,7},{5,4},{6,5},{7,6},{8,11},{9,8},{10,9... | collective-permute-start | bytes 786440 | tf_op jit(solution)/shard_map/ppermute | solution.py:511
  71.3 1.0 copy-start.2
  71.4 24.8 %collective-permute-start.11 = (bf16[256,2048]{1,0:T(8,128)(2,1)S(1)}, bf16[256,2048]{1,0:T(8,128)(2,1)S(1)}, u32[]{:S(2)}, u32[]{:S(2)}) collective-permute-start(bf16[256,2048]{1,0:T(8,128)(2,1)S(1)} %constant_dynamic-update-slice_fusion.4.refs_2_.panel_ref.refs_7_), channel_id=1, source_target_pairs={{0,16},{16,0},{1,17},{17,1},{2,18},{18,2},{3,19},{19,3},{4,20},{20... | collective-permute-start | bytes 3145736 | tf_op jit(solution)/shard_map/ppermute | solution.py:511
  72.0 1.0 copy-start.5
  73.0 0.9 copy-start.8
  74.5 0.9 copy-start.9
  78.2 21.9 %collective-permute-start.10 = (bf16[128,3584]{1,0:T(8,128)(2,1)}, bf16[128,3584]{1,0:T(8,128)(2,1)S(1)}, u32[]{:S(2)}, u32[]{:S(2)}) collective-permute-start(bf16[128,3584]{1,0:T(8,128)(2,1)} %shard_map.124.refs_0_), channel_id=1, source_target_pairs={{0,8},{4,12},{8,0},{12,4},{1,9},{5,13},{9,1},{13,5},{2,10},{6,14},... | collective-permute-start | bytes 2752520 | tf_op jit(solution)/shard_map/ppermute | solution.py:511
  92.4 17.0 %collective-permute-start.13 = (bf16[128,3584]{1,0:T(8,128)(2,1)}, bf16[128,3584]{1,0:T(8,128)(2,1)S(1)}, u32[]{:S(2)}, u32[]{:S(2)}) collective-permute-start(bf16[128,3584]{1,0:T(8,128)(2,1)} %get-tuple-element.32.refs_0_), channel_id=1, source_target_pairs={{0,4},{4,0},{8,12},{12,8},{1,5},{5,1},{9,13},{13,9},{2,6},{6,2},{1... | collective-permute-start | bytes 2752520 | tf_op jit(solution)/shard_map/ppermute | solution.py:516
  96.2 3.9 %copy-start.6 = (bf16[256,2048]{1,0:T(8,128)(2,1)}, bf16[256,2048]{1,0:T(8,128)(2,1)S(1)}, u32[]{:S(2)}) copy-start(bf16[256,2048]{1,0:T(8,128)(2,1)S(1)} %collective-permute-done.11.refs_2_.refs_8_) | copy-start | bytes 3145732
  100.1 0.9 copy-start.10
  107.9 5.8 %collective-permute-start.12 = (bf16[1,128,3584]{2,1,0:T(8,128)(2,1)}, bf16[1,128,3584]{2,1,0:T(8,128)(2,1)S(1)}, u32[]{:S(2)}, u32[]{:S(2)}) collective-permute-start(bf16[1,128,3584]{2,1,0:T(8,128)(2,1)} %get-tuple-element.33.refs_0_.refs_3_), channel_id=1, source_target_pairs={{0,4},{4,0},{8,12},{12,8},{1,5},{5,1},{9,13},{13,9},{2,6},{6,2},{1... | collective-permute-start | bytes 2752520 | tf_op jit(solution)/shard_map/ppermute | solution.py:516
  107.9 23.0 %collective-permute-start.18 = (bf16[1,128,3584]{2,1,0:T(8,128)(2,1)}, bf16[1,128,3584]{2,1,0:T(8,128)(2,1)S(1)}, u32[]{:S(2)}, u32[]{:S(2)}) collective-permute-start(bf16[1,128,3584]{2,1,0:T(8,128)(2,1)} %get-tuple-element.33.refs_0_.refs_3_), channel_id=1, source_target_pairs={{0,16},{16,0},{1,17},{17,1},{2,18},{18,2},{3,19},{19,3},{4,20},{20... | collective-permute-start | bytes 2752520 | tf_op jit(solution)/shard_map/ppermute | solution.py:511
  109.4 0.9 copy-start.14
  113.1 22.7 %collective-permute-start.17 = (bf16[128,3584]{1,0:T(8,128)(2,1)}, bf16[128,3584]{1,0:T(8,128)(2,1)S(1)}, u32[]{:S(2)}, u32[]{:S(2)}) collective-permute-start(bf16[128,3584]{1,0:T(8,128)(2,1)} %shard_map.128.refs_3_), channel_id=1, source_target_pairs={{0,8},{4,12},{8,0},{12,4},{1,9},{5,13},{9,1},{13,5},{2,10},{6,14},... | collective-permute-start | bytes 2752520 | tf_op jit(solution)/shard_map/ppermute | solution.py:511
  113.6 0.9 copy-start.13
  130.8 0.9 copy-start.3
  131.8 4.0 %collective-permute-start.19 = (bf16[1,128,3584]{2,1,0:T(8,128)(2,1)}, bf16[1,128,3584]{2,1,0:T(8,128)(2,1)S(1)}, u32[]{:S(2)}, u32[]{:S(2)}) collective-permute-start(bf16[1,128,3584]{2,1,0:T(8,128)(2,1)} %shard_map.130.refs_2_.refs_5_), channel_id=1, source_target_pairs={{0,4},{4,0},{8,12},{12,8},{1,5},{5,1},{9,13},{13,9},{2,6},{6,2},{1... | collective-permute-start | bytes 2752520 | tf_op jit(solution)/shard_map/ppermute | solution.py:516
  135.8 0.9 copy-start.12
  138.3 5.4 %copy-start.25 = (bf16[64,2048]{1,0:T(8,128)(2,1)S(1)}, bf16[64,2048]{1,0:T(8,128)(2,1)}, u32[]{:S(2)}) copy-start(bf16[64,2048]{1,0:T(8,128)(2,1)} %get-tuple-element.37) | copy-start | bytes 786436
  138.3 9.7 %copy-start.24 = (bf16[64,2048]{1,0:T(8,128)(2,1)S(1)}, bf16[64,2048]{1,0:T(8,128)(2,1)}, u32[]{:S(2)}) copy-start(bf16[64,2048]{1,0:T(8,128)(2,1)} %get-tuple-element.38) | copy-start | bytes 786436
  138.3 9.7 %copy-start.23 = (bf16[64,2048]{1,0:T(8,128)(2,1)S(1)}, bf16[64,2048]{1,0:T(8,128)(2,1)}, u32[]{:S(2)}) copy-start(bf16[64,2048]{1,0:T(8,128)(2,1)} %get-tuple-element.39) | copy-start | bytes 786436
  143.1 6.1 %collective-permute-start.20 = (bf16[2,128,3584]{2,1,0:T(8,128)(2,1)}, bf16[2,128,3584]{2,1,0:T(8,128)(2,1)S(1)}, u32[]{:S(2)}, u32[]{:S(2)}) collective-permute-start(bf16[2,128,3584]{2,1,0:T(8,128)(2,1)} %shard_map.132.refs_0_.refs_7_), channel_id=1, source_target_pairs={{0,4},{4,0},{8,12},{12,8},{1,5},{5,1},{9,13},{13,9},{2,6},{6,2},{1... | collective-permute-start | bytes 5505032 | tf_op jit(solution)/shard_map/ppermute | solution.py:516
  143.1 44.0 %collective-permute-start.24 = (bf16[2,128,3584]{2,1,0:T(8,128)(2,1)}, bf16[2,128,3584]{2,1,0:T(8,128)(2,1)S(1)}, u32[]{:S(2)}, u32[]{:S(2)}) collective-permute-start(bf16[2,128,3584]{2,1,0:T(8,128)(2,1)} %shard_map.132.refs_0_.refs_7_), channel_id=1, source_target_pairs={{0,16},{16,0},{1,17},{17,1},{2,18},{18,2},{3,19},{19,3},{4,20},{20... | collective-permute-start | bytes 5505032 | tf_op jit(solution)/shard_map/ppermute | solution.py:511
  143.7 40.5 %collective-permute-start.14 = (bf16[64,2048]{1,0:T(8,128)(2,1)S(1)}, bf16[64,2048]{1,0:T(8,128)(2,1)S(1)}, u32[]{:S(2)}, u32[]{:S(2)}) collective-permute-start(bf16[64,2048]{1,0:T(8,128)(2,1)S(1)} %copy-done.25), channel_id=1, source_target_pairs={{0,3},{1,0},{2,1},{3,2},{4,7},{5,4},{6,5},{7,6},{8,11},{9,8},{10,9... | collective-permute-start | bytes 786440 | tf_op jit(solution)/shard_map/ppermute | solution.py:511
  148.0 36.2 %collective-permute-start.15 = (bf16[64,2048]{1,0:T(8,128)(2,1)S(1)}, bf16[64,2048]{1,0:T(8,128)(2,1)S(1)}, u32[]{:S(2)}, u32[]{:S(2)}) collective-permute-start(bf16[64,2048]{1,0:T(8,128)(2,1)S(1)} %copy-done.24), channel_id=1, source_target_pairs={{0,1},{1,2},{2,3},{3,0},{4,5},{5,6},{6,7},{7,4},{8,9},{9,10},{10,1... | collective-permute-start | bytes 786440 | tf_op jit(solution)/shard_map/ppermute | solution.py:511
  148.0 36.2 %collective-permute-start.16 = (bf16[64,2048]{1,0:T(8,128)(2,1)S(1)}, bf16[64,2048]{1,0:T(8,128)(2,1)S(1)}, u32[]{:S(2)}, u32[]{:S(2)}) collective-permute-start(bf16[64,2048]{1,0:T(8,128)(2,1)S(1)} %copy-done.23), channel_id=1, source_target_pairs={{0,2},{1,3},{2,0},{3,1},{4,6},{5,7},{6,4},{7,5},{8,10},{9,11},{10,... | collective-permute-start | bytes 786440 | tf_op jit(solution)/shard_map/ppermute | solution.py:511
  149.2 1.2 copy-start
  187.1 1.2 copy-start.28
  187.1 4.2 %copy-start.27 = (bf16[64,2048]{1,0:T(8,128)(2,1)S(1)}, bf16[64,2048]{1,0:T(8,128)(2,1)}, u32[]{:S(2)}) copy-start(bf16[64,2048]{1,0:T(8,128)(2,1)} %get-tuple-element.45) | copy-start | bytes 786436
  187.1 4.6 %copy-start.26 = (bf16[64,2048]{1,0:T(8,128)(2,1)S(1)}, bf16[64,2048]{1,0:T(8,128)(2,1)}, u32[]{:S(2)}) copy-start(bf16[64,2048]{1,0:T(8,128)(2,1)} %get-tuple-element.46) | copy-start | bytes 786436
  187.1 1.2 copy-start.4
  188.3 6.1 %collective-permute-start.25 = (bf16[2,128,3584]{2,1,0:T(8,128)(2,1)}, bf16[2,128,3584]{2,1,0:T(8,128)(2,1)S(1)}, u32[]{:S(2)}, u32[]{:S(2)}) collective-permute-start(bf16[2,128,3584]{2,1,0:T(8,128)(2,1)} %shard_map.136.refs_9_), channel_id=1, source_target_pairs={{0,4},{4,0},{8,12},{12,8},{1,5},{5,1},{9,13},{13,9},{2,6},{6,2},{1... | collective-permute-start | bytes 5505032 | tf_op jit(solution)/shard_map/ppermute | solution.py:516
  188.3 36.9 %collective-permute-start.21 = (bf16[64,2048]{1,0:T(8,128)(2,1)S(1)}, bf16[64,2048]{1,0:T(8,128)(2,1)S(1)}, u32[]{:S(2)}, u32[]{:S(2)}) collective-permute-start(bf16[64,2048]{1,0:T(8,128)(2,1)S(1)} %copy-done.28), channel_id=1, source_target_pairs={{0,3},{1,0},{2,1},{3,2},{4,7},{5,4},{6,5},{7,6},{8,11},{9,8},{10,9... | collective-permute-start | bytes 786440 | tf_op jit(solution)/shard_map/ppermute | solution.py:511
  191.3 34.0 %collective-permute-start.22 = (bf16[64,2048]{1,0:T(8,128)(2,1)S(1)}, bf16[64,2048]{1,0:T(8,128)(2,1)S(1)}, u32[]{:S(2)}, u32[]{:S(2)}) collective-permute-start(bf16[64,2048]{1,0:T(8,128)(2,1)S(1)} %copy-done.27), channel_id=1, source_target_pairs={{0,1},{1,2},{2,3},{3,0},{4,5},{5,6},{6,7},{7,4},{8,9},{9,10},{10,1... | collective-permute-start | bytes 786440 | tf_op jit(solution)/shard_map/ppermute | solution.py:511
  191.7 33.6 %collective-permute-start.23 = (bf16[64,2048]{1,0:T(8,128)(2,1)S(1)}, bf16[64,2048]{1,0:T(8,128)(2,1)S(1)}, u32[]{:S(2)}, u32[]{:S(2)}) collective-permute-start(bf16[64,2048]{1,0:T(8,128)(2,1)S(1)} %copy-done.26), channel_id=1, source_target_pairs={{0,2},{1,3},{2,0},{3,1},{4,6},{5,7},{6,4},{7,5},{8,10},{9,11},{10,... | collective-permute-start | bytes 786440 | tf_op jit(solution)/shard_map/ppermute | solution.py:511
  194.4 1.2 copy-start.15
  (7 other events, 5.5 us)

commit v3 on v2

--- a/solution.py
+++ b/solution.py
@@ -10,9 +10,12 @@
 
 BLK = 128
 AHEAD = 3
+PROJECT_TILE = 512
+BACK_TILE = 512
+GRAD_WIDE = 512
+POINT_WIDE = 1792
 COST = 0.000001
 MARK = 200000
-WIDE = 1792
 FF = 14336
 VMEM_LIMIT = 56 * 1024 * 1024
 VM = pltpu.VMEM
@@ -39,15 +42,6 @@
 
 def whole(memory_space):
     return pl.BlockSpec(memory_space=memory_space)
-
-
-def natural_to_own(core, parts, ref, columns=slice(None)):
-    rows = ref.shape[0] // (2 * parts)
-    pieces = []
-    for p in range(parts):
-        pieces.append(ref[rows_at((2 * p + core) * rows, rows), columns])
-        pieces.append(ref[rows_at((2 * p + 1 - core) * rows, rows), columns])
-    return pieces
 
 
 def after(x, *earlier):
@@ -123,24 +117,20 @@
     )(*tables, *blocks, *earlier)
 
 
-def stream(weights, stores, sem, tile, transposed, by_tile, ahead):
-    length = weights[0].shape[0] if transposed else weights[0].shape[1]
-    order = [(i, w) for i in range(length // tile) for w in range(len(weights))]
-    if not by_tile:
-        order.sort(key=lambda pair: pair[1])
-
-    def copy(i, w):
-        at = (pl.ds(i * tile, tile),) if transposed else (slice(None), pl.ds(i * tile, tile))
-        return pltpu.make_async_copy(weights[w].at[at], stores[w].at[at], sem.at[w, i])
-
-    for pair in order[:ahead]:
-        copy(*pair).start()
-    for n, (i, w) in enumerate(order):
-        copy(i, w).wait()
-        if n + ahead < len(order):
-            copy(*order[n + ahead]).start()
-        place = pl.ds(i * tile, tile)
-        yield i, w, (stores[w].at[place] if transposed else stores[w].at[:, place])
+def stream(copies, first):
+    for copy in first:
+        copy.start()
+    copies[0].start()
+    for copy in first:
+        copy.wait()
+    for n, copy in enumerate(copies):
+        if n == 0:
+            for ahead in copies[1:AHEAD]:
+                ahead.start()
+        copy.wait()
+        if n + AHEAD < len(copies):
+            copies[n + AHEAD].start()
+        yield n
 
 
 def product(panel, held, transposed):
@@ -148,59 +138,61 @@
     return lax.dot_general(panel, held[...], dims, preferred_element_type=jnp.float32)
 
 
-def project_kernel(transposed, parts, mats, tile, core_ref, *refs):
-    panels, weights = refs[:parts], refs[parts : parts + mats]
-    outs = refs[-1 - mats - 2 * parts : -1 - mats]
-    stores, sem = refs[-1 - mats : -1], refs[-1]
+def project_kernel(transposed, tile, core_ref, panel, weight, *refs):
+    mine_ref, other_ref = refs[-5:-3]
+    held_panel, store, sem = refs[-3:]
+    load = pltpu.make_async_copy(panel, held_panel, sem.at[0])
     is_first = core_ref[0] == 0
-    half = panels[0].shape[0] // 2
-    width = outs[0].shape[1] // mats
-    panel = jnp.concatenate([ref[...] for ref in panels], axis=0)
-    for i, w, held in stream(weights, stores, sem, tile, transposed, False, AHEAD):
-        full = product(panel, held, transposed)
-        span = slice(w * width + i * tile, w * width + (i + 1) * tile)
-        for p in range(parts):
-            first = full[2 * p * half : (2 * p + 1) * half]
-            second = full[(2 * p + 1) * half : (2 * p + 2) * half]
-            outs[2 * p][:, span] = jnp.where(is_first, first, second)
-            outs[2 * p + 1][:, span] = jnp.where(is_first, second, first).astype(jnp.bfloat16)
-
-
-def project(core, panels, weights, transposed, *earlier):
-    parts, mats = len(panels), len(weights)
-    tokens, depth = panels[0].shape
-    width = weights[0].shape[0] if transposed else weights[0].shape[1]
-    tile = tile_of(width, 512)
-    shapes = (
-        jax.ShapeDtypeStruct((tokens // 2, mats * width), jnp.float32),
-        jax.ShapeDtypeStruct((tokens // 2, mats * width), jnp.bfloat16),
-    )
-    return pl.pallas_call(
-        functools.partial(project_kernel, transposed, parts, mats, tile),
-        out_shape=shapes * parts,
-        in_specs=[whole(SM)]
-        + [whole(VM)] * parts
-        + [whole(pl.ANY)] * (mats + len(earlier)),
-        out_specs=(whole(VM),) * (2 * parts),
-        scratch_shapes=[VM(w.shape, jnp.bfloat16) for w in weights]
-        + [pltpu.SemaphoreType.DMA((mats, width // tile))],
-        compiler_params=params(),
-        cost_estimate=cost(
-            2 * parts * tokens * depth * width * mats, 2 * depth * width * mats
+    half = panel.shape[0] // 2
+    spans = [pl.ds(i * tile, tile) for i in range(mine_ref.shape[1] // tile)]
+    places = [(at,) if transposed else (slice(None), at) for at in spans]
+    copies = [
+        pltpu.make_async_copy(weight.at[at], store.at[at], sem.at[1 + i])
+        for i, at in enumerate(places)
+    ]
+    for i in stream(copies, [load]):
+        full = product(held_panel[...], store.at[places[i]], transposed)
+        first, second = full[:half], full[half:]
+        mine_ref[:, spans[i]] = jnp.where(is_first, first, second)
+        other_ref[:, spans[i]] = jnp.where(is_first, second, first).astype(jnp.bfloat16)
+
+
+def project(core, panel, weight, transposed, *earlier):
+    tokens, depth = panel.shape
+    width = weight.shape[0] if transposed else weight.shape[1]
+    tile = tile_of(width, PROJECT_TILE)
+    shape = (tokens // 2, width)
+    return pl.pallas_call(
+        functools.partial(project_kernel, transposed, tile),
+        out_shape=(
+            jax.ShapeDtypeStruct(shape, jnp.float32),
+            jax.ShapeDtypeStruct(shape, jnp.bfloat16),
         ),
-    )(core, *panels, *weights, *earlier)
-
-
-def project_blocks_kernel(transposed, rows, cols, high, ring, core_ref, table, panel_ref, blocks, *refs):
-    mine_ref, other_ref, dense = refs[-7:-4]
-    store, stage, in_sem, out_sem = refs[-4:]
+        in_specs=[whole(SM)] + [whole(pl.ANY)] * (2 + len(earlier)),
+        out_specs=(whole(VM),) * 2,
+        scratch_shapes=[
+            VM(panel.shape, jnp.bfloat16),
+            VM(weight.shape, jnp.bfloat16),
+            pltpu.SemaphoreType.DMA((1 + width // tile,)),
+        ],
+        compiler_params=params(),
+        cost_estimate=cost(2 * tokens * depth * width, 2 * depth * width),
+    )(core, panel, weight, *earlier)
+
+
+def project_blocks_kernel(transposed, rows, cols, high, ring, core_ref, table, panel, blocks, *refs):
+    mine_ref, other_ref, dense = refs[-8:-5]
+    store, panel_ref, stage, in_sem, out_sem = refs[-5:]
     slots = blocks.shape[0]
-    load = pltpu.make_async_copy(blocks, store.at[pl.ds(0, slots)], in_sem)
+    load = pltpu.make_async_copy(blocks, store.at[pl.ds(0, slots)], in_sem.at[0])
     load.start()
+    load_panel = pltpu.make_async_copy(panel, panel_ref, in_sem.at[1])
+    load_panel.start()
     store[slots] = jnp.zeros((BLK, BLK), jnp.bfloat16)
     is_first = core_ref[0] == 0
     half = panel_ref.shape[0] // 2
     load.wait()
+    load_panel.wait()
     writes = []
     for i in range((rows if transposed else cols) // high):
         held = stage.at[i % ring]
@@ -242,12 +234,13 @@
             jax.ShapeDtypeStruct(shape, jnp.bfloat16),
             jax.ShapeDtypeStruct((rows * BLK, cols * BLK), jnp.bfloat16),
         ),
-        in_specs=[whole(SM)] * 2 + [whole(VM)] + [whole(pl.ANY)] * (1 + len(earlier)),
+        in_specs=[whole(SM)] * 2 + [whole(pl.ANY)] * (2 + len(earlier)),
         out_specs=(whole(VM), whole(VM), whole(pl.ANY)),
         scratch_shapes=[
             VM((slots + 1, BLK, BLK), jnp.bfloat16),
+            VM(panel.shape, jnp.bfloat16),
             VM((ring, *tile_shape), jnp.bfloat16),
-            pltpu.SemaphoreType.DMA,
+            pltpu.SemaphoreType.DMA((2,)),
             pltpu.SemaphoreType.DMA((ring,)),
         ],
         compiler_params=params(),
@@ -257,34 +250,45 @@
 
 def back_kernel(transposed, n_pieces, mats, chunks, tile, core_ref, *refs):
     pieces, weights = refs[:n_pieces], refs[n_pieces : n_pieces + mats]
-    outs = refs[-1 - mats - chunks : -1 - mats]
-    stores, sem = refs[-1 - mats : -1], refs[-1]
+    outs = refs[-4 - chunks : -4]
+    store, panel, sem, piece_sem = refs[-4:]
+    half, depth = pieces[0].shape[1:]
+    loads = [
+        pltpu.make_async_copy(
+            piece.at[w],
+            panel.at[pl.ds(k * half, half), pl.ds(w * depth, depth)],
+            piece_sem.at[w * n_pieces + k],
+        )
+        for w in range(mats)
+        for k, piece in enumerate(pieces)
+    ]
     is_first = core_ref[0] == 0
-    half = pieces[0].shape[1]
     rows = n_pieces * half // chunks
-    panels = [jnp.concatenate([ref[w] for ref in pieces], axis=0) for w in range(mats)]
-    total = None
-    for i, w, held in stream(weights, stores, sem, tile, transposed, True, AHEAD):
-        part = product(panels[w], held, transposed)
-        total = part if w == 0 else total + part
-        if w < mats - 1:
+    copies = []
+    for i in range(outs[0].shape[1] // tile):
+        at = pl.ds(i * tile, tile)
+        for w, weight in enumerate(weights):
+            deep = pl.ds(w * depth, depth)
+            source = weight.at[at] if transposed else weight.at[:, at]
+            target = store.at[at, deep] if transposed else store.at[deep, at]
+            copies.append(pltpu.make_async_copy(source, target, sem.at[w, i]))
+    for n in stream(copies, loads):
+        if n % mats < mats - 1:
             continue
-        span = slice(i * tile, (i + 1) * tile)
-        for p in range(n_pieces // 2):
-            mine = total[2 * p * half : (2 * p + 1) * half]
-            other = total[(2 * p + 1) * half : (2 * p + 2) * half]
-            ordered = (jnp.where(is_first, mine, other), jnp.where(is_first, other, mine))
-            for d in range(2 * half // rows):
-                ref = outs[p * (2 * half // rows) + d]
-                which, at = divmod(d * rows, half)
-                ref[:, span] = ordered[which][at : at + rows].astype(ref.dtype)
+        at = pl.ds(n // mats * tile, tile)
+        total = product(panel[...], store.at[at] if transposed else store.at[:, at], transposed)
+        mine, other = total[:half], total[half:]
+        ordered = (jnp.where(is_first, mine, other), jnp.where(is_first, other, mine))
+        for d in range(chunks):
+            which, start = divmod(d * rows, half)
+            outs[d][:, at] = ordered[which][start : start + rows].astype(outs[d].dtype)
 
 
 def back(core, pieces, weights, chunks, transposed, *earlier):
     n_pieces, mats = len(pieces), len(weights)
     half, depth = pieces[0].shape[1:]
     width = weights[0].shape[0] if transposed else weights[0].shape[1]
-    tile = tile_of(width, 512)
+    tile = tile_of(width, BACK_TILE)
     rows = n_pieces * half // chunks
     shapes = tuple(
         jax.ShapeDtypeStruct((rows, width), jnp.bfloat16 if d else jnp.float32)
@@ -293,12 +297,14 @@
     return pl.pallas_call(
         functools.partial(back_kernel, transposed, n_pieces, mats, chunks, tile),
         out_shape=shapes,
-        in_specs=[whole(SM)]
-        + [whole(VM)] * n_pieces
-        + [whole(pl.ANY)] * (mats + len(earlier)),
+        in_specs=[whole(SM)] + [whole(pl.ANY)] * (n_pieces + mats + len(earlier)),
         out_specs=(whole(VM),) * chunks,
-        scratch_shapes=[VM(w.shape, jnp.bfloat16) for w in weights]
-        + [pltpu.SemaphoreType.DMA((mats, width // tile))],
+        scratch_shapes=[
+            VM((width, mats * depth) if transposed else (mats * depth, width), jnp.bfloat16),
+            VM((n_pieces * half, mats * depth), jnp.bfloat16),
+            pltpu.SemaphoreType.DMA((mats, width // tile)),
+            pltpu.SemaphoreType.DMA((mats * n_pieces,)),
+        ],
         compiler_params=params(),
         cost_estimate=cost(
             2 * n_pieces * half * depth * width * mats, 2 * depth * width * mats
@@ -340,19 +346,24 @@
     )(x, *earlier)
 
 
-def sum_kernel(n_sum, *refs):
-    refs[-1][...] = add_up([ref[...] for ref in refs[:n_sum]]).astype(refs[-1].dtype)
-
-
-def sum_chunks(kept, *earlier):
-    return pl.pallas_call(
-        functools.partial(sum_kernel, len(kept)),
-        out_shape=jax.ShapeDtypeStruct(kept[0].shape, jnp.bfloat16),
-        in_specs=[whole(VM)] * len(kept) + [whole(pl.ANY)] * len(earlier),
-        out_specs=whole(VM),
-        compiler_params=params(),
-        cost_estimate=cost(0, kept[0].size * 10),
-    )(*kept, *earlier)
+def sum_kernel(counts, *refs):
+    at = 0
+    for out, count in zip(refs[len(refs) - len(counts) :], counts):
+        out[...] = add_up([ref[...] for ref in refs[at : at + count]]).astype(out.dtype)
+        at += count
+
+
+def sum_chunks(lists, *earlier):
+    counts = [len(parts) for parts in lists]
+    parts = [part for parts in lists for part in parts]
+    return pl.pallas_call(
+        functools.partial(sum_kernel, counts),
+        out_shape=tuple(jax.ShapeDtypeStruct(p[0].shape, jnp.bfloat16) for p in lists),
+        in_specs=[whole(VM)] * len(parts) + [whole(pl.ANY)] * len(earlier),
+        out_specs=(whole(VM),) * len(lists),
+        compiler_params=params(),
+        cost_estimate=cost(0, parts[0].size * 10),
+    )(*parts, *earlier)
 
 
 def mark_kernel(*refs):
@@ -370,19 +381,21 @@
     )(*earlier)
 
 
+def across(rows, width):
+    return pl.BlockSpec((rows, tile_of(width, POINT_WIDE)), lambda i: (0, i))
+
+
 def act_kernel(n_sum, *refs):
     gates, ups = refs[:n_sum], refs[n_sum : 2 * n_sum]
     hidden_ref, by_gate_ref, by_up_ref = refs[-3:]
-    wide = tile_of(gates[0].shape[1], 512)
-    for i in range(gates[0].shape[1] // wide):
-        span = slice(i * wide, (i + 1) * wide)
-        gate = add_up([ref[:, span] for ref in gates])
-        up = add_up([ref[:, span] for ref in ups])
-        sigma = jax.nn.sigmoid(gate)
-        active = gate * sigma
-        hidden_ref[0, :, span] = (active * up).astype(jnp.bfloat16)
-        by_gate_ref[:, span] = up * sigma * (1.0 + gate * (1.0 - sigma))
-        by_up_ref[:, span] = active
+    span = slice(None)
+    gate = add_up([ref[:, span] for ref in gates])
+    up = add_up([ref[:, span] for ref in ups])
+    sigma = jax.nn.sigmoid(gate)
+    active = gate * sigma
+    hidden_ref[0, :, span] = (active * up).astype(jnp.bfloat16)
+    by_gate_ref[:, span] = up * sigma * (1.0 + gate * (1.0 - sigma))
+    by_up_ref[:, span] = active
 
 
 def act(gates, ups, *earlier):
@@ -391,8 +404,13 @@
     return pl.pallas_call(
         functools.partial(act_kernel, len(gates)),
         out_shape=(jax.ShapeDtypeStruct((1, rows, width), jnp.bfloat16), wide, wide),
-        in_specs=[whole(VM)] * (2 * len(gates)) + [whole(pl.ANY)] * len(earlier),
-        out_specs=(whole(VM),) * 3,
+        grid=(width // tile_of(width, POINT_WIDE),),
+        in_specs=[across(rows, width)] * (2 * len(gates)) + [whole(pl.ANY)] * len(earlier),
+        out_specs=(
+            pl.BlockSpec((1, rows, tile_of(width, POINT_WIDE)), lambda i: (0, 0, i)),
+            across(rows, width),
+            across(rows, width),
+        ),
         compiler_params=params(),
         cost_estimate=cost(0, rows * width * 30),
     )(*gates, *ups, *earlier)
@@ -401,61 +419,90 @@
 def grads_kernel(n_sum, *refs):
     sums, (by_gate_ref, by_up_ref) = refs[:n_sum], refs[n_sum : n_sum + 2]
     both_ref = refs[-1]
-    wide = tile_of(sums[0].shape[1], 512)
-    for i in range(sums[0].shape[1] // wide):
-        span = slice(i * wide, (i + 1) * wide)
-        grad_hidden = add_up([ref[:, span] for ref in sums])
-        both_ref[0, :, span] = (grad_hidden * by_gate_ref[:, span]).astype(jnp.bfloat16)
-        both_ref[1, :, span] = (grad_hidden * by_up_ref[:, span]).astype(jnp.bfloat16)
+    span = slice(None)
+    grad_hidden = add_up([ref[:, span] for ref in sums])
+    both_ref[0, :, span] = (grad_hidden * by_gate_ref[:, span]).astype(jnp.bfloat16)
+    both_ref[1, :, span] = (grad_hidden * by_up_ref[:, span]).astype(jnp.bfloat16)
 
 
 def act_grads(sums, by_gate, by_up, *earlier):
     return pl.pallas_call(
         functools.partial(grads_kernel, len(sums)),
         out_shape=jax.ShapeDtypeStruct((2, *by_gate.shape), jnp.bfloat16),
-        in_specs=[whole(VM)] * (len(sums) + 2) + [whole(pl.ANY)] * len(earlier),
-        out_specs=whole(VM),
+        grid=(by_gate.shape[1] // tile_of(by_gate.shape[1], POINT_WIDE),),
+        in_specs=[across(*by_gate.shape)] * (len(sums) + 2) + [whole(pl.ANY)] * len(earlier),
+        out_specs=pl.BlockSpec(
+            (2, by_gate.shape[0], tile_of(by_gate.shape[1], POINT_WIDE)), lambda i: (0, 0, i)
+        ),
         compiler_params=params(),
         cost_estimate=cost(0, by_gate.size * 20),
     )(*sums, by_gate, by_up, *earlier)
 
 
-def block_grad_kernel(parts, mats, n_left, n_right, left_whole, scale, cols, wide, *refs):
-    core_ref, tables, counts = refs[0], refs[1 : 1 + mats], refs[1 + mats : 1 + 2 * mats]
-    rest = refs[1 + 2 * mats :]
-    lefts, rights = rest[:n_left], rest[n_left : n_left + n_right]
-    outs, stores = rest[-2 - 2 * mats : -2 - mats], rest[-2 - mats : -2]
-    turned, sem = rest[-2:]
+def own_order(core, ref):
+    half = ref.shape[0] // 2
+    return [ref.at[rows_at(core * half, half)], ref.at[rows_at((1 - core) * half, half)]]
+
+
+def block_grad_kernel(mats, n_left, n_right, scale, cols, wide, core_ref, *refs):
+    tables, counts = refs[:mats], refs[mats : 2 * mats]
+    lefts = refs[2 * mats : 2 * mats + n_left]
+    rights = refs[2 * mats + n_left : 2 * mats + n_left + n_right]
+    outs, stores = refs[-6 - 2 * mats : -6 - mats], refs[-6 - mats : -6]
+    left, right, turned, in_sem, left_sem, out_sem = refs[-6:]
     core = core_ref[0]
     slots = outs[0].shape[0]
-    length, width = turned.shape[0], rights[0].shape[-1]
+    length, width = left.shape[1], right.shape[2]
     tall = tile_of(length, 512)
 
+    def rows_of(refs, m):
+        rows = []
+        for ref in refs:
+            rows += own_order(core, ref) if len(ref.shape) == 2 else [ref.at[m]]
+        return rows
+
+    def loads(sources, target, sem):
+        rows = sources[0].shape[0]
+        copies = [
+            pltpu.make_async_copy(source, target.at[pl.ds(k * rows, rows)], sem.at[k])
+            for k, source in enumerate(sources)
+        ]
+        return copies
+
+    left_loads = loads(rows_of(lefts, 0), left, left_sem)
+    right_loads = [loads(rows_of(rights, m), right.at[m], in_sem.at[m]) for m in range(mats)]
+    for load in left_loads:
+        load.start()
+
+    def clear(slot, carry, m):
+        stores[m][slot] = jnp.zeros((BLK, BLK), jnp.bfloat16)
+        return carry
+
+    for m in range(mats):
+        lax.fori_loop(counts[m][0], slots, functools.partial(clear, m=m), 0)
+    for load in left_loads:
+        load.wait()
+    for load in right_loads[0]:
+        load.start()
     for a in range(length // tall):
         span = slice(a * tall, (a + 1) * tall)
-        if left_whole:
-            pieces = [q for ref in lefts for q in natural_to_own(core, parts, ref, span)]
-        else:
-            pieces = [ref[0, :, span] for ref in lefts]
-        turned[span, :] = jnp.concatenate(pieces, axis=0).T
+        turned[span, :] = left[:, span].T
 
     copies = []
     for m in range(mats):
-
-        def clear(slot, carry, m=m):
-            stores[m][slot] = jnp.zeros((BLK, BLK), jnp.bfloat16)
-            return carry
+        for load in right_loads[m]:
+            load.wait()
+        if m + 1 < mats:
+            for load in right_loads[m + 1]:
+                load.start()
 
         def column(at, carry, m=m):
             span = pl.ds(pl.multiple_of(at * wide, wide), wide)
-            if left_whole:
-                panel = [ref[m, :, span] for ref in rights]
-            else:
-                panel = [q for ref in rights for q in natural_to_own(core, parts, ref, span)]
-            panel = jnp.concatenate(panel, axis=0)
             for a in range(length // tall):
                 full = jnp.dot(
-                    turned[a * tall : (a + 1) * tall, :], panel, preferred_element_type=jnp.float32
+                    turned[a * tall : (a + 1) * tall, :],
+                    right[m, :, span],
+                    preferred_element_type=jnp.float32,
                 )
                 full = (full * scale).astype(jnp.bfloat16)
                 for di in range(tall // BLK):
@@ -467,40 +514,44 @@
                         ]
             return carry
 
-        lax.fori_loop(counts[m][0], slots, clear, 0)
         lax.fori_loop(0, width // wide, column, 0)
         copies.append(
-            pltpu.make_async_copy(stores[m].at[pl.ds(0, slots)], outs[m], sem.at[m])
+            pltpu.make_async_copy(stores[m].at[pl.ds(0, slots)], outs[m], out_sem.at[m])
         )
         copies[m].start()
     for copy in copies:
         copy.wait()
 
 
-def block_grads(core, tables, counts, lefts, rights, left_whole, parts, slots, scale, *earlier):
+def block_grads(core, tables, counts, lefts, rights, slots, scale, *earlier):
     mats = len(tables)
-    tokens = sum(a.shape[0] for a in (lefts if left_whole else rights))
+    tokens = sum(a.shape[-2] for a in lefts)
     length, width = lefts[0].shape[-1], rights[0].shape[-1]
-    wide = tile_of(width, 512)
+    wide = tile_of(width, GRAD_WIDE)
+    n_rows = [sum(2 if a.ndim == 2 else 1 for a in side) for side in (lefts, rights)]
     return pl.pallas_call(
         functools.partial(
             block_grad_kernel,
-            parts,
             mats,
             len(lefts),
             len(rights),
-            left_whole,
             scale,
             width // BLK,
             wide,
         ),
         out_shape=(jax.ShapeDtypeStruct((slots, BLK, BLK), jnp.bfloat16),) * mats,
         in_specs=[whole(SM)] * (1 + 2 * mats)
-        + [whole(VM)] * (len(lefts) + len(rights))
-        + [whole(pl.ANY)] * len(earlier),
+        + [whole(pl.ANY)] * (len(lefts) + len(rights) + len(earlier)),
         out_specs=(whole(pl.ANY),) * mats,
         scratch_shapes=[VM((slots + 1, BLK, BLK), jnp.bfloat16)] * mats
-        + [VM((length, tokens), jnp.bfloat16), pltpu.SemaphoreType.DMA((mats,))],
+        + [
+            VM((tokens, length), jnp.bfloat16),
+            VM((mats, tokens, width), jnp.bfloat16),
+            VM((length, tokens), jnp.bfloat16),
+            pltpu.SemaphoreType.DMA((mats, n_rows[1])),
+            pltpu.SemaphoreType.DMA((n_rows[0],)),
+            pltpu.SemaphoreType.DMA((mats,)),
+        ],
         compiler_params=params(),
         cost_estimate=cost(2 * tokens * length * width * mats, slots * BLK * BLK * 2 * mats),
     )(core, *tables, *counts, *lefts, *rights, *earlier)
@@ -559,9 +610,8 @@
             for p in range(parts)
         ]
 
-    def scatter(cut, *earlier):
-        kept = [cut[0]] + [shift(cut[d], "col", -d) for d in z_order(n_col)]
-        return sum_chunks(kept, *earlier)
+    def scatter(cut):
+        return [cut[0]] + [shift(cut[d], "col", -d) for d in z_order(n_col)]
 
     def far_pieces(pairs):
         pieces = []
@@ -577,7 +627,7 @@
     x_parts = gather(tokens)
     x_whole = jnp.concatenate(x_parts, axis=0)
     (w_gate,) = densify((gate_table,), (gate_blocks[0, 0],), feats, units)
-    gate_mine, gate_other = project(core, x_parts, [w_gate], False)
+    gate_mine, gate_other = project(core, x_whole, w_gate, False)
     gate_swapped = swap_cores(gate_other)
     gate_sent = pair_sum(gate_mine, gate_swapped)
 
@@ -598,20 +648,19 @@
         core, c_whole, down_table, down_blocks[0, 0], units, feats, True, up_sent
     )
     token = mark(back_other, *up_got, *c_groups[1:])
+    back_swapped = swap_cores(back_other)
+    back_sent = pair_sum(back_mine, back_swapped, token)
+
+    back_got = other_chips(back_sent)
     hidden, by_gate, by_up = act(
-        [gate_mine, gate_swapped] + gate_got, [up_mine, up_swapped] + up_got, token
-    )
-    back_swapped = swap_cores(back_other)
-    back_sent = pair_sum(back_mine, back_swapped, hidden)
-
-    back_got = other_chips(back_sent)
+        [gate_mine, gate_swapped] + gate_got, [up_mine, up_swapped] + up_got, back_sent
+    )
     hidden_far = other_groups(hidden)
     hidden_pieces = [hidden, swap_cores(hidden)]
-    out_cut = back(core, hidden_pieces, [w_down], n_col, False, back_sent)
-    hidden_far = [hold(far, out_cut[0]) for far in hidden_far]
-    hidden_pieces += far_pieces([hidden_far])
-    token = mark(out_cut[0], *back_got, *hidden_pieces[2:])
+    out_cut = back(core, hidden_pieces, [w_down], n_col, False)
+    token = mark(out_cut[0], *back_got)
     grads = act_grads([back_mine, back_swapped] + back_got, by_gate, by_up, token)
+    hidden_pieces += far_pieces([[hold(far, grads) for far in hidden_far]])
 
     grads_far = other_groups(grads)
     grad_pieces = [grads, swap_cores(grads)]
@@ -621,27 +670,23 @@
         (down_count,),
         hidden_pieces,
         c_groups,
-        False,
-        parts,
         slots,
         scale,
         grad_pieces[1],
     )
     in_cut = back(core, grad_pieces, [w_gate, w_up], n_col, True, down_grad)
-    output = scatter(out_cut, in_cut[0])
-    grads_far = [hold(far, output) for far in grads_far]
+    out_kept = scatter(out_cut)
+    grads_far = [hold(far, in_cut[0], *out_kept[1:]) for far in grads_far]
     gate_grad, up_grad = block_grads(
         core,
         (gate_table, up_table),
         (gate_count, up_count),
         x_groups,
         grad_pieces + far_pieces([grads_far]),
-        True,
-        parts,
         slots,
         scale,
     )
-    input_grad = scatter(in_cut, gate_grad)
+    output, input_grad = sum_chunks([out_kept, scatter(in_cut)], gate_grad)
     shape = gate_blocks.shape
     return (
         output,

time: 229 us -> 224 us (0.978)
  Pallas kernels: 144 us -> 135 us
  waiting for transfers between devices: 26.1 us -> 28.9 us
    pallas_call x5 -> x4, Pallas kernels: 61.2 us -> 56.9 us  [the longest x2 45.4 us: block_grads(): pl.pallas_call(functools.partial(block_grad_kernel, mats, len(lefts), len...]
    pallas_call x2, Pallas kernels: 24.9 us -> 22.5 us  [back(): pl.pallas_call(functools.partial(back_kernel, transposed, n_pieces, mats,...]
    unnamed x64 -> x66, local copies, waits for them, and re-layouts: 16.8 us -> 16.1 us
  transfers between devices with their start and end apart: 26 -> 26, of which waited for: 7 -> 8; matrix products, arithmetic and copies ran while one was open for 3% -> 3% of each run, Pallas kernels for 56% -> 52%
where the time goes in v3:
time: 224 us; the launch traced here: 223 us
  Pallas kernels  135 us (60%)
  starting transfers between devices  35.9 us (16%)
  waiting for transfers between devices  28.9 us (13%)
  local copies, waits for them, and re-layouts  16.1 us (7%)
  other arithmetic  5.53 us (2%)
    pallas_call x2, Pallas kernels, block_grads(): pl.pallas_call(functools.partial(block_grad_kernel, mats, len(lefts), len...  45.4 us
    ppermute x19, starting transfers between devices, shift(): return lax.ppermute(x, axis, [(i, (i + by) % n) for i in range(n)])  35.4 us
    ppermute x19, waiting for transfers between devices, shift(): return lax.ppermute(x, axis, [(i, (i + by) % n) for i in range(n)])  28.2 us
    pallas_call x2, Pallas kernels, project_blocks(): pl.pallas_call(functools.partial(project_blocks_kernel, transposed, rows,...  25.6 us
    pallas_call x2, Pallas kernels, back(): pl.pallas_call(functools.partial(back_kernel, transposed, n_pieces, mats,...  22.5 us
    unnamed x66, local copies, waits for them, and re-layouts  16.1 us
    pallas_call x1, Pallas kernels, densify(): pl.pallas_call(functools.partial(densify_kernel, mats, rows, cols, panels...  10.8 us
    pallas_call x1, Pallas kernels, project(): pl.pallas_call(functools.partial(project_kernel, transposed, tile), out_s...  8.87 us
  transfers between devices with their start and end apart: 26, of which 8 were waited for; matrix products, arithmetic and copies ran while one was open for 3% of the time, Pallas kernels for 52%

profile of v3, /device:TPU:0, one launch (start us, length us, event | category | flops | bytes accessed | tf_op | source)
XLA Modules:
  0.0 222.7 jit_solution(1317063161431820610)
XLA Ops:
  0.6 4.1 %collective-permute-start.1 = (bf16[64,2048]{1,0:T(8,128)(2,1)}, bf16[64,2048]{1,0:T(8,128)(2,1)S(1)}, u32[]{:S(2)}, u32[]{:S(2)}) collective-permute-start(bf16[64,2048]{1,0:T(8,128)(2,1)} %param.8), channel_id=1, source_target_pairs={{0,2},{1,3},{2,0},{3,1},{4,6},{5,7},{6,4},{7,5},{8,10},{9,11},{10,... | collective-permute-start | bytes 786440 | tf_op jit(solution)/shard_map/ppermute | solution.py:562
  4.7 1.6 collective-permute-start
  6.3 2.2 %collective-permute-start.2 = (bf16[64,2048]{1,0:T(8,128)(2,1)}, bf16[64,2048]{1,0:T(8,128)(2,1)S(1)}, u32[]{:S(2)}, u32[]{:S(2)}) collective-permute-start(bf16[64,2048]{1,0:T(8,128)(2,1)} %param.8), channel_id=1, source_target_pairs={{0,3},{1,0},{2,1},{3,2},{4,7},{5,4},{6,5},{7,6},{8,11},{9,8},{10,9... | collective-permute-start | bytes 786440 | tf_op jit(solution)/shard_map/ppermute | solution.py:562
  8.6 1.0 constant_dynamic-update-slice_fusion.3
  9.6 0.8 fusion.2
  10.3 0.8 fusion
  12.0 10.8 %shard_map.119.weight.refs_2_ = bf16[2048,3584]{1,0:T(8,128)(2,1)} custom-call(s32[448]{0:T(512)} %broadcast_subtract_fusion.2.refs_0_, bf16[336,128,128]{2,1,0:T(8,128)(2,1)} %bitcast.14), custom_call_target="tpu_custom_call" | custom-call | bytes 25 | tf_op jit(solution)/shard_map/pallas_call | solution.py:104
  24.1 1.0 copy-done.1
  25.1 8.9 %shard_map.120 = (f32[128,3584]{1,0:T(8,128)}, bf16[128,3584]{1,0:T(8,128)(2,1)}) custom-call(s32[1]{0:T(128)} %bitcast.core_ref, bf16[256,2048]{1,0:T(8,128)(2,1)} %copy-done.1, bf16[2048,3584]{1,0:T(8,128)(2,1)} %shard_map.119.weight.refs_2_), custom_call_target="tpu_custom_call" | custom-call | flops 3758 | bytes 14 | tf_op jit(solution)/shard_map/pallas_call | solution.py:165
  34.1 5.0 %collective-permute-start.6 = (bf16[64,2048]{1,0:T(8,128)(2,1)S(1)}, bf16[64,2048]{1,0:T(8,128)(2,1)S(1)}, u32[]{:S(2)}, u32[]{:S(2)}) collective-permute-start(bf16[64,2048]{1,0:T(8,128)(2,1)S(1)} %copy-done.20), channel_id=1, source_target_pairs={{0,1},{1,2},{2,3},{3,0},{4,5},{5,6},{6,7},{7,4},{8,9},{9,10},{10,1... | collective-permute-start | bytes 786440 | tf_op jit(solution)/shard_map/ppermute | solution.py:562
  39.6 1.8 collective-permute-start.7
  41.5 1.5 collective-permute-start.9
  43.0 0.9 copy-done.6
  43.9 2.8 %shard_map.121.refs_0_ = bf16[128,3584]{1,0:T(8,128)(2,1)} custom-call(f32[128,3584]{1,0:T(8,128)} %get-tuple-element.29.mine_ref.refs_0_, bf16[128,3584]{1,0:T(8,128)(2,1)} %copy-done.6), custom_call_target="tpu_custom_call" | custom-call | bytes 3 | tf_op jit(solution)/shard_map/pallas_call | solution.py:323
  46.7 1.5 collective-permute-start.4
  48.2 12.7 %shard_map.122 = (f32[128,3584]{1,0:T(8,128)}, bf16[128,3584]{1,0:T(8,128)(2,1)}, bf16[2048,3584]{1,0:T(8,128)(2,1)}) custom-call(s32[1]{0:T(128)} %bitcast.core_ref, s32[448]{0:T(512)} %broadcast_subtract_fusion.1.table.refs_1_, bf16[256,2048]{1,0:T(8,128)(2,1)} %copy-done.1, bf16[336,128,128]{2,1,0:T(8,128)(2,1)} %bitcast.15, ...), custom_call_target="tpu_custom_call" | custom-call | flops 3758 | bytes 29 | tf_op jit(solution)/shard_map/pallas_call | solution.py:230
  61.1 3.1 %collective-permute-start.8 = (bf16[64,2048]{1,0:T(8,128)(2,1)S(1)}, bf16[64,2048]{1,0:T(8,128)(2,1)S(1)}, u32[]{:S(2)}, u32[]{:S(2)}) collective-permute-start(bf16[64,2048]{1,0:T(8,128)(2,1)S(1)} %copy-done.20), channel_id=1, source_target_pairs={{0,3},{1,0},{2,1},{3,2},{4,7},{5,4},{6,5},{7,6},{8,11},{9,8},{10,9... | collective-permute-start | bytes 786440 | tf_op jit(solution)/shard_map/ppermute | solution.py:562
  64.3 6.2 %collective-permute-done.8 = bf16[64,2048]{1,0:T(8,128)(2,1)S(1)} collective-permute-done((bf16[64,2048]{1,0:T(8,128)(2,1)S(1)}, bf16[64,2048]{1,0:T(8,128)(2,1)S(1)}, u32[]{:S(2)}, u32[]{:S(2)}) %collective-permute-start.8) | collective-permute-done | bytes 262176 | tf_op jit(solution)/shard_map/ppermute | solution.py:562
  71.7 1.0 copy-done.4
  72.6 0.9 copy-done.8
  74.2 0.9 copy-done.9
  75.1 2.8 %shard_map.124.refs_0_ = bf16[128,3584]{1,0:T(8,128)(2,1)} custom-call(f32[128,3584]{1,0:T(8,128)} %get-tuple-element.31.mine_ref.refs_3_, bf16[128,3584]{1,0:T(8,128)(2,1)} %copy-done.9, f32[8,128]{1,0:T(8,128)} %shard_map.123.refs_0_), custom_call_target="tpu_custom_call" | custom-call | bytes 3 | tf_op jit(solution)/shard_map/pallas_call | solution.py:323
  78.4 12.8 %shard_map.125 = (f32[128,3584]{1,0:T(8,128)}, bf16[128,3584]{1,0:T(8,128)(2,1)}, bf16[3584,2048]{1,0:T(8,128)(2,1)}) custom-call(s32[1]{0:T(128)} %bitcast.core_ref, s32[448]{0:T(512)} %broadcast_subtract_fusion.table.refs_0_, bf16[256,2048]{1,0:T(8,128)(2,1)} %copy-done.2, bf16[336,128,128]{2,1,0:T(8,128)(2,1)} %bitcast.16, ...), custom_call_target="tpu_custom_call" | custom-call | flops 3758 | bytes 29 | tf_op jit(solution)/shard_map/pallas_call | solution.py:230
  91.3 4.0 %collective-permute-done.12.refs_2_.refs_7_ = bf16[256,2048]{1,0:T(8,128)(2,1)S(1)} collective-permute-done((bf16[256,2048]{1,0:T(8,128)(2,1)S(1)}, bf16[256,2048]{1,0:T(8,128)(2,1)S(1)}, u32[]{:S(2)}, u32[]{:S(2)}) %collective-permute-start.12) | collective-permute-done | bytes 1048608 | tf_op jit(solution)/shard_map/ppermute | solution.py:562
  95.3 4.6 %collective-permute-done.10.refs_1_.refs_5_ = bf16[128,3584]{1,0:T(8,128)(2,1)S(1)} collective-permute-done((bf16[128,3584]{1,0:T(8,128)(2,1)}, bf16[128,3584]{1,0:T(8,128)(2,1)S(1)}, u32[]{:S(2)}, u32[]{:S(2)}) %collective-permute-start.10) | collective-permute-done | bytes 917536 | tf_op jit(solution)/shard_map/ppermute | solution.py:562
  99.9 0.9 copy-done.12
  101.4 0.9 copy-done.10
  102.3 2.9 %shard_map.127.refs_6_ = bf16[128,3584]{1,0:T(8,128)(2,1)} custom-call(f32[128,3584]{1,0:T(8,128)} %get-tuple-element.34.mine_ref.refs_0_, bf16[128,3584]{1,0:T(8,128)(2,1)} %copy-done.10, f32[8,128]{1,0:T(8,128)} %shard_map.126.refs_0_), custom_call_target="tpu_custom_call" | custom-call | bytes 3 | tf_op jit(solution)/shard_map/pallas_call | solution.py:323
  105.2 5.1 %shard_map.128 = (bf16[1,128,3584]{2,1,0:T(8,128)(2,1)}, f32[128,3584]{1,0:T(8,128)}, f32[128,3584]{1,0:T(8,128)}) custom-call(f32[128,3584]{1,0:T(8,128)} %get-tuple-element.29.mine_ref.refs_0_, bf16[128,3584]{1,0:T(8,128)(2,1)} %copy-done.6, bf16[128,3584]{1,0:T(8,128)(2,1)} %copy-done.8, f32[128,3584]{1,0:T(8,128)} %get-tuple-element.31.mine_ref.refs_3_, ...), custom_call_target="tpu_custom_call" | custom-call | bytes 13 | tf_op jit(solution)/shard_map/pallas_call | solution.py:404
  111.0 1.4 collective-permute-start.19
  113.1 0.9 copy-done.14
  114.0 8.4 %shard_map.129 = (f32[64,2048]{1,0:T(8,128)}, bf16[64,2048]{1,0:T(8,128)(2,1)}, bf16[64,2048]{1,0:T(8,128)(2,1)}, bf16[64,2048]{1,0:T(8,128)(2,1)}) custom-call(s32[1]{0:T(128)} %bitcast.core_ref, bf16[1,128,3584]{2,1,0:T(8,128)(2,1)} %get-tuple-element.36.refs_0_.refs_2_, bf16[1,128,3584]{2,1,0:T(8,128)(2,1)} %copy-done.14, ...), custom_call_target="tpu_custom_call" | custom-call | flops 3758 | bytes 14 | tf_op jit(solution)/shard_map/pallas_call | solution.py:297
  122.4 10.8 %collective-permute-done.17.refs_1_.refs_2_ = bf16[128,3584]{1,0:T(8,128)(2,1)S(1)} collective-permute-done((bf16[128,3584]{1,0:T(8,128)(2,1)S(1)}, bf16[128,3584]{1,0:T(8,128)(2,1)S(1)}, u32[]{:S(2)}, u32[]{:S(2)}) %collective-permute-start.17) | collective-permute-done | bytes 917536 | tf_op jit(solution)/shard_map/ppermute | solution.py:562
  133.2 0.9 copy-done.13
  134.7 4.3 %shard_map.131.refs_1_.refs_0_.refs_6_ = bf16[2,128,3584]{2,1,0:T(8,128)(2,1)} custom-call(f32[128,3584]{1,0:T(8,128)} %get-tuple-element.34.mine_ref.refs_0_, bf16[128,3584]{1,0:T(8,128)(2,1)} %copy-done.10, bf16[128,3584]{1,0:T(8,128)(2,1)} %copy-done.13, f32[128,3584]{1,0:T(8,128)} %get-tuple-element.42.refs_3_, f32[128,3584]{1,0:T(8,128)} %get-tuple-element.43.refs_4_, ...), custom_call_target="tpu_custom_call" | custom-call | bytes 9 | tf_op jit(solution)/shard_map/pallas_call | solution.py:429
  139.1 1.5 collective-permute-start.24
  140.6 0.9 copy-done.7
  141.7 4.3 %collective-permute-start.14 = (bf16[64,2048]{1,0:T(8,128)(2,1)S(1)}, bf16[64,2048]{1,0:T(8,128)(2,1)S(1)}, u32[]{:S(2)}, u32[]{:S(2)}) collective-permute-start(bf16[64,2048]{1,0:T(8,128)(2,1)S(1)} %copy-done.26), channel_id=1, source_target_pairs={{0,3},{1,0},{2,1},{3,2},{4,7},{5,4},{6,5},{7,6},{8,11},{9,8},{10,9... | collective-permute-start | bytes 786440 | tf_op jit(solution)/shard_map/ppermute | solution.py:562
  147.3 1.2 copy-done
  148.5 17.6 %shard_map.133.refs_4_ = bf16[336,128,128]{2,1,0:T(8,128)(2,1)} custom-call(s32[1]{0:T(128)} %bitcast.core_ref, s32[448]{0:T(512)} %broadcast_subtract_fusion.table.refs_0_, s32[1]{0:T(128)} %bitcast.7.refs_1_, bf16[1,128,3584]{2,1,0:T(8,128)(2,1)} %get-tuple-element.36.refs_0_.refs_2_, bf16[1,128,3584]{2,1,0:T(8,128)(2,1)} %copy-done.14, ...), custom_call_target="tpu_custom_call" | custom-call | flops 7516 | bytes 11 | tf_op jit(solution)/shard_map/pallas_call | solution.py:532
  166.1 14.1 %shard_map.134 = (f32[64,2048]{1,0:T(8,128)}, bf16[64,2048]{1,0:T(8,128)(2,1)}, bf16[64,2048]{1,0:T(8,128)(2,1)}, bf16[64,2048]{1,0:T(8,128)(2,1)}) custom-call(s32[1]{0:T(128)} %bitcast.core_ref, bf16[2,128,3584]{2,1,0:T(8,128)(2,1)} %shard_map.131.refs_1_.refs_0_.refs_6_, bf16[2,128,3584]{2,1,0:T(8,128)(2,1)} %copy-done, ...), custom_call_target="tpu_custom_call" | custom-call | flops 7516 | bytes 29 | tf_op jit(solution)/shard_map/pallas_call | solution.py:297
  180.2 1.5 collective-permute-done.24.refs_0_
  181.7 1.2 copy-done.3
  182.9 0.9 copy-done.29
  183.9 4.3 %collective-permute-start.21 = (bf16[64,2048]{1,0:T(8,128)(2,1)S(1)}, bf16[64,2048]{1,0:T(8,128)(2,1)S(1)}, u32[]{:S(2)}, u32[]{:S(2)}) collective-permute-start(bf16[64,2048]{1,0:T(8,128)(2,1)S(1)} %copy-done.29), channel_id=1, source_target_pairs={{0,3},{1,0},{2,1},{3,2},{4,7},{5,4},{6,5},{7,6},{8,11},{9,8},{10,9... | collective-permute-start | bytes 786440 | tf_op jit(solution)/shard_map/ppermute | solution.py:562
  190.1 1.2 copy-done.15
  191.3 27.8 %shard_map.136 = (bf16[336,128,128]{2,1,0:T(8,128)(2,1)}, bf16[336,128,128]{2,1,0:T(8,128)(2,1)}) custom-call(s32[1]{0:T(128)} %bitcast.core_ref, s32[448]{0:T(512)} %broadcast_subtract_fusion.2.refs_0_, s32[448]{0:T(512)} %broadcast_subtract_fusion.1.table.refs_1_, s32[1]{0:T(128)} %bitcast.8.refs_2_, s32[1]{0:T(128)} %bitcast.9.refs_3_, ...), custom_call_target="tpu_custom_call" | custom-call | flops 15032 | bytes 22 | tf_op jit(solution)/shard_map/pallas_call | solution.py:532
  220.1 2.6 %shard_map.137 = (bf16[64,2048]{1,0:T(8,128)(2,1)}, bf16[64,2048]{1,0:T(8,128)(2,1)}) custom-call(f32[64,2048]{1,0:T(8,128)} %get-tuple-element.38.refs_0_, bf16[64,2048]{1,0:T(8,128)(2,1)} %copy-done.16, bf16[64,2048]{1,0:T(8,128)(2,1)} %copy-done.17, bf16[64,2048]{1,0:T(8,128)(2,1)} %copy-done.18, f32[64,2048]{1,0:T(8,128)} %get-tuple-element.45.refs_1_.refs_4_, ...), custom_call_target="tpu_custom_call" | custom-call | bytes 1 | tf_op jit(solution)/shard_map/pallas_call | solution.py:359
  (101 shorter events, 12.2 us)
Async XLA Ops:
  0.6 22.7 %collective-permute-start.1 = (bf16[64,2048]{1,0:T(8,128)(2,1)}, bf16[64,2048]{1,0:T(8,128)(2,1)S(1)}, u32[]{:S(2)}, u32[]{:S(2)}) collective-permute-start(bf16[64,2048]{1,0:T(8,128)(2,1)} %param.8), channel_id=1, source_target_pairs={{0,2},{1,3},{2,0},{3,1},{4,6},{5,7},{6,4},{7,5},{8,10},{9,11},{10,... | collective-permute-start | bytes 786440 | tf_op jit(solution)/shard_map/ppermute | solution.py:562
  4.7 18.1 %collective-permute-start = (bf16[64,2048]{1,0:T(8,128)(2,1)}, bf16[64,2048]{1,0:T(8,128)(2,1)S(1)}, u32[]{:S(2)}, u32[]{:S(2)}) collective-permute-start(bf16[64,2048]{1,0:T(8,128)(2,1)} %param.8), channel_id=1, source_target_pairs={{0,1},{1,2},{2,3},{3,0},{4,5},{5,6},{6,7},{7,4},{8,9},{9,10},{10,1... | collective-permute-start | bytes 786440 | tf_op jit(solution)/shard_map/ppermute | solution.py:562
  6.3 17.8 %collective-permute-start.2 = (bf16[64,2048]{1,0:T(8,128)(2,1)}, bf16[64,2048]{1,0:T(8,128)(2,1)S(1)}, u32[]{:S(2)}, u32[]{:S(2)}) collective-permute-start(bf16[64,2048]{1,0:T(8,128)(2,1)} %param.8), channel_id=1, source_target_pairs={{0,3},{1,0},{2,1},{3,2},{4,7},{5,4},{6,5},{7,6},{8,11},{9,8},{10,9... | collective-permute-start | bytes 786440 | tf_op jit(solution)/shard_map/ppermute | solution.py:562
  24.1 1.0 copy-start.1
  25.1 9.0 %copy-start.20 = (bf16[64,2048]{1,0:T(8,128)(2,1)S(1)}, bf16[64,2048]{1,0:T(8,128)(2,1)}, u32[]{:S(2)}) copy-start(bf16[64,2048]{1,0:T(8,128)(2,1)} %param.9) | copy-start | bytes 786436
  34.0 9.0 %collective-permute-start.3 = (bf16[128,3584]{1,0:T(8,128)(2,1)}, bf16[128,3584]{1,0:T(8,128)(2,1)S(1)}, u32[]{:S(2)}, u32[]{:S(2)}) collective-permute-start(bf16[128,3584]{1,0:T(8,128)(2,1)} %get-tuple-element.30), channel_id=1, source_target_pairs={{0,4},{4,0},{8,12},{12,8},{1,5},{5,1},{9,13},{13,9},{2,6},{6,2},{1... | collective-permute-start | bytes 2752520 | tf_op jit(solution)/shard_map/ppermute | solution.py:567
  34.1 27.0 %collective-permute-start.6 = (bf16[64,2048]{1,0:T(8,128)(2,1)S(1)}, bf16[64,2048]{1,0:T(8,128)(2,1)S(1)}, u32[]{:S(2)}, u32[]{:S(2)}) collective-permute-start(bf16[64,2048]{1,0:T(8,128)(2,1)S(1)} %copy-done.20), channel_id=1, source_target_pairs={{0,1},{1,2},{2,3},{3,0},{4,5},{5,6},{6,7},{7,4},{8,9},{9,10},{10,1... | collective-permute-start | bytes 786440 | tf_op jit(solution)/shard_map/ppermute | solution.py:562
  39.6 24.6 %collective-permute-start.7 = (bf16[64,2048]{1,0:T(8,128)(2,1)S(1)}, bf16[64,2048]{1,0:T(8,128)(2,1)S(1)}, u32[]{:S(2)}, u32[]{:S(2)}) collective-permute-start(bf16[64,2048]{1,0:T(8,128)(2,1)S(1)} %copy-done.20), channel_id=1, source_target_pairs={{0,2},{1,3},{2,0},{3,1},{4,6},{5,7},{6,4},{7,5},{8,10},{9,11},{10,... | collective-permute-start | bytes 786440 | tf_op jit(solution)/shard_map/ppermute | solution.py:562
  41.5 30.2 %collective-permute-start.9 = (bf16[256,2048]{1,0:T(8,128)(2,1)}, bf16[256,2048]{1,0:T(8,128)(2,1)S(1)}, u32[]{:S(2)}, u32[]{:S(2)}) collective-permute-start(bf16[256,2048]{1,0:T(8,128)(2,1)} %copy-done.1), channel_id=1, source_target_pairs={{0,16},{16,0},{1,17},{17,1},{2,18},{18,2},{3,19},{19,3},{4,20},{20... | collective-permute-start | bytes 3145736 | tf_op jit(solution)/shard_map/ppermute | solution.py:562
  46.7 25.0 %collective-permute-start.4 = (bf16[128,3584]{1,0:T(8,128)(2,1)}, bf16[128,3584]{1,0:T(8,128)(2,1)S(1)}, u32[]{:S(2)}, u32[]{:S(2)}) collective-permute-start(bf16[128,3584]{1,0:T(8,128)(2,1)} %shard_map.121.refs_0_), channel_id=1, source_target_pairs={{0,8},{4,12},{8,0},{12,4},{1,9},{5,13},{9,1},{13,5},{2,10},{6,14},... | collective-permute-start | bytes 2752520 | tf_op jit(solution)/shard_map/ppermute | solution.py:562
  61.0 13.2 %collective-permute-start.5 = (bf16[128,3584]{1,0:T(8,128)(2,1)}, bf16[128,3584]{1,0:T(8,128)(2,1)S(1)}, u32[]{:S(2)}, u32[]{:S(2)}) collective-permute-start(bf16[128,3584]{1,0:T(8,128)(2,1)} %get-tuple-element.32.refs_0_), channel_id=1, source_target_pairs={{0,4},{4,0},{8,12},{12,8},{1,5},{5,1},{9,13},{13,9},{2,6},{6,2},{1... | collective-permute-start | bytes 2752520 | tf_op jit(solution)/shard_map/ppermute | solution.py:567
  61.1 9.4 %collective-permute-start.8 = (bf16[64,2048]{1,0:T(8,128)(2,1)S(1)}, bf16[64,2048]{1,0:T(8,128)(2,1)S(1)}, u32[]{:S(2)}, u32[]{:S(2)}) collective-permute-start(bf16[64,2048]{1,0:T(8,128)(2,1)S(1)} %copy-done.20), channel_id=1, source_target_pairs={{0,3},{1,0},{2,1},{3,2},{4,7},{5,4},{6,5},{7,6},{8,11},{9,8},{10,9... | collective-permute-start | bytes 786440 | tf_op jit(solution)/shard_map/ppermute | solution.py:562
  70.5 1.2 copy-start.2
  70.5 24.8 %collective-permute-start.12 = (bf16[256,2048]{1,0:T(8,128)(2,1)S(1)}, bf16[256,2048]{1,0:T(8,128)(2,1)S(1)}, u32[]{:S(2)}, u32[]{:S(2)}) collective-permute-start(bf16[256,2048]{1,0:T(8,128)(2,1)S(1)} %constant_dynamic-update-slice_fusion.4.refs_2_.panel.refs_6_), channel_id=1, source_target_pairs={{0,16},{16,0},{1,17},{17,1},{2,18},{18,2},{3,19},{19,3},{4,20},{20... | collective-permute-start | bytes 3145736 | tf_op jit(solution)/shard_map/ppermute | solution.py:562
  71.6 1.0 copy-start.4
  72.6 0.9 copy-start.8
  74.2 0.9 copy-start.9
  77.9 21.9 %collective-permute-start.10 = (bf16[128,3584]{1,0:T(8,128)(2,1)}, bf16[128,3584]{1,0:T(8,128)(2,1)S(1)}, u32[]{:S(2)}, u32[]{:S(2)}) collective-permute-start(bf16[128,3584]{1,0:T(8,128)(2,1)} %shard_map.124.refs_0_), channel_id=1, source_target_pairs={{0,8},{4,12},{8,0},{12,4},{1,9},{5,13},{9,1},{13,5},{2,10},{6,14},... | collective-permute-start | bytes 2752520 | tf_op jit(solution)/shard_map/ppermute | solution.py:562
  91.2 10.1 %collective-permute-start.11 = (bf16[128,3584]{1,0:T(8,128)(2,1)}, bf16[128,3584]{1,0:T(8,128)(2,1)S(1)}, u32[]{:S(2)}, u32[]{:S(2)}) collective-permute-start(bf16[128,3584]{1,0:T(8,128)(2,1)} %get-tuple-element.35.refs_0_), channel_id=1, source_target_pairs={{0,4},{4,0},{8,12},{12,8},{1,5},{5,1},{9,13},{13,9},{2,6},{6,2},{1... | collective-permute-start | bytes 2752520 | tf_op jit(solution)/shard_map/ppermute | solution.py:567
  95.3 4.6 %copy-start.5 = (bf16[256,2048]{1,0:T(8,128)(2,1)}, bf16[256,2048]{1,0:T(8,128)(2,1)S(1)}, u32[]{:S(2)}) copy-start(bf16[256,2048]{1,0:T(8,128)(2,1)S(1)} %collective-permute-done.12.refs_2_.refs_7_) | copy-start | bytes 3145732
  101.4 0.9 copy-start.10
  105.2 5.2 %copy-start.11 = (bf16[128,3584]{1,0:T(8,128)(2,1)S(1)}, bf16[128,3584]{1,0:T(8,128)(2,1)}, u32[]{:S(2)}) copy-start(bf16[128,3584]{1,0:T(8,128)(2,1)} %shard_map.127.refs_6_) | copy-start | bytes 2752516
  110.3 2.7 %collective-permute-start.13 = (bf16[1,128,3584]{2,1,0:T(8,128)(2,1)}, bf16[1,128,3584]{2,1,0:T(8,128)(2,1)S(1)}, u32[]{:S(2)}, u32[]{:S(2)}) collective-permute-start(bf16[1,128,3584]{2,1,0:T(8,128)(2,1)} %get-tuple-element.36.refs_0_.refs_2_), channel_id=1, source_target_pairs={{0,4},{4,0},{8,12},{12,8},{1,5},{5,1},{9,13},{13,9},{2,6},{6,2},{1... | collective-permute-start | bytes 2752520 | tf_op jit(solution)/shard_map/ppermute | solution.py:567
  110.4 22.8 %collective-permute-start.17 = (bf16[128,3584]{1,0:T(8,128)(2,1)S(1)}, bf16[128,3584]{1,0:T(8,128)(2,1)S(1)}, u32[]{:S(2)}, u32[]{:S(2)}) collective-permute-start(bf16[128,3584]{1,0:T(8,128)(2,1)S(1)} %copy-done.11), channel_id=1, source_target_pairs={{0,8},{4,12},{8,0},{12,4},{1,9},{5,13},{9,1},{13,5},{2,10},{6,14},... | collective-permute-start | bytes 2752520 | tf_op jit(solution)/shard_map/ppermute | solution.py:562
  111.0 29.6 %collective-permute-start.19 = (bf16[1,128,3584]{2,1,0:T(8,128)(2,1)}, bf16[1,128,3584]{2,1,0:T(8,128)(2,1)S(1)}, u32[]{:S(2)}, u32[]{:S(2)}) collective-permute-start(bf16[1,128,3584]{2,1,0:T(8,128)(2,1)} %get-tuple-element.36.refs_0_.refs_2_), channel_id=1, source_target_pairs={{0,16},{16,0},{1,17},{17,1},{2,18},{18,2},{3,19},{19,3},{4,20},{20... | collective-permute-start | bytes 2752520 | tf_op jit(solution)/shard_map/ppermute | solution.py:562
  139.0 2.7 %copy-start.26 = (bf16[64,2048]{1,0:T(8,128)(2,1)S(1)}, bf16[64,2048]{1,0:T(8,128)(2,1)}, u32[]{:S(2)}) copy-start(bf16[64,2048]{1,0:T(8,128)(2,1)} %get-tuple-element.39) | copy-start | bytes 786436
  139.0 7.0 %copy-start.25 = (bf16[64,2048]{1,0:T(8,128)(2,1)S(1)}, bf16[64,2048]{1,0:T(8,128)(2,1)}, u32[]{:S(2)}) copy-start(bf16[64,2048]{1,0:T(8,128)(2,1)} %get-tuple-element.40) | copy-start | bytes 786436
  139.0 7.0 %copy-start.24 = (bf16[64,2048]{1,0:T(8,128)(2,1)S(1)}, bf16[64,2048]{1,0:T(8,128)(2,1)}, u32[]{:S(2)}) copy-start(bf16[64,2048]{1,0:T(8,128)(2,1)} %get-tuple-element.41) | copy-start | bytes 786436
  139.0 8.3 %collective-permute-start.18 = (bf16[2,128,3584]{2,1,0:T(8,128)(2,1)}, bf16[2,128,3584]{2,1,0:T(8,128)(2,1)S(1)}, u32[]{:S(2)}, u32[]{:S(2)}) collective-permute-start(bf16[2,128,3584]{2,1,0:T(8,128)(2,1)} %shard_map.131.refs_1_.refs_0_.refs_6_), channel_id=1, source_target_pairs={{0,4},{4,0},{8,12},{12,8},{1,5},{5,1},{9,13},{13,9},{2,6},{6,2},{1... | collective-permute-start | bytes 5505032 | tf_op jit(solution)/shard_map/ppermute | solution.py:567
  139.1 42.6 %collective-permute-start.24 = (bf16[2,128,3584]{2,1,0:T(8,128)(2,1)}, bf16[2,128,3584]{2,1,0:T(8,128)(2,1)S(1)}, u32[]{:S(2)}, u32[]{:S(2)}) collective-permute-start(bf16[2,128,3584]{2,1,0:T(8,128)(2,1)} %shard_map.131.refs_1_.refs_0_.refs_6_), channel_id=1, source_target_pairs={{0,16},{16,0},{1,17},{17,1},{2,18},{18,2},{3,19},{19,3},{4,20},{20... | collective-permute-start | bytes 5505032 | tf_op jit(solution)/shard_map/ppermute | solution.py:562
  141.5 4.5 %collective-permute-start.20 = (bf16[1,128,3584]{2,1,0:T(8,128)(2,1)}, bf16[1,128,3584]{2,1,0:T(8,128)(2,1)S(1)}, u32[]{:S(2)}, u32[]{:S(2)}) collective-permute-start(bf16[1,128,3584]{2,1,0:T(8,128)(2,1)} %shard_map.132.refs_4_), channel_id=1, source_target_pairs={{0,4},{4,0},{8,12},{12,8},{1,5},{5,1},{9,13},{13,9},{2,6},{6,2},{1... | collective-permute-start | bytes 2752520 | tf_op jit(solution)/shard_map/ppermute | solution.py:567
  141.7 38.5 %collective-permute-start.14 = (bf16[64,2048]{1,0:T(8,128)(2,1)S(1)}, bf16[64,2048]{1,0:T(8,128)(2,1)S(1)}, u32[]{:S(2)}, u32[]{:S(2)}) collective-permute-start(bf16[64,2048]{1,0:T(8,128)(2,1)S(1)} %copy-done.26), channel_id=1, source_target_pairs={{0,3},{1,0},{2,1},{3,2},{4,7},{5,4},{6,5},{7,6},{8,11},{9,8},{10,9... | collective-permute-start | bytes 786440 | tf_op jit(solution)/shard_map/ppermute | solution.py:562
  145.9 34.2 %collective-permute-start.15 = (bf16[64,2048]{1,0:T(8,128)(2,1)S(1)}, bf16[64,2048]{1,0:T(8,128)(2,1)S(1)}, u32[]{:S(2)}, u32[]{:S(2)}) collective-permute-start(bf16[64,2048]{1,0:T(8,128)(2,1)S(1)} %copy-done.25), channel_id=1, source_target_pairs={{0,1},{1,2},{2,3},{3,0},{4,5},{5,6},{6,7},{7,4},{8,9},{9,10},{10,1... | collective-permute-start | bytes 786440 | tf_op jit(solution)/shard_map/ppermute | solution.py:562
  146.0 1.3 copy-start.19
  146.0 34.2 %collective-permute-start.16 = (bf16[64,2048]{1,0:T(8,128)(2,1)S(1)}, bf16[64,2048]{1,0:T(8,128)(2,1)S(1)}, u32[]{:S(2)}, u32[]{:S(2)}) collective-permute-start(bf16[64,2048]{1,0:T(8,128)(2,1)S(1)} %copy-done.24), channel_id=1, source_target_pairs={{0,2},{1,3},{2,0},{3,1},{4,6},{5,7},{6,4},{7,5},{8,10},{9,11},{10,... | collective-permute-start | bytes 786440 | tf_op jit(solution)/shard_map/ppermute | solution.py:562
  147.3 1.2 copy-start
  180.2 1.5 copy-start.16
  180.2 1.5 copy-start.17
  180.2 1.5 copy-start.18
  181.7 1.2 copy-start.3
  182.9 0.9 copy-start.29
  182.9 5.2 %copy-start.28 = (bf16[64,2048]{1,0:T(8,128)(2,1)S(1)}, bf16[64,2048]{1,0:T(8,128)(2,1)}, u32[]{:S(2)}) copy-start(bf16[64,2048]{1,0:T(8,128)(2,1)} %get-tuple-element.47) | copy-start | bytes 786436
  182.9 5.2 %copy-start.27 = (bf16[64,2048]{1,0:T(8,128)(2,1)S(1)}, bf16[64,2048]{1,0:T(8,128)(2,1)}, u32[]{:S(2)}) copy-start(bf16[64,2048]{1,0:T(8,128)(2,1)} %get-tuple-element.48) | copy-start | bytes 786436
  182.9 7.1 %collective-permute-start.25 = (bf16[2,128,3584]{2,1,0:T(8,128)(2,1)}, bf16[2,128,3584]{2,1,0:T(8,128)(2,1)S(1)}, u32[]{:S(2)}, u32[]{:S(2)}) collective-permute-start(bf16[2,128,3584]{2,1,0:T(8,128)(2,1)} %shard_map.135.refs_8_), channel_id=1, source_target_pairs={{0,4},{4,0},{8,12},{12,8},{1,5},{5,1},{9,13},{13,9},{2,6},{6,2},{1... | collective-permute-start | bytes 5505032 | tf_op jit(solution)/shard_map/ppermute | solution.py:567
  183.9 35.3 %collective-permute-start.21 = (bf16[64,2048]{1,0:T(8,128)(2,1)S(1)}, bf16[64,2048]{1,0:T(8,128)(2,1)S(1)}, u32[]{:S(2)}, u32[]{:S(2)}) collective-permute-start(bf16[64,2048]{1,0:T(8,128)(2,1)S(1)} %copy-done.29), channel_id=1, source_target_pairs={{0,3},{1,0},{2,1},{3,2},{4,7},{5,4},{6,5},{7,6},{8,11},{9,8},{10,9... | collective-permute-start | bytes 786440 | tf_op jit(solution)/shard_map/ppermute | solution.py:562
  188.2 31.0 %collective-permute-start.22 = (bf16[64,2048]{1,0:T(8,128)(2,1)S(1)}, bf16[64,2048]{1,0:T(8,128)(2,1)S(1)}, u32[]{:S(2)}, u32[]{:S(2)}) collective-permute-start(bf16[64,2048]{1,0:T(8,128)(2,1)S(1)} %copy-done.28), channel_id=1, source_target_pairs={{0,1},{1,2},{2,3},{3,0},{4,5},{5,6},{6,7},{7,4},{8,9},{9,10},{10,1... | collective-permute-start | bytes 786440 | tf_op jit(solution)/shard_map/ppermute | solution.py:562
  188.2 31.0 %collective-permute-start.23 = (bf16[64,2048]{1,0:T(8,128)(2,1)S(1)}, bf16[64,2048]{1,0:T(8,128)(2,1)S(1)}, u32[]{:S(2)}, u32[]{:S(2)}) collective-permute-start(bf16[64,2048]{1,0:T(8,128)(2,1)S(1)} %copy-done.27), channel_id=1, source_target_pairs={{0,2},{1,3},{2,0},{3,1},{4,6},{5,7},{6,4},{7,5},{8,10},{9,11},{10,... | collective-permute-start | bytes 786440 | tf_op jit(solution)/shard_map/ppermute | solution.py:562
  190.1 1.2 copy-start.15
  (8 other events, 7.0 us)

commit v4 on v3

--- a/solution.py
+++ b/solution.py
@@ -312,22 +312,11 @@
     )(core, *pieces, *weights, *earlier)
 
 
-def pair_kernel(mine_ref, other_ref, *refs):
-    wide = tile_of(mine_ref.shape[1], 512)
-    for i in range(mine_ref.shape[1] // wide):
-        span = slice(i * wide, (i + 1) * wide)
-        refs[-1][:, span] = add_up([mine_ref[:, span], other_ref[:, span]]).astype(jnp.bfloat16)
-
-
-def pair_sum(mine, other, *earlier):
-    return pl.pallas_call(
-        pair_kernel,
-        out_shape=jax.ShapeDtypeStruct(mine.shape, jnp.bfloat16),
-        in_specs=[whole(VM)] * 2 + [whole(pl.ANY)] * len(earlier),
-        out_specs=whole(VM),
-        compiler_params=params(),
-        cost_estimate=cost(0, mine.size * 8),
-    )(mine, other, *earlier)
+def pair_sum(mine, other, token=None):
+    total = mine + other.astype(jnp.float32)
+    if token is not None:
+        total = total + token
+    return total.astype(jnp.bfloat16)
 
 
 def hold_kernel(*refs):
@@ -366,19 +355,12 @@
     )(*parts, *earlier)
 
 
-def mark_kernel(*refs):
-    refs[-1][...] = jnp.zeros_like(refs[-1])
-
-
 def mark(*earlier):
-    return pl.pallas_call(
-        mark_kernel,
-        out_shape=jax.ShapeDtypeStruct((8, BLK), jnp.float32),
-        in_specs=[whole(pl.ANY)] * len(earlier),
-        out_specs=whole(VM),
-        compiler_params=params(),
-        cost_estimate=pl.CostEstimate(flops=0, bytes_accessed=MARK, transcendentals=0),
-    )(*earlier)
+    total = 0.0
+    for x in earlier:
+        corner = lax.slice(x, (0,) * x.ndim, (1,) * x.ndim).reshape(())
+        total = total + jnp.abs(corner.astype(jnp.float32))
+    return lax.optimization_barrier(jnp.minimum(total, 0.0))
 
 
 def across(rows, width):
@@ -638,7 +620,7 @@
     up_mine, up_other, w_up = project_blocks(
         core, x_whole, up_table, up_blocks[0, 0], feats, units, False, gate_sent
     )
-    token = mark(up_other, *gate_got, c_whole, *x_groups[1:])
+    token = mark(*gate_got, c_whole, *x_groups[1:])
     up_swapped = swap_cores(up_other)
     up_sent = pair_sum(up_mine, up_swapped, token)
 
@@ -647,7 +629,7 @@
     back_mine, back_other, w_down = project_blocks(
         core, c_whole, down_table, down_blocks[0, 0], units, feats, True, up_sent
     )
-    token = mark(back_other, *up_got, *c_groups[1:])
+    token = mark(*up_got, *c_groups[1:])
     back_swapped = swap_cores(back_other)
     back_sent = pair_sum(back_mine, back_swapped, token)
 
@@ -658,8 +640,7 @@
     hidden_far = other_groups(hidden)
     hidden_pieces = [hidden, swap_cores(hidden)]
     out_cut = back(core, hidden_pieces, [w_down], n_col, False)
-    token = mark(out_cut[0], *back_got)
-    grads = act_grads([back_mine, back_swapped] + back_got, by_gate, by_up, token)
+    grads = act_grads([back_mine, back_swapped] + back_got, by_gate, by_up, out_cut[0])
     hidden_pieces += far_pieces([[hold(far, grads) for far in hidden_far]])
 
     grads_far = other_groups(grads)
@@ -672,7 +653,7 @@
         c_groups,
         slots,
         scale,
-        grad_pieces[1],
+        grads,
     )
     in_cut = back(core, grad_pieces, [w_gate, w_up], n_col, True, down_grad)
     out_kept = scatter(out_cut)

time: 224 us -> 220 us (0.982)
  Pallas kernels: 135 us -> 125 us
  other arithmetic: 5.53 us -> 10.9 us
  between operations: 1.03 us -> 4.43 us
    pallas_call x6 -> x0, Pallas kernels: 10.2 us -> none  [the longest x3 8.46 us: pair_sum(): pl.pallas_call(pair_kernel, out_shape=jax.ShapeDtypeStruct(mine.shape, jn...]
    convert_element_type x0 -> x3, other arithmetic: none -> 5.3 us  [pair_sum(): return total.astype(jnp.bfloat16)]
    unnamed x66 -> x70, local copies, waits for them, and re-layouts: 16.1 us -> 11.1 us
    slice x0 -> x5, local copies, waits for them, and re-layouts: none -> 3.29 us  [mark(): corner = lax.slice(x, (0,) * x.ndim, (1,) * x.ndim).reshape(())]
  transfers between devices with their start and end apart: 26 -> 26, of which waited for: 8 -> 7; matrix products, arithmetic and copies ran while one was open for 3% -> 6% of each run, Pallas kernels for 52% -> 50%
where the time goes in v4:
time: 220 us; the launch traced here: 218 us
  Pallas kernels  125 us (57%)
  starting transfers between devices  37.1 us (17%)
  waiting for transfers between devices  27 us (12%)
  local copies, waits for them, and re-layouts  14.4 us (7%)
  other arithmetic  10.9 us (5%)
  between operations  4.43 us (2%)
    pallas_call x2, Pallas kernels, block_grads(): pl.pallas_call(functools.partial(block_grad_kernel, mats, len(lefts), len...  45.2 us
    ppermute x19, starting transfers between devices, shift(): return lax.ppermute(x, axis, [(i, (i + by) % n) for i in range(n)])  36.5 us
    ppermute x19, waiting for transfers between devices, shift(): return lax.ppermute(x, axis, [(i, (i + by) % n) for i in range(n)])  26.4 us
    pallas_call x2, Pallas kernels, project_blocks(): pl.pallas_call(functools.partial(project_blocks_kernel, transposed, rows,...  25.5 us
    pallas_call x2, Pallas kernels, back(): pl.pallas_call(functools.partial(back_kernel, transposed, n_pieces, mats,...  22.5 us
    unnamed x70, local copies, waits for them, and re-layouts  11.1 us
    pallas_call x1, Pallas kernels, densify(): pl.pallas_call(functools.partial(densify_kernel, mats, rows, cols, panels...  10.8 us
    pallas_call x1, Pallas kernels, project(): pl.pallas_call(functools.partial(project_kernel, transposed, tile), out_s...  8.87 us
  transfers between devices with their start and end apart: 26, of which 7 were waited for; matrix products, arithmetic and copies ran while one was open for 6% of the time, Pallas kernels for 50%

profile of v4, /device:TPU:0, one launch (start us, length us, event | category | flops | bytes accessed | tf_op | source)
XLA Modules:
  0.0 218.4 jit_solution(17832871345040099367)
XLA Ops:
  0.6 4.1 %collective-permute-start.1 = (bf16[64,2048]{1,0:T(8,128)(2,1)}, bf16[64,2048]{1,0:T(8,128)(2,1)S(1)}, u32[]{:S(2)}, u32[]{:S(2)}) collective-permute-start(bf16[64,2048]{1,0:T(8,128)(2,1)} %param.8), channel_id=1, source_target_pairs={{0,2},{1,3},{2,0},{3,1},{4,6},{5,7},{6,4},{7,5},{8,10},{9,11},{10,... | collective-permute-start | bytes 786440 | tf_op jit(solution)/shard_map/ppermute | solution.py:544
  4.7 1.6 collective-permute-start
  6.3 2.2 %collective-permute-start.2 = (bf16[64,2048]{1,0:T(8,128)(2,1)}, bf16[64,2048]{1,0:T(8,128)(2,1)S(1)}, u32[]{:S(2)}, u32[]{:S(2)}) collective-permute-start(bf16[64,2048]{1,0:T(8,128)(2,1)} %param.8), channel_id=1, source_target_pairs={{0,3},{1,0},{2,1},{3,2},{4,7},{5,4},{6,5},{7,6},{8,11},{9,8},{10,9... | collective-permute-start | bytes 786440 | tf_op jit(solution)/shard_map/ppermute | solution.py:544
  8.6 1.0 constant_dynamic-update-slice_fusion.3
  9.6 0.8 fusion.2
  10.3 0.8 fusion
  12.0 10.8 %shard_map.119.weight.refs_2_ = bf16[2048,3584]{1,0:T(8,128)(2,1)} custom-call(s32[448]{0:T(512)} %broadcast_subtract_fusion.2.refs_0_, bf16[336,128,128]{2,1,0:T(8,128)(2,1)} %bitcast.16), custom_call_target="tpu_custom_call" | custom-call | bytes 25 | tf_op jit(solution)/shard_map/pallas_call | solution.py:104
  23.4 0.7 collective-permute-done.2
  24.1 1.0 copy-done
  25.1 8.9 %shard_map.120 = (f32[128,3584]{1,0:T(8,128)}, bf16[128,3584]{1,0:T(8,128)(2,1)}) custom-call(s32[1]{0:T(128)} %bitcast.core_ref, bf16[256,2048]{1,0:T(8,128)(2,1)} %copy-done, bf16[2048,3584]{1,0:T(8,128)(2,1)} %shard_map.119.weight.refs_2_), custom_call_target="tpu_custom_call" | custom-call | flops 3758 | bytes 14 | tf_op jit(solution)/shard_map/pallas_call | solution.py:165
  34.6 6.7 %collective-permute-start.9 = (bf16[64,2048]{1,0:T(8,128)(2,1)S(1)}, bf16[64,2048]{1,0:T(8,128)(2,1)S(1)}, u32[]{:S(2)}, u32[]{:S(2)}) collective-permute-start(bf16[64,2048]{1,0:T(8,128)(2,1)S(1)} %copy-done.22), channel_id=1, source_target_pairs={{0,2},{1,3},{2,0},{3,1},{4,6},{5,7},{6,4},{7,5},{8,10},{9,11},{10,... | collective-permute-start | bytes 786440 | tf_op jit(solution)/shard_map/ppermute | solution.py:544
  41.4 1.5 collective-permute-start.6
  42.9 2.0 add_convert_fusion.2.refs_0_
  44.9 1.6 collective-permute-start.4
  46.5 12.8 %shard_map.121 = (f32[128,3584]{1,0:T(8,128)}, bf16[128,3584]{1,0:T(8,128)(2,1)}, bf16[2048,3584]{1,0:T(8,128)(2,1)}) custom-call(s32[1]{0:T(128)} %bitcast.core_ref, s32[448]{0:T(512)} %broadcast_subtract_fusion.1.table.refs_1_, bf16[256,2048]{1,0:T(8,128)(2,1)} %copy-done, bf16[336,128,128]{2,1,0:T(8,128)(2,1)} %bitcast.17, bf16[128,3584]{1,0:T(8,128)(2,1)} %copy-done.7), custom_call_target="tpu_custom_call" | custom-call | flops 3758 | bytes 29 | tf_op jit(solution)/shard_map/pallas_call | solution.py:230
  60.6 4.1 %collective-permute-start.10 = (bf16[64,2048]{1,0:T(8,128)(2,1)S(1)}, bf16[64,2048]{1,0:T(8,128)(2,1)S(1)}, u32[]{:S(2)}, u32[]{:S(2)}) collective-permute-start(bf16[64,2048]{1,0:T(8,128)(2,1)S(1)} %copy-done.22), channel_id=1, source_target_pairs={{0,3},{1,0},{2,1},{3,2},{4,7},{5,4},{6,5},{7,6},{8,11},{9,8},{10,9... | collective-permute-start | bytes 786440 | tf_op jit(solution)/shard_map/ppermute | solution.py:544
  64.7 6.2 %collective-permute-done.10 = bf16[64,2048]{1,0:T(8,128)(2,1)S(1)} collective-permute-done((bf16[64,2048]{1,0:T(8,128)(2,1)S(1)}, bf16[64,2048]{1,0:T(8,128)(2,1)S(1)}, u32[]{:S(2)}, u32[]{:S(2)}) %collective-permute-start.10) | collective-permute-done | bytes 262176 | tf_op jit(solution)/shard_map/ppermute | solution.py:544
  74.9 0.8 collective-permute-start.7
  76.3 12.8 %shard_map.122 = (f32[128,3584]{1,0:T(8,128)}, bf16[128,3584]{1,0:T(8,128)(2,1)}, bf16[3584,2048]{1,0:T(8,128)(2,1)}) custom-call(s32[1]{0:T(128)} %bitcast.core_ref, s32[448]{0:T(512)} %broadcast_subtract_fusion.table.refs_0_, bf16[256,2048]{1,0:T(8,128)(2,1)} %copy-done.4, bf16[336,128,128]{2,1,0:T(8,128)(2,1)} %bitcast.18, bf16[128,3584]{1,0:T(8,128)(2,1)} %copy-done.12), custom_call_target="tpu_custom_call" | custom-call | flops 3758 | bytes 29 | tf_op jit(solution)/shard_map/pallas_call | solution.py:230
  89.2 6.5 %collective-permute-done.12.refs_7_ = bf16[256,2048]{1,0:T(8,128)(2,1)S(1)} collective-permute-done((bf16[256,2048]{1,0:T(8,128)(2,1)S(1)}, bf16[256,2048]{1,0:T(8,128)(2,1)S(1)}, u32[]{:S(2)}, u32[]{:S(2)}) %collective-permute-start.12) | collective-permute-done | bytes 1048608 | tf_op jit(solution)/shard_map/ppermute | solution.py:544
  96.9 1.1 slice.55
  98.8 3.0 %add_convert_fusion.refs_6_ = bf16[128,3584]{1,0:T(8,128)(2,1)} fusion(f32[128,3584]{1,0:T(8,128)} %get-tuple-element.34.refs_0_, bf16[128,3584]{1,0:T(8,128)(2,1)S(1)} %collective-permute-done.11.refs_1_, f32[]{:T(128)} %bitcast.8), kind=kLoop, calls=%fused_computation | loop fusion | flops 1835008 | bytes 3670020 | tf_op jit(solution)/shard_map/convert_element_type | solution.py:319
  101.8 5.0 %shard_map.123 = (bf16[1,128,3584]{2,1,0:T(8,128)(2,1)}, f32[128,3584]{1,0:T(8,128)}, f32[128,3584]{1,0:T(8,128)}) custom-call(f32[128,3584]{1,0:T(8,128)} %get-tuple-element.29.refs_0_, bf16[128,3584]{1,0:T(8,128)(2,1)} %copy-done.6, bf16[128,3584]{1,0:T(8,128)(2,1)} %copy-done.20, f32[128,3584]{1,0:T(8,128)} %get-tuple-element.31.refs_3_, ...), custom_call_target="tpu_custom_call" | custom-call | bytes 13 | tf_op jit(solution)/shard_map/pallas_call | solution.py:386
  106.9 0.9 collective-permute-start.17
  107.8 1.2 collective-permute-start.19
  109.6 0.9 copy-done.10
  110.5 8.3 %shard_map.124 = (f32[64,2048]{1,0:T(8,128)}, bf16[64,2048]{1,0:T(8,128)(2,1)}, bf16[64,2048]{1,0:T(8,128)(2,1)}, bf16[64,2048]{1,0:T(8,128)(2,1)}) custom-call(s32[1]{0:T(128)} %bitcast.core_ref, bf16[1,128,3584]{2,1,0:T(8,128)(2,1)} %get-tuple-element.36.refs_0_.refs_2_, bf16[1,128,3584]{2,1,0:T(8,128)(2,1)} %copy-done.10, ...), custom_call_target="tpu_custom_call" | custom-call | flops 3758 | bytes 14 | tf_op jit(solution)/shard_map/pallas_call | solution.py:297
  118.8 10.8 %collective-permute-done.17.refs_2_ = bf16[128,3584]{1,0:T(8,128)(2,1)S(1)} collective-permute-done((bf16[128,3584]{1,0:T(8,128)(2,1)S(1)}, bf16[128,3584]{1,0:T(8,128)(2,1)S(1)}, u32[]{:S(2)}, u32[]{:S(2)}) %collective-permute-start.17) | collective-permute-done | bytes 917536 | tf_op jit(solution)/shard_map/ppermute | solution.py:544
  129.7 0.9 copy-done.19
  130.6 4.3 %shard_map.125.refs_1_.refs_8_.refs_0_.refs_6_ = bf16[2,128,3584]{2,1,0:T(8,128)(2,1)} custom-call(f32[128,3584]{1,0:T(8,128)} %get-tuple-element.34.refs_0_, bf16[128,3584]{1,0:T(8,128)(2,1)} %copy-done.5, bf16[128,3584]{1,0:T(8,128)(2,1)} %copy-done.19, f32[128,3584]{1,0:T(8,128)} %get-tuple-element.42.refs_3_, f32[128,3584]{1,0:T(8,128)} %get-tuple-element.43.refs_4_, ...), custom_call_target="tpu_custom_call" | custom-call | bytes 9 | tf_op jit(solution)/shard_map/pallas_call | solution.py:411
  135.0 1.3 collective-permute-start.24
  136.3 0.9 copy-done.8
  137.4 4.3 %collective-permute-start.14 = (bf16[64,2048]{1,0:T(8,128)(2,1)S(1)}, bf16[64,2048]{1,0:T(8,128)(2,1)S(1)}, u32[]{:S(2)}, u32[]{:S(2)}) collective-permute-start(bf16[64,2048]{1,0:T(8,128)(2,1)S(1)} %copy-done.28), channel_id=1, source_target_pairs={{0,3},{1,0},{2,1},{3,2},{4,7},{5,4},{6,5},{7,6},{8,11},{9,8},{10,9... | collective-permute-start | bytes 786440 | tf_op jit(solution)/shard_map/ppermute | solution.py:544
  141.7 0.7 collective-permute-start.16
  142.4 0.6 convert_reduce_fusion.2
  143.0 17.6 %shard_map.127.refs_4_ = bf16[336,128,128]{2,1,0:T(8,128)(2,1)} custom-call(s32[1]{0:T(128)} %bitcast.core_ref, s32[448]{0:T(512)} %broadcast_subtract_fusion.table.refs_0_, s32[1]{0:T(128)} %bitcast.9.refs_1_, bf16[1,128,3584]{2,1,0:T(8,128)(2,1)} %get-tuple-element.36.refs_0_.refs_2_, bf16[1,128,3584]{2,1,0:T(8,128)(2,1)} %copy-done.10, ...), custom_call_target="tpu_custom_call" | custom-call | flops 7516 | bytes 11 | tf_op jit(solution)/shard_map/pallas_call | solution.py:514
  160.6 1.2 copy-done.2
  161.8 14.1 %shard_map.128 = (f32[64,2048]{1,0:T(8,128)}, bf16[64,2048]{1,0:T(8,128)(2,1)}, bf16[64,2048]{1,0:T(8,128)(2,1)}, bf16[64,2048]{1,0:T(8,128)(2,1)}) custom-call(s32[1]{0:T(128)} %bitcast.core_ref, bf16[2,128,3584]{2,1,0:T(8,128)(2,1)} %shard_map.125.refs_1_.refs_8_.refs_0_.refs_6_, bf16[2,128,3584]{2,1,0:T(8,128)(2,1)} %copy-done.2, ...), custom_call_target="tpu_custom_call" | custom-call | flops 7516 | bytes 29 | tf_op jit(solution)/shard_map/pallas_call | solution.py:297
  176.0 1.7 collective-permute-done.24.refs_0_
  177.7 1.2 copy-done.1
  178.9 0.9 copy-done.31
  179.8 4.3 %collective-permute-start.21 = (bf16[64,2048]{1,0:T(8,128)(2,1)S(1)}, bf16[64,2048]{1,0:T(8,128)(2,1)S(1)}, u32[]{:S(2)}, u32[]{:S(2)}) collective-permute-start(bf16[64,2048]{1,0:T(8,128)(2,1)S(1)} %copy-done.31), channel_id=1, source_target_pairs={{0,3},{1,0},{2,1},{3,2},{4,7},{5,4},{6,5},{7,6},{8,11},{9,8},{10,9... | collective-permute-start | bytes 786440 | tf_op jit(solution)/shard_map/ppermute | solution.py:544
  184.1 0.6 collective-permute-start.23
  185.4 0.6 convert_reduce_fusion.1
  186.0 1.3 copy-done.13
  187.3 27.6 %shard_map.130 = (bf16[336,128,128]{2,1,0:T(8,128)(2,1)}, bf16[336,128,128]{2,1,0:T(8,128)(2,1)}) custom-call(s32[1]{0:T(128)} %bitcast.core_ref, s32[448]{0:T(512)} %broadcast_subtract_fusion.2.refs_0_, s32[448]{0:T(512)} %broadcast_subtract_fusion.1.table.refs_1_, s32[1]{0:T(128)} %bitcast.10.refs_2_, s32[1]{0:T(128)} %bitcast.11.refs_3_, ...), custom_call_target="tpu_custom_call" | custom-call | flops 15032 | bytes 22 | tf_op jit(solution)/shard_map/pallas_call | solution.py:514
  215.0 0.7 copy-done.23
  215.9 2.6 %shard_map.131 = (bf16[64,2048]{1,0:T(8,128)(2,1)}, bf16[64,2048]{1,0:T(8,128)(2,1)}) custom-call(f32[64,2048]{1,0:T(8,128)} %get-tuple-element.38.refs_5_.refs_0_, bf16[64,2048]{1,0:T(8,128)(2,1)} %copy-done.16, bf16[64,2048]{1,0:T(8,128)(2,1)} %copy-done.17, bf16[64,2048]{1,0:T(8,128)(2,1)} %copy-done.18, f32[64,2048]{1,0:T(8,128)} %get-tuple-element.45.refs_1_.refs_4_, ...), custom_call_target="tpu_custom_call" | custom-call | bytes 1 | tf_op jit(solution)/shard_map/pallas_call | solution.py:348
  (107 shorter events, 8.4 us)
Async XLA Ops:
  0.6 22.7 %collective-permute-start.1 = (bf16[64,2048]{1,0:T(8,128)(2,1)}, bf16[64,2048]{1,0:T(8,128)(2,1)S(1)}, u32[]{:S(2)}, u32[]{:S(2)}) collective-permute-start(bf16[64,2048]{1,0:T(8,128)(2,1)} %param.8), channel_id=1, source_target_pairs={{0,2},{1,3},{2,0},{3,1},{4,6},{5,7},{6,4},{7,5},{8,10},{9,11},{10,... | collective-permute-start | bytes 786440 | tf_op jit(solution)/shard_map/ppermute | solution.py:544
  4.7 18.1 %collective-permute-start = (bf16[64,2048]{1,0:T(8,128)(2,1)}, bf16[64,2048]{1,0:T(8,128)(2,1)S(1)}, u32[]{:S(2)}, u32[]{:S(2)}) collective-permute-start(bf16[64,2048]{1,0:T(8,128)(2,1)} %param.8), channel_id=1, source_target_pairs={{0,1},{1,2},{2,3},{3,0},{4,5},{5,6},{6,7},{7,4},{8,9},{9,10},{10,1... | collective-permute-start | bytes 786440 | tf_op jit(solution)/shard_map/ppermute | solution.py:544
  6.3 17.8 %collective-permute-start.2 = (bf16[64,2048]{1,0:T(8,128)(2,1)}, bf16[64,2048]{1,0:T(8,128)(2,1)S(1)}, u32[]{:S(2)}, u32[]{:S(2)}) collective-permute-start(bf16[64,2048]{1,0:T(8,128)(2,1)} %param.8), channel_id=1, source_target_pairs={{0,3},{1,0},{2,1},{3,2},{4,7},{5,4},{6,5},{7,6},{8,11},{9,8},{10,9... | collective-permute-start | bytes 786440 | tf_op jit(solution)/shard_map/ppermute | solution.py:544
  25.1 9.5 %copy-start.22 = (bf16[64,2048]{1,0:T(8,128)(2,1)S(1)}, bf16[64,2048]{1,0:T(8,128)(2,1)}, u32[]{:S(2)}) copy-start(bf16[64,2048]{1,0:T(8,128)(2,1)} %param.9) | copy-start | bytes 786436
  34.0 8.9 %collective-permute-start.3 = (bf16[128,3584]{1,0:T(8,128)(2,1)}, bf16[128,3584]{1,0:T(8,128)(2,1)S(1)}, u32[]{:S(2)}, u32[]{:S(2)}) collective-permute-start(bf16[128,3584]{1,0:T(8,128)(2,1)} %get-tuple-element.30), channel_id=1, source_target_pairs={{0,4},{4,0},{8,12},{12,8},{1,5},{5,1},{9,13},{13,9},{2,6},{6,2},{1... | collective-permute-start | bytes 2752520 | tf_op jit(solution)/shard_map/ppermute | solution.py:549
  34.6 30.0 %collective-permute-start.9 = (bf16[64,2048]{1,0:T(8,128)(2,1)S(1)}, bf16[64,2048]{1,0:T(8,128)(2,1)S(1)}, u32[]{:S(2)}, u32[]{:S(2)}) collective-permute-start(bf16[64,2048]{1,0:T(8,128)(2,1)S(1)} %copy-done.22), channel_id=1, source_target_pairs={{0,2},{1,3},{2,0},{3,1},{4,6},{5,7},{6,4},{7,5},{8,10},{9,11},{10,... | collective-permute-start | bytes 786440 | tf_op jit(solution)/shard_map/ppermute | solution.py:544
  41.4 19.2 %collective-permute-start.8 = (bf16[64,2048]{1,0:T(8,128)(2,1)S(1)}, bf16[64,2048]{1,0:T(8,128)(2,1)S(1)}, u32[]{:S(2)}, u32[]{:S(2)}) collective-permute-start(bf16[64,2048]{1,0:T(8,128)(2,1)S(1)} %copy-done.22), channel_id=1, source_target_pairs={{0,1},{1,2},{2,3},{3,0},{4,5},{5,6},{6,7},{7,4},{8,9},{9,10},{10,1... | collective-permute-start | bytes 786440 | tf_op jit(solution)/shard_map/ppermute | solution.py:544
  41.4 30.1 %collective-permute-start.6 = (bf16[256,2048]{1,0:T(8,128)(2,1)}, bf16[256,2048]{1,0:T(8,128)(2,1)S(1)}, u32[]{:S(2)}, u32[]{:S(2)}) collective-permute-start(bf16[256,2048]{1,0:T(8,128)(2,1)} %copy-done), channel_id=1, source_target_pairs={{0,16},{16,0},{1,17},{17,1},{2,18},{18,2},{3,19},{19,3},{4,20},{20... | collective-permute-start | bytes 3145736 | tf_op jit(solution)/shard_map/ppermute | solution.py:544
  42.9 2.0 copy-start.6
  44.9 1.6 copy-start.7
  44.9 27.8 %collective-permute-start.4 = (bf16[128,3584]{1,0:T(8,128)(2,1)S(1)}, bf16[128,3584]{1,0:T(8,128)(2,1)S(1)}, u32[]{:S(2)}, u32[]{:S(2)}) collective-permute-start(bf16[128,3584]{1,0:T(8,128)(2,1)S(1)} %add_convert_fusion.2.refs_0_), channel_id=1, source_target_pairs={{0,8},{4,12},{8,0},{12,4},{1,9},{5,13},{9,1},{13,5},{2,10},{6,14},... | collective-permute-start | bytes 2752520 | tf_op jit(solution)/shard_map/ppermute | solution.py:544
  59.3 14.7 %copy-start.3 = (f32[128,3584]{1,0:T(8,128)S(1)}, f32[128,3584]{1,0:T(8,128)}, u32[]{:S(2)}) copy-start(f32[128,3584]{1,0:T(8,128)} %get-tuple-element.31.refs_3_) | copy-start | bytes 5505028
  59.3 14.7 %collective-permute-start.5 = (bf16[128,3584]{1,0:T(8,128)(2,1)}, bf16[128,3584]{1,0:T(8,128)(2,1)S(1)}, u32[]{:S(2)}, u32[]{:S(2)}) collective-permute-start(bf16[128,3584]{1,0:T(8,128)(2,1)} %get-tuple-element.32), channel_id=1, source_target_pairs={{0,4},{4,0},{8,12},{12,8},{1,5},{5,1},{9,13},{13,9},{2,6},{6,2},{1... | collective-permute-start | bytes 2752520 | tf_op jit(solution)/shard_map/ppermute | solution.py:549
  60.6 10.3 %collective-permute-start.10 = (bf16[64,2048]{1,0:T(8,128)(2,1)S(1)}, bf16[64,2048]{1,0:T(8,128)(2,1)S(1)}, u32[]{:S(2)}, u32[]{:S(2)}) collective-permute-start(bf16[64,2048]{1,0:T(8,128)(2,1)S(1)} %copy-done.22), channel_id=1, source_target_pairs={{0,3},{1,0},{2,1},{3,2},{4,7},{5,4},{6,5},{7,6},{8,11},{9,8},{10,9... | collective-permute-start | bytes 786440 | tf_op jit(solution)/shard_map/ppermute | solution.py:544
  70.9 3.4 %copy-start.4 = (bf16[256,2048]{1,0:T(8,128)(2,1)}, bf16[256,2048]{1,0:T(8,128)(2,1)S(1)}, u32[]{:S(2)}) copy-start(bf16[256,2048]{1,0:T(8,128)(2,1)S(1)} %constant_dynamic-update-slice_fusion.4.panel.refs_6_) | copy-start | bytes 3145732
  70.9 24.8 %collective-permute-start.12 = (bf16[256,2048]{1,0:T(8,128)(2,1)S(1)}, bf16[256,2048]{1,0:T(8,128)(2,1)S(1)}, u32[]{:S(2)}, u32[]{:S(2)}) collective-permute-start(bf16[256,2048]{1,0:T(8,128)(2,1)S(1)} %constant_dynamic-update-slice_fusion.4.panel.refs_6_), channel_id=1, source_target_pairs={{0,16},{16,0},{1,17},{17,1},{2,18},{18,2},{3,19},{19,3},{4,20},{20... | collective-permute-start | bytes 3145736 | tf_op jit(solution)/shard_map/ppermute | solution.py:544
  71.5 2.8 %copy-start.14 = (bf16[256,2048]{1,0:T(8,128)(2,1)}, bf16[256,2048]{1,0:T(8,128)(2,1)S(1)}, u32[]{:S(2)}) copy-start(bf16[256,2048]{1,0:T(8,128)(2,1)S(1)} %collective-permute-done.6.refs_5_) | copy-start | bytes 3145732
  72.7 16.4 %copy-start.20 = (bf16[128,3584]{1,0:T(8,128)(2,1)}, bf16[128,3584]{1,0:T(8,128)(2,1)S(1)}, u32[]{:S(2)}) copy-start(bf16[128,3584]{1,0:T(8,128)(2,1)S(1)} %collective-permute-done.4.refs_2_) | copy-start | bytes 2752516
  74.9 1.4 copy-start.12
  74.9 22.0 %collective-permute-start.7 = (bf16[128,3584]{1,0:T(8,128)(2,1)S(1)}, bf16[128,3584]{1,0:T(8,128)(2,1)}, u32[]{:S(2)}, u32[]{:S(2)}) collective-permute-start(bf16[128,3584]{1,0:T(8,128)(2,1)S(1)} %add_convert_fusion.1.refs_0_), channel_id=1, source_target_pairs={{0,8},{4,12},{8,0},{12,4},{1,9},{5,13},{9,1},{13,5},{2,10},{6,14},... | collective-permute-start | bytes 2752520 | tf_op jit(solution)/shard_map/ppermute | solution.py:544
  89.1 9.6 %collective-permute-start.11 = (bf16[128,3584]{1,0:T(8,128)(2,1)}, bf16[128,3584]{1,0:T(8,128)(2,1)S(1)}, u32[]{:S(2)}, u32[]{:S(2)}) collective-permute-start(bf16[128,3584]{1,0:T(8,128)(2,1)} %get-tuple-element.35), channel_id=1, source_target_pairs={{0,4},{4,0},{8,12},{12,8},{1,5},{5,1},{9,13},{13,9},{2,6},{6,2},{1... | collective-permute-start | bytes 2752520 | tf_op jit(solution)/shard_map/ppermute | solution.py:549
  95.7 6.0 %copy-start.15 = (bf16[256,2048]{1,0:T(8,128)(2,1)}, bf16[256,2048]{1,0:T(8,128)(2,1)S(1)}, u32[]{:S(2)}) copy-start(bf16[256,2048]{1,0:T(8,128)(2,1)S(1)} %collective-permute-done.12.refs_7_) | copy-start | bytes 3145732
  98.7 3.0 %copy-start.5 = (bf16[128,3584]{1,0:T(8,128)(2,1)}, bf16[128,3584]{1,0:T(8,128)(2,1)S(1)}, u32[]{:S(2)}) copy-start(bf16[128,3584]{1,0:T(8,128)(2,1)S(1)} %collective-permute-done.11.refs_1_) | copy-start | bytes 2752516
  101.8 5.1 %copy-start.11 = (bf16[128,3584]{1,0:T(8,128)(2,1)S(1)}, bf16[128,3584]{1,0:T(8,128)(2,1)}, u32[]{:S(2)}) copy-start(bf16[128,3584]{1,0:T(8,128)(2,1)} %add_convert_fusion.refs_6_) | copy-start | bytes 2752516
  106.8 2.7 %collective-permute-start.13 = (bf16[1,128,3584]{2,1,0:T(8,128)(2,1)}, bf16[1,128,3584]{2,1,0:T(8,128)(2,1)S(1)}, u32[]{:S(2)}, u32[]{:S(2)}) collective-permute-start(bf16[1,128,3584]{2,1,0:T(8,128)(2,1)} %get-tuple-element.36.refs_0_.refs_2_), channel_id=1, source_target_pairs={{0,4},{4,0},{8,12},{12,8},{1,5},{5,1},{9,13},{13,9},{2,6},{6,2},{1... | collective-permute-start | bytes 2752520 | tf_op jit(solution)/shard_map/ppermute | solution.py:549
  106.9 22.8 %collective-permute-start.17 = (bf16[128,3584]{1,0:T(8,128)(2,1)S(1)}, bf16[128,3584]{1,0:T(8,128)(2,1)S(1)}, u32[]{:S(2)}, u32[]{:S(2)}) collective-permute-start(bf16[128,3584]{1,0:T(8,128)(2,1)S(1)} %copy-done.11), channel_id=1, source_target_pairs={{0,8},{4,12},{8,0},{12,4},{1,9},{5,13},{9,1},{13,5},{2,10},{6,14},... | collective-permute-start | bytes 2752520 | tf_op jit(solution)/shard_map/ppermute | solution.py:544
  107.8 28.5 %collective-permute-start.19 = (bf16[1,128,3584]{2,1,0:T(8,128)(2,1)}, bf16[1,128,3584]{2,1,0:T(8,128)(2,1)S(1)}, u32[]{:S(2)}, u32[]{:S(2)}) collective-permute-start(bf16[1,128,3584]{2,1,0:T(8,128)(2,1)} %get-tuple-element.36.refs_0_.refs_2_), channel_id=1, source_target_pairs={{0,16},{16,0},{1,17},{17,1},{2,18},{18,2},{3,19},{19,3},{4,20},{20... | collective-permute-start | bytes 2752520 | tf_op jit(solution)/shard_map/ppermute | solution.py:544
  134.9 2.5 %copy-start.28 = (bf16[64,2048]{1,0:T(8,128)(2,1)S(1)}, bf16[64,2048]{1,0:T(8,128)(2,1)}, u32[]{:S(2)}) copy-start(bf16[64,2048]{1,0:T(8,128)(2,1)} %get-tuple-element.39) | copy-start | bytes 786436
  134.9 6.8 %copy-start.27 = (bf16[64,2048]{1,0:T(8,128)(2,1)S(1)}, bf16[64,2048]{1,0:T(8,128)(2,1)}, u32[]{:S(2)}) copy-start(bf16[64,2048]{1,0:T(8,128)(2,1)} %get-tuple-element.40) | copy-start | bytes 786436
  134.9 6.8 %copy-start.26 = (bf16[64,2048]{1,0:T(8,128)(2,1)S(1)}, bf16[64,2048]{1,0:T(8,128)(2,1)}, u32[]{:S(2)}) copy-start(bf16[64,2048]{1,0:T(8,128)(2,1)} %get-tuple-element.41) | copy-start | bytes 786436
  134.9 25.6 %collective-permute-start.18 = (bf16[2,128,3584]{2,1,0:T(8,128)(2,1)}, bf16[2,128,3584]{2,1,0:T(8,128)(2,1)S(1)}, u32[]{:S(2)}, u32[]{:S(2)}) collective-permute-start(bf16[2,128,3584]{2,1,0:T(8,128)(2,1)} %shard_map.125.refs_1_.refs_8_.refs_0_.refs_6_), channel_id=1, source_target_pairs={{0,4},{4,0},{8,12},{12,8},{1,5},{5,1},{9,13},{13,9},{2,6},{6,2},{1... | collective-permute-start | bytes 5505032 | tf_op jit(solution)/shard_map/ppermute | solution.py:549
  135.0 42.6 %collective-permute-start.24 = (bf16[2,128,3584]{2,1,0:T(8,128)(2,1)}, bf16[2,128,3584]{2,1,0:T(8,128)(2,1)S(1)}, u32[]{:S(2)}, u32[]{:S(2)}) collective-permute-start(bf16[2,128,3584]{2,1,0:T(8,128)(2,1)} %shard_map.125.refs_1_.refs_8_.refs_0_.refs_6_), channel_id=1, source_target_pairs={{0,16},{16,0},{1,17},{17,1},{2,18},{18,2},{3,19},{19,3},{4,20},{20... | collective-permute-start | bytes 5505032 | tf_op jit(solution)/shard_map/ppermute | solution.py:544
  137.2 4.5 %collective-permute-start.20 = (bf16[1,128,3584]{2,1,0:T(8,128)(2,1)}, bf16[1,128,3584]{2,1,0:T(8,128)(2,1)S(1)}, u32[]{:S(2)}, u32[]{:S(2)}) collective-permute-start(bf16[1,128,3584]{2,1,0:T(8,128)(2,1)} %shard_map.126.refs_4_), channel_id=1, source_target_pairs={{0,4},{4,0},{8,12},{12,8},{1,5},{5,1},{9,13},{13,9},{2,6},{6,2},{1... | collective-permute-start | bytes 2752520 | tf_op jit(solution)/shard_map/ppermute | solution.py:549
  137.4 38.5 %collective-permute-start.14 = (bf16[64,2048]{1,0:T(8,128)(2,1)S(1)}, bf16[64,2048]{1,0:T(8,128)(2,1)S(1)}, u32[]{:S(2)}, u32[]{:S(2)}) collective-permute-start(bf16[64,2048]{1,0:T(8,128)(2,1)S(1)} %copy-done.28), channel_id=1, source_target_pairs={{0,3},{1,0},{2,1},{3,2},{4,7},{5,4},{6,5},{7,6},{8,11},{9,8},{10,9... | collective-permute-start | bytes 786440 | tf_op jit(solution)/shard_map/ppermute | solution.py:544
  141.7 34.2 %collective-permute-start.15 = (bf16[64,2048]{1,0:T(8,128)(2,1)S(1)}, bf16[64,2048]{1,0:T(8,128)(2,1)S(1)}, u32[]{:S(2)}, u32[]{:S(2)}) collective-permute-start(bf16[64,2048]{1,0:T(8,128)(2,1)S(1)} %copy-done.27), channel_id=1, source_target_pairs={{0,1},{1,2},{2,3},{3,0},{4,5},{5,6},{6,7},{7,4},{8,9},{9,10},{10,1... | collective-permute-start | bytes 786440 | tf_op jit(solution)/shard_map/ppermute | solution.py:544
  141.7 1.3 copy-start.21
  141.7 34.2 %collective-permute-start.16 = (bf16[64,2048]{1,0:T(8,128)(2,1)S(1)}, bf16[64,2048]{1,0:T(8,128)(2,1)S(1)}, u32[]{:S(2)}, u32[]{:S(2)}) collective-permute-start(bf16[64,2048]{1,0:T(8,128)(2,1)S(1)} %copy-done.26), channel_id=1, source_target_pairs={{0,2},{1,3},{2,0},{3,1},{4,6},{5,7},{6,4},{7,5},{8,10},{9,11},{10,... | collective-permute-start | bytes 786440 | tf_op jit(solution)/shard_map/ppermute | solution.py:544
  175.9 1.7 copy-start.16
  175.9 1.7 copy-start.17
  176.0 1.7 copy-start.18
  177.7 1.2 copy-start.1
  178.9 5.2 %copy-start.30 = (bf16[64,2048]{1,0:T(8,128)(2,1)S(1)}, bf16[64,2048]{1,0:T(8,128)(2,1)}, u32[]{:S(2)}) copy-start(bf16[64,2048]{1,0:T(8,128)(2,1)} %get-tuple-element.47) | copy-start | bytes 786436
  178.9 5.2 %copy-start.29 = (bf16[64,2048]{1,0:T(8,128)(2,1)S(1)}, bf16[64,2048]{1,0:T(8,128)(2,1)}, u32[]{:S(2)}) copy-start(bf16[64,2048]{1,0:T(8,128)(2,1)} %get-tuple-element.48) | copy-start | bytes 786436
  178.9 7.1 %collective-permute-start.25 = (bf16[2,128,3584]{2,1,0:T(8,128)(2,1)}, bf16[2,128,3584]{2,1,0:T(8,128)(2,1)S(1)}, u32[]{:S(2)}, u32[]{:S(2)}) collective-permute-start(bf16[2,128,3584]{2,1,0:T(8,128)(2,1)} %shard_map.129.refs_8_), channel_id=1, source_target_pairs={{0,4},{4,0},{8,12},{12,8},{1,5},{5,1},{9,13},{13,9},{2,6},{6,2},{1... | collective-permute-start | bytes 5505032 | tf_op jit(solution)/shard_map/ppermute | solution.py:549
  179.8 35.1 %collective-permute-start.21 = (bf16[64,2048]{1,0:T(8,128)(2,1)S(1)}, bf16[64,2048]{1,0:T(8,128)(2,1)S(1)}, u32[]{:S(2)}, u32[]{:S(2)}) collective-permute-start(bf16[64,2048]{1,0:T(8,128)(2,1)S(1)} %copy-done.31), channel_id=1, source_target_pairs={{0,3},{1,0},{2,1},{3,2},{4,7},{5,4},{6,5},{7,6},{8,11},{9,8},{10,9... | collective-permute-start | bytes 786440 | tf_op jit(solution)/shard_map/ppermute | solution.py:544
  184.1 30.8 %collective-permute-start.22 = (bf16[64,2048]{1,0:T(8,128)(2,1)S(1)}, bf16[64,2048]{1,0:T(8,128)(2,1)S(1)}, u32[]{:S(2)}, u32[]{:S(2)}) collective-permute-start(bf16[64,2048]{1,0:T(8,128)(2,1)S(1)} %copy-done.30), channel_id=1, source_target_pairs={{0,1},{1,2},{2,3},{3,0},{4,5},{5,6},{6,7},{7,4},{8,9},{9,10},{10,1... | collective-permute-start | bytes 786440 | tf_op jit(solution)/shard_map/ppermute | solution.py:544
  184.1 30.8 %collective-permute-start.23 = (bf16[64,2048]{1,0:T(8,128)(2,1)S(1)}, bf16[64,2048]{1,0:T(8,128)(2,1)S(1)}, u32[]{:S(2)}, u32[]{:S(2)}) collective-permute-start(bf16[64,2048]{1,0:T(8,128)(2,1)S(1)} %copy-done.29), channel_id=1, source_target_pairs={{0,2},{1,3},{2,0},{3,1},{4,6},{5,7},{6,4},{7,5},{8,10},{9,11},{10,... | collective-permute-start | bytes 786440 | tf_op jit(solution)/shard_map/ppermute | solution.py:544
  186.0 1.3 copy-start.13
  (10 other events, 9.2 us)

commit v5 on v4

--- a/solution.py
+++ b/solution.py
@@ -367,35 +367,44 @@
     return pl.BlockSpec((rows, tile_of(width, POINT_WIDE)), lambda i: (0, i))
 
 
-def act_kernel(n_sum, *refs):
-    gates, ups = refs[:n_sum], refs[n_sum : 2 * n_sum]
-    hidden_ref, by_gate_ref, by_up_ref = refs[-3:]
-    span = slice(None)
-    gate = add_up([ref[:, span] for ref in gates])
-    up = add_up([ref[:, span] for ref in ups])
+def hidden_kernel(n_sum, *refs):
+    gate = add_up([ref[...] for ref in refs[:n_sum]])
+    up = add_up([ref[...] for ref in refs[n_sum : 2 * n_sum]])
+    refs[-1][0] = (gate * jax.nn.sigmoid(gate) * up).astype(jnp.bfloat16)
+
+
+def slopes_kernel(n_sum, *refs):
+    gate = add_up([ref[...] for ref in refs[:n_sum]])
+    up = add_up([ref[...] for ref in refs[n_sum : 2 * n_sum]])
     sigma = jax.nn.sigmoid(gate)
-    active = gate * sigma
-    hidden_ref[0, :, span] = (active * up).astype(jnp.bfloat16)
-    by_gate_ref[:, span] = up * sigma * (1.0 + gate * (1.0 - sigma))
-    by_up_ref[:, span] = active
+    refs[-2][...] = up * sigma * (1.0 + gate * (1.0 - sigma))
+    refs[-1][...] = gate * sigma
+
+
+def pointwise(kernel, gates, ups, outs, *earlier):
+    rows, width = gates[0].shape
+    return pl.pallas_call(
+        functools.partial(kernel, len(gates)),
+        out_shape=tuple(shape for shape, _ in outs),
+        grid=(width // tile_of(width, POINT_WIDE),),
+        in_specs=[across(rows, width)] * (2 * len(gates)) + [whole(pl.ANY)] * len(earlier),
+        out_specs=tuple(spec for _, spec in outs),
+        compiler_params=params(),
+        cost_estimate=cost(0, rows * width * 30),
+    )(*gates, *ups, *earlier)
 
 
 def act(gates, ups, *earlier):
     rows, width = gates[0].shape
-    wide = jax.ShapeDtypeStruct((rows, width), jnp.float32)
-    return pl.pallas_call(
-        functools.partial(act_kernel, len(gates)),
-        out_shape=(jax.ShapeDtypeStruct((1, rows, width), jnp.bfloat16), wide, wide),
-        grid=(width // tile_of(width, POINT_WIDE),),
-        in_specs=[across(rows, width)] * (2 * len(gates)) + [whole(pl.ANY)] * len(earlier),
-        out_specs=(
-            pl.BlockSpec((1, rows, tile_of(width, POINT_WIDE)), lambda i: (0, 0, i)),
-            across(rows, width),
-            across(rows, width),
-        ),
-        compiler_params=params(),
-        cost_estimate=cost(0, rows * width * 30),
-    )(*gates, *ups, *earlier)
+    spec = pl.BlockSpec((1, rows, tile_of(width, POINT_WIDE)), lambda i: (0, 0, i))
+    outs = [(jax.ShapeDtypeStruct((1, rows, width), jnp.bfloat16), spec)]
+    return pointwise(hidden_kernel, gates, ups, outs, *earlier)[0]
+
+
+def slopes(gates, ups, *earlier):
+    rows, width = gates[0].shape
+    out = (jax.ShapeDtypeStruct((rows, width), jnp.float32), across(rows, width))
+    return pointwise(slopes_kernel, gates, ups, [out, out], *earlier)
 
 
 def grads_kernel(n_sum, *refs):
@@ -634,13 +643,14 @@
     back_sent = pair_sum(back_mine, back_swapped, token)
 
     back_got = other_chips(back_sent)
-    hidden, by_gate, by_up = act(
-        [gate_mine, gate_swapped] + gate_got, [up_mine, up_swapped] + up_got, back_sent
-    )
+    gate_sums = [gate_mine, gate_swapped] + gate_got
+    up_sums = [up_mine, up_swapped] + up_got
+    hidden = act(gate_sums, up_sums, back_sent)
     hidden_far = other_groups(hidden)
     hidden_pieces = [hidden, swap_cores(hidden)]
     out_cut = back(core, hidden_pieces, [w_down], n_col, False)
-    grads = act_grads([back_mine, back_swapped] + back_got, by_gate, by_up, out_cut[0])
+    by_gate, by_up = slopes(gate_sums, up_sums, out_cut[0])
+    grads = act_grads([back_mine, back_swapped] + back_got, by_gate, by_up)
     hidden_pieces += far_pieces([[hold(far, grads) for far in hidden_far]])
 
     grads_far = other_groups(grads)

time: 220 us -> 216 us (0.982)
  starting transfers between devices: 37.1 us -> 31 us
  Pallas kernels: 125 us -> 130 us
    ppermute x19, starting transfers between devices: 36.5 us -> 30.6 us  [shift(): return lax.ppermute(x, axis, [(i, (i + by) % n) for i in range(n)])]
    pallas_call x1 -> x2, Pallas kernels: 5.04 us -> 9.18 us  [pointwise(): pl.pallas_call(functools.partial(kernel, len(gates)), out_shape=tuple((sh...]
    unnamed x70 -> x72, local copies, waits for them, and re-layouts: 11.1 us -> 11.1 us
  transfers between devices with their start and end apart: 26 -> 26, of which waited for: 7 -> 7; matrix products, arithmetic and copies ran while one was open for 6% -> 5% of each run, Pallas kernels for 50% -> 53%
where the time goes in v5:
time: 216 us; the launch traced here: 215 us
  Pallas kernels  130 us (60%)
  starting transfers between devices  31 us (14%)
  waiting for transfers between devices  25.5 us (12%)
  local copies, waits for them, and re-layouts  13.8 us (6%)
  other arithmetic  10.8 us (5%)
  between operations  4.43 us (2%)
    pallas_call x2, Pallas kernels, block_grads(): pl.pallas_call(functools.partial(block_grad_kernel, mats, len(lefts), len...  45.8 us
    ppermute x19, starting transfers between devices, shift(): return lax.ppermute(x, axis, [(i, (i + by) % n) for i in range(n)])  30.6 us
    pallas_call x2, Pallas kernels, project_blocks(): pl.pallas_call(functools.partial(project_blocks_kernel, transposed, rows,...  25.8 us
    ppermute x19, waiting for transfers between devices, shift(): return lax.ppermute(x, axis, [(i, (i + by) % n) for i in range(n)])  24.3 us
    pallas_call x2, Pallas kernels, back(): pl.pallas_call(functools.partial(back_kernel, transposed, n_pieces, mats,...  22.4 us
    unnamed x72, local copies, waits for them, and re-layouts  11.1 us
    pallas_call x1, Pallas kernels, densify(): pl.pallas_call(functools.partial(densify_kernel, mats, rows, cols, panels...  10.8 us
    pallas_call x2, Pallas kernels, pointwise(): pl.pallas_call(functools.partial(kernel, len(gates)), out_shape=tuple((sh...  9.18 us
  transfers between devices with their start and end apart: 26, of which 7 were waited for; matrix products, arithmetic and copies ran while one was open for 5% of the time, Pallas kernels for 53%

profile of v5, /device:TPU:0, one launch (start us, length us, event | category | flops | bytes accessed | tf_op | source)
XLA Modules:
  0.0 215.2 jit_solution(14671629570310821748)
XLA Ops:
  0.6 3.1 %collective-permute-start = (bf16[64,2048]{1,0:T(8,128)(2,1)}, bf16[64,2048]{1,0:T(8,128)(2,1)S(1)}, u32[]{:S(2)}, u32[]{:S(2)}) collective-permute-start(bf16[64,2048]{1,0:T(8,128)(2,1)} %param.8), channel_id=1, source_target_pairs={{0,1},{1,2},{2,3},{3,0},{4,5},{5,6},{6,7},{7,4},{8,9},{9,10},{10,1... | collective-permute-start | bytes 786440 | tf_op jit(solution)/shard_map/ppermute | solution.py:553
  3.7 2.6 %collective-permute-start.1 = (bf16[64,2048]{1,0:T(8,128)(2,1)}, bf16[64,2048]{1,0:T(8,128)(2,1)S(1)}, u32[]{:S(2)}, u32[]{:S(2)}) collective-permute-start(bf16[64,2048]{1,0:T(8,128)(2,1)} %param.8), channel_id=1, source_target_pairs={{0,2},{1,3},{2,0},{3,1},{4,6},{5,7},{6,4},{7,5},{8,10},{9,11},{10,... | collective-permute-start | bytes 786440 | tf_op jit(solution)/shard_map/ppermute | solution.py:553
  6.3 1.3 collective-permute-start.2
  7.6 1.0 constant_dynamic-update-slice_fusion.3
  8.6 0.8 fusion.2
  9.4 0.8 fusion
  11.1 10.8 %shard_map.119.weight.refs_2_ = bf16[2048,3584]{1,0:T(8,128)(2,1)} custom-call(s32[448]{0:T(512)} %broadcast_subtract_fusion.2.refs_0_, bf16[336,128,128]{2,1,0:T(8,128)(2,1)} %bitcast.16), custom_call_target="tpu_custom_call" | custom-call | bytes 25 | tf_op jit(solution)/shard_map/pallas_call | solution.py:104
  22.0 1.7 collective-permute-done.1
  23.7 0.9 copy-done.1
  24.6 8.9 %shard_map.120 = (f32[128,3584]{1,0:T(8,128)}, bf16[128,3584]{1,0:T(8,128)(2,1)}) custom-call(s32[1]{0:T(128)} %bitcast.core_ref, bf16[256,2048]{1,0:T(8,128)(2,1)} %copy-done.1, bf16[2048,3584]{1,0:T(8,128)(2,1)} %shard_map.119.weight.refs_2_), custom_call_target="tpu_custom_call" | custom-call | flops 3758 | bytes 14 | tf_op jit(solution)/shard_map/pallas_call | solution.py:165
  34.2 1.5 collective-permute-start.6
  35.7 6.1 %collective-permute-start.8 = (bf16[64,2048]{1,0:T(8,128)(2,1)S(1)}, bf16[64,2048]{1,0:T(8,128)(2,1)S(1)}, u32[]{:S(2)}, u32[]{:S(2)}) collective-permute-start(bf16[64,2048]{1,0:T(8,128)(2,1)S(1)} %copy-done.23), channel_id=1, source_target_pairs={{0,1},{1,2},{2,3},{3,0},{4,5},{5,6},{6,7},{7,4},{8,9},{9,10},{10,1... | collective-permute-start | bytes 786440 | tf_op jit(solution)/shard_map/ppermute | solution.py:553
  41.7 1.6 collective-permute-start.9
  43.3 2.0 add_convert_fusion.2.refs_0_
  45.4 1.6 collective-permute-start.4
  47.0 12.8 %shard_map.121 = (f32[128,3584]{1,0:T(8,128)}, bf16[128,3584]{1,0:T(8,128)(2,1)}, bf16[2048,3584]{1,0:T(8,128)(2,1)}) custom-call(s32[1]{0:T(128)} %bitcast.core_ref, s32[448]{0:T(512)} %broadcast_subtract_fusion.1.table.refs_1_, bf16[256,2048]{1,0:T(8,128)(2,1)} %copy-done.1, bf16[336,128,128]{2,1,0:T(8,128)(2,1)} %bitcast.17, bf16[128,3584]{1,0:T(8,128)(2,1)} %copy-done.11), custom_call_target="tpu_custom_call" | custom-call | flops 3758 | bytes 29 | tf_op jit(solution)/shard_map/pallas_call | solution.py:230
  61.1 1.0 collective-permute-start.10
  62.2 7.9 %collective-permute-done.10 = bf16[64,2048]{1,0:T(8,128)(2,1)S(1)} collective-permute-done((bf16[64,2048]{1,0:T(8,128)(2,1)S(1)}, bf16[64,2048]{1,0:T(8,128)(2,1)S(1)}, u32[]{:S(2)}, u32[]{:S(2)}) %collective-permute-start.10) | collective-permute-done | bytes 262176 | tf_op jit(solution)/shard_map/ppermute | solution.py:553
  73.4 0.7 copy-done.3
  74.1 0.8 collective-permute-start.7
  75.5 12.9 %shard_map.122 = (f32[128,3584]{1,0:T(8,128)}, bf16[128,3584]{1,0:T(8,128)(2,1)}, bf16[3584,2048]{1,0:T(8,128)(2,1)}) custom-call(s32[1]{0:T(128)} %bitcast.core_ref, s32[448]{0:T(512)} %broadcast_subtract_fusion.table.refs_0_, bf16[256,2048]{1,0:T(8,128)(2,1)} %copy-done.6, bf16[336,128,128]{2,1,0:T(8,128)(2,1)} %bitcast.18, bf16[128,3584]{1,0:T(8,128)(2,1)} %copy-done.14), custom_call_target="tpu_custom_call" | custom-call | flops 3758 | bytes 29 | tf_op jit(solution)/shard_map/pallas_call | solution.py:230
  88.6 6.4 %collective-permute-done.12.refs_7_ = bf16[256,2048]{1,0:T(8,128)(2,1)S(1)} collective-permute-done((bf16[256,2048]{1,0:T(8,128)(2,1)S(1)}, bf16[256,2048]{1,0:T(8,128)(2,1)S(1)}, u32[]{:S(2)}, u32[]{:S(2)}) %collective-permute-start.12) | collective-permute-done | bytes 1048608 | tf_op jit(solution)/shard_map/ppermute | solution.py:553
  97.4 3.0 %add_convert_fusion.refs_6_ = bf16[128,3584]{1,0:T(8,128)(2,1)} fusion(f32[128,3584]{1,0:T(8,128)} %get-tuple-element.33.refs_0_, bf16[128,3584]{1,0:T(8,128)(2,1)S(1)} %collective-permute-done.11.refs_1_, f32[]{:T(128)} %bitcast.8), kind=kLoop, calls=%fused_computation | loop fusion | flops 1835008 | bytes 3670020 | tf_op jit(solution)/shard_map/convert_element_type | solution.py:319
  100.4 4.3 %shard_map.123.refs_0_.refs_2_ = bf16[1,128,3584]{2,1,0:T(8,128)(2,1)} custom-call(f32[128,3584]{1,0:T(8,128)} %get-tuple-element.28.refs_0_, bf16[128,3584]{1,0:T(8,128)(2,1)} %copy-done.2, bf16[128,3584]{1,0:T(8,128)(2,1)} %copy-done.7, f32[128,3584]{1,0:T(8,128)} %get-tuple-element.30.refs_3_, bf16[128,3584]{1,0:T(8,128)(2,1)} %copy-done.3, ...), custom_call_target="tpu_custom_call" | custom-call | bytes 13 | tf_op jit(solution)/shard_map/pallas_call | solution.py:386
  104.7 0.9 collective-permute-start.17
  105.6 1.1 collective-permute-start.19
  106.7 0.7 collective-permute-done.13.refs_1_.refs_3_
  107.4 0.9 copy-done.13
  108.3 8.3 %shard_map.124 = (f32[64,2048]{1,0:T(8,128)}, bf16[64,2048]{1,0:T(8,128)(2,1)}, bf16[64,2048]{1,0:T(8,128)(2,1)}, bf16[64,2048]{1,0:T(8,128)(2,1)}) custom-call(s32[1]{0:T(128)} %bitcast.core_ref, bf16[1,128,3584]{2,1,0:T(8,128)(2,1)} %shard_map.123.refs_0_.refs_2_, bf16[1,128,3584]{2,1,0:T(8,128)(2,1)} %copy-done.13, ...), custom_call_target="tpu_custom_call" | custom-call | flops 3758 | bytes 14 | tf_op jit(solution)/shard_map/pallas_call | solution.py:297
  116.7 4.8 %shard_map.125 = (f32[128,3584]{1,0:T(8,128)}, f32[128,3584]{1,0:T(8,128)}) custom-call(f32[128,3584]{1,0:T(8,128)} %get-tuple-element.28.refs_0_, bf16[128,3584]{1,0:T(8,128)(2,1)} %copy-done.2, bf16[128,3584]{1,0:T(8,128)(2,1)} %copy-done.7, f32[128,3584]{1,0:T(8,128)} %get-tuple-element.30.refs_3_, bf16[128,3584]{1,0:T(8,128)(2,1)} %copy-done.3, ...), custom_call_target="tpu_custom_call" | custom-call | bytes 13 | tf_op jit(solution)/shard_map/pallas_call | solution.py:386
  121.5 6.0 %collective-permute-done.17.refs_2_ = bf16[128,3584]{1,0:T(8,128)(2,1)S(1)} collective-permute-done((bf16[128,3584]{1,0:T(8,128)(2,1)S(1)}, bf16[128,3584]{1,0:T(8,128)(2,1)S(1)}, u32[]{:S(2)}, u32[]{:S(2)}) %collective-permute-start.17) | collective-permute-done | bytes 917536 | tf_op jit(solution)/shard_map/ppermute | solution.py:553
  127.5 0.9 copy-done.21
  128.4 4.3 %shard_map.126.refs_1_.refs_8_.refs_0_.refs_6_ = bf16[2,128,3584]{2,1,0:T(8,128)(2,1)} custom-call(f32[128,3584]{1,0:T(8,128)} %get-tuple-element.33.refs_0_, bf16[128,3584]{1,0:T(8,128)(2,1)} %copy-done.9, bf16[128,3584]{1,0:T(8,128)(2,1)} %copy-done.21, f32[128,3584]{1,0:T(8,128)} %get-tuple-element.40.refs_3_, f32[128,3584]{1,0:T(8,128)} %get-tuple-element.41.refs_4_), custom_call_target="tpu_custom_call" | custom-call | bytes 9 | tf_op jit(solution)/shard_map/pallas_call | solution.py:420
  132.8 1.2 collective-permute-start.24
  134.0 0.9 copy-done.12
  135.1 2.5 %collective-permute-start.14 = (bf16[64,2048]{1,0:T(8,128)(2,1)S(1)}, bf16[64,2048]{1,0:T(8,128)(2,1)S(1)}, u32[]{:S(2)}, u32[]{:S(2)}) collective-permute-start(bf16[64,2048]{1,0:T(8,128)(2,1)S(1)} %copy-done.29), channel_id=1, source_target_pairs={{0,3},{1,0},{2,1},{3,2},{4,7},{5,4},{6,5},{7,6},{8,11},{9,8},{10,9... | collective-permute-start | bytes 786440 | tf_op jit(solution)/shard_map/ppermute | solution.py:553
  138.1 1.3 collective-permute-start.16
  140.0 17.6 %shard_map.128.refs_4_ = bf16[336,128,128]{2,1,0:T(8,128)(2,1)} custom-call(s32[1]{0:T(128)} %bitcast.core_ref, s32[448]{0:T(512)} %broadcast_subtract_fusion.table.refs_0_, s32[1]{0:T(128)} %bitcast.9.refs_1_, bf16[1,128,3584]{2,1,0:T(8,128)(2,1)} %shard_map.123.refs_0_.refs_2_, bf16[1,128,3584]{2,1,0:T(8,128)(2,1)} %copy-done.13, ...), custom_call_target="tpu_custom_call" | custom-call | flops 7516 | bytes 11 | tf_op jit(solution)/shard_map/pallas_call | solution.py:523
  157.6 1.2 copy-done.5
  158.8 14.1 %shard_map.129 = (f32[64,2048]{1,0:T(8,128)}, bf16[64,2048]{1,0:T(8,128)(2,1)}, bf16[64,2048]{1,0:T(8,128)(2,1)}, bf16[64,2048]{1,0:T(8,128)(2,1)}) custom-call(s32[1]{0:T(128)} %bitcast.core_ref, bf16[2,128,3584]{2,1,0:T(8,128)(2,1)} %shard_map.126.refs_1_.refs_8_.refs_0_.refs_6_, bf16[2,128,3584]{2,1,0:T(8,128)(2,1)} %copy-done.5, ...), custom_call_target="tpu_custom_call" | custom-call | flops 7516 | bytes 29 | tf_op jit(solution)/shard_map/pallas_call | solution.py:297
  173.0 2.4 %collective-permute-done.24.refs_0_ = bf16[2,128,3584]{2,1,0:T(8,128)(2,1)S(1)} collective-permute-done((bf16[2,128,3584]{2,1,0:T(8,128)(2,1)}, bf16[2,128,3584]{2,1,0:T(8,128)(2,1)S(1)}, u32[]{:S(2)}, u32[]{:S(2)}) %collective-permute-start.24) | collective-permute-done | bytes 1835040 | tf_op jit(solution)/shard_map/ppermute | solution.py:553
  175.5 1.2 copy-done.4
  176.7 0.9 copy-done.32
  177.6 2.5 %collective-permute-start.21 = (bf16[64,2048]{1,0:T(8,128)(2,1)S(1)}, bf16[64,2048]{1,0:T(8,128)(2,1)S(1)}, u32[]{:S(2)}, u32[]{:S(2)}) collective-permute-start(bf16[64,2048]{1,0:T(8,128)(2,1)S(1)} %copy-done.32), channel_id=1, source_target_pairs={{0,3},{1,0},{2,1},{3,2},{4,7},{5,4},{6,5},{7,6},{8,11},{9,8},{10,9... | collective-permute-start | bytes 786440 | tf_op jit(solution)/shard_map/ppermute | solution.py:553
  180.2 0.8 collective-permute-start.23
  182.2 1.2 copy-done.15
  183.5 28.2 %shard_map.131 = (bf16[336,128,128]{2,1,0:T(8,128)(2,1)}, bf16[336,128,128]{2,1,0:T(8,128)(2,1)}) custom-call(s32[1]{0:T(128)} %bitcast.core_ref, s32[448]{0:T(512)} %broadcast_subtract_fusion.2.refs_0_, s32[448]{0:T(512)} %broadcast_subtract_fusion.1.table.refs_1_, s32[1]{0:T(128)} %bitcast.10.refs_2_, s32[1]{0:T(128)} %bitcast.11.refs_3_, ...), custom_call_target="tpu_custom_call" | custom-call | flops 15032 | bytes 22 | tf_op jit(solution)/shard_map/pallas_call | solution.py:523
  212.7 2.6 %shard_map.132 = (bf16[64,2048]{1,0:T(8,128)(2,1)}, bf16[64,2048]{1,0:T(8,128)(2,1)}) custom-call(f32[64,2048]{1,0:T(8,128)} %get-tuple-element.36.refs_6_.refs_0_, bf16[64,2048]{1,0:T(8,128)(2,1)} %copy-done.18, bf16[64,2048]{1,0:T(8,128)(2,1)} %copy-done.19, bf16[64,2048]{1,0:T(8,128)(2,1)} %copy-done.20, f32[64,2048]{1,0:T(8,128)} %get-tuple-element.43.refs_1_.refs_4_, ...), custom_call_target="tpu_custom_call" | custom-call | bytes 1 | tf_op jit(solution)/shard_map/pallas_call | solution.py:348
  (110 shorter events, 9.6 us)
Async XLA Ops:
  0.6 21.3 %collective-permute-start = (bf16[64,2048]{1,0:T(8,128)(2,1)}, bf16[64,2048]{1,0:T(8,128)(2,1)S(1)}, u32[]{:S(2)}, u32[]{:S(2)}) collective-permute-start(bf16[64,2048]{1,0:T(8,128)(2,1)} %param.8), channel_id=1, source_target_pairs={{0,1},{1,2},{2,3},{3,0},{4,5},{5,6},{6,7},{7,4},{8,9},{9,10},{10,1... | collective-permute-start | bytes 786440 | tf_op jit(solution)/shard_map/ppermute | solution.py:553
  3.7 19.9 %collective-permute-start.1 = (bf16[64,2048]{1,0:T(8,128)(2,1)}, bf16[64,2048]{1,0:T(8,128)(2,1)S(1)}, u32[]{:S(2)}, u32[]{:S(2)}) collective-permute-start(bf16[64,2048]{1,0:T(8,128)(2,1)} %param.8), channel_id=1, source_target_pairs={{0,2},{1,3},{2,0},{3,1},{4,6},{5,7},{6,4},{7,5},{8,10},{9,11},{10,... | collective-permute-start | bytes 786440 | tf_op jit(solution)/shard_map/ppermute | solution.py:553
  6.3 17.4 %collective-permute-start.2 = (bf16[64,2048]{1,0:T(8,128)(2,1)}, bf16[64,2048]{1,0:T(8,128)(2,1)S(1)}, u32[]{:S(2)}, u32[]{:S(2)}) collective-permute-start(bf16[64,2048]{1,0:T(8,128)(2,1)} %param.8), channel_id=1, source_target_pairs={{0,3},{1,0},{2,1},{3,2},{4,7},{5,4},{6,5},{7,6},{8,11},{9,8},{10,9... | collective-permute-start | bytes 786440 | tf_op jit(solution)/shard_map/ppermute | solution.py:553
  24.6 11.0 %copy-start.23 = (bf16[64,2048]{1,0:T(8,128)(2,1)S(1)}, bf16[64,2048]{1,0:T(8,128)(2,1)}, u32[]{:S(2)}) copy-start(bf16[64,2048]{1,0:T(8,128)(2,1)} %param.9) | copy-start | bytes 786436
  33.5 9.8 %collective-permute-start.3 = (bf16[128,3584]{1,0:T(8,128)(2,1)}, bf16[128,3584]{1,0:T(8,128)(2,1)S(1)}, u32[]{:S(2)}, u32[]{:S(2)}) collective-permute-start(bf16[128,3584]{1,0:T(8,128)(2,1)} %get-tuple-element.29), channel_id=1, source_target_pairs={{0,4},{4,0},{8,12},{12,8},{1,5},{5,1},{9,13},{13,9},{2,6},{6,2},{1... | collective-permute-start | bytes 2752520 | tf_op jit(solution)/shard_map/ppermute | solution.py:558
  34.2 36.5 %collective-permute-start.6 = (bf16[256,2048]{1,0:T(8,128)(2,1)}, bf16[256,2048]{1,0:T(8,128)(2,1)S(1)}, u32[]{:S(2)}, u32[]{:S(2)}) collective-permute-start(bf16[256,2048]{1,0:T(8,128)(2,1)} %copy-done.1), channel_id=1, source_target_pairs={{0,16},{16,0},{1,17},{17,1},{2,18},{18,2},{3,19},{19,3},{4,20},{20... | collective-permute-start | bytes 3145736 | tf_op jit(solution)/shard_map/ppermute | solution.py:553
  35.7 25.4 %collective-permute-start.8 = (bf16[64,2048]{1,0:T(8,128)(2,1)S(1)}, bf16[64,2048]{1,0:T(8,128)(2,1)S(1)}, u32[]{:S(2)}, u32[]{:S(2)}) collective-permute-start(bf16[64,2048]{1,0:T(8,128)(2,1)S(1)} %copy-done.23), channel_id=1, source_target_pairs={{0,1},{1,2},{2,3},{3,0},{4,5},{5,6},{6,7},{7,4},{8,9},{9,10},{10,1... | collective-permute-start | bytes 786440 | tf_op jit(solution)/shard_map/ppermute | solution.py:553
  41.7 20.4 %collective-permute-start.9 = (bf16[64,2048]{1,0:T(8,128)(2,1)S(1)}, bf16[64,2048]{1,0:T(8,128)(2,1)S(1)}, u32[]{:S(2)}, u32[]{:S(2)}) collective-permute-start(bf16[64,2048]{1,0:T(8,128)(2,1)S(1)} %copy-done.23), channel_id=1, source_target_pairs={{0,2},{1,3},{2,0},{3,1},{4,6},{5,7},{6,4},{7,5},{8,10},{9,11},{10,... | collective-permute-start | bytes 786440 | tf_op jit(solution)/shard_map/ppermute | solution.py:553
  43.3 2.0 copy-start.2
  45.4 1.6 copy-start.11
  45.4 26.5 %collective-permute-start.4 = (bf16[128,3584]{1,0:T(8,128)(2,1)S(1)}, bf16[128,3584]{1,0:T(8,128)(2,1)S(1)}, u32[]{:S(2)}, u32[]{:S(2)}) collective-permute-start(bf16[128,3584]{1,0:T(8,128)(2,1)S(1)} %add_convert_fusion.2.refs_0_), channel_id=1, source_target_pairs={{0,8},{4,12},{8,0},{12,4},{1,9},{5,13},{9,1},{13,5},{2,10},{6,14},... | collective-permute-start | bytes 2752520 | tf_op jit(solution)/shard_map/ppermute | solution.py:553
  59.8 13.3 %copy-start = (f32[128,3584]{1,0:T(8,128)S(1)}, f32[128,3584]{1,0:T(8,128)}, u32[]{:S(2)}) copy-start(f32[128,3584]{1,0:T(8,128)} %get-tuple-element.30.refs_3_) | copy-start | bytes 5505028
  59.8 13.3 %collective-permute-start.5 = (bf16[128,3584]{1,0:T(8,128)(2,1)}, bf16[128,3584]{1,0:T(8,128)(2,1)S(1)}, u32[]{:S(2)}, u32[]{:S(2)}) collective-permute-start(bf16[128,3584]{1,0:T(8,128)(2,1)} %get-tuple-element.31), channel_id=1, source_target_pairs={{0,4},{4,0},{8,12},{12,8},{1,5},{5,1},{9,13},{13,9},{2,6},{6,2},{1... | collective-permute-start | bytes 2752520 | tf_op jit(solution)/shard_map/ppermute | solution.py:558
  61.1 8.9 %collective-permute-start.10 = (bf16[64,2048]{1,0:T(8,128)(2,1)S(1)}, bf16[64,2048]{1,0:T(8,128)(2,1)S(1)}, u32[]{:S(2)}, u32[]{:S(2)}) collective-permute-start(bf16[64,2048]{1,0:T(8,128)(2,1)S(1)} %copy-done.23), channel_id=1, source_target_pairs={{0,3},{1,0},{2,1},{3,2},{4,7},{5,4},{6,5},{7,6},{8,11},{9,8},{10,9... | collective-permute-start | bytes 786440 | tf_op jit(solution)/shard_map/ppermute | solution.py:553
  70.1 3.3 %copy-start.6 = (bf16[256,2048]{1,0:T(8,128)(2,1)}, bf16[256,2048]{1,0:T(8,128)(2,1)S(1)}, u32[]{:S(2)}) copy-start(bf16[256,2048]{1,0:T(8,128)(2,1)S(1)} %constant_dynamic-update-slice_fusion.4.panel.refs_6_) | copy-start | bytes 3145732
  70.1 24.8 %collective-permute-start.12 = (bf16[256,2048]{1,0:T(8,128)(2,1)S(1)}, bf16[256,2048]{1,0:T(8,128)(2,1)S(1)}, u32[]{:S(2)}, u32[]{:S(2)}) collective-permute-start(bf16[256,2048]{1,0:T(8,128)(2,1)S(1)} %constant_dynamic-update-slice_fusion.4.panel.refs_6_), channel_id=1, source_target_pairs={{0,16},{16,0},{1,17},{17,1},{2,18},{18,2},{3,19},{19,3},{4,20},{20... | collective-permute-start | bytes 3145736 | tf_op jit(solution)/shard_map/ppermute | solution.py:553
  70.7 17.8 %copy-start.16 = (bf16[256,2048]{1,0:T(8,128)(2,1)}, bf16[256,2048]{1,0:T(8,128)(2,1)S(1)}, u32[]{:S(2)}) copy-start(bf16[256,2048]{1,0:T(8,128)(2,1)S(1)} %collective-permute-done.6.refs_5_) | copy-start | bytes 3145732
  71.9 1.5 copy-start.7
  74.1 1.4 copy-start.14
  74.1 22.0 %collective-permute-start.7 = (bf16[128,3584]{1,0:T(8,128)(2,1)S(1)}, bf16[128,3584]{1,0:T(8,128)(2,1)S(1)}, u32[]{:S(2)}, u32[]{:S(2)}) collective-permute-start(bf16[128,3584]{1,0:T(8,128)(2,1)S(1)} %add_convert_fusion.1.refs_0_), channel_id=1, source_target_pairs={{0,8},{4,12},{8,0},{12,4},{1,9},{5,13},{9,1},{13,5},{2,10},{6,14},... | collective-permute-start | bytes 2752520 | tf_op jit(solution)/shard_map/ppermute | solution.py:553
  88.5 8.9 %collective-permute-start.11 = (bf16[128,3584]{1,0:T(8,128)(2,1)}, bf16[128,3584]{1,0:T(8,128)(2,1)S(1)}, u32[]{:S(2)}, u32[]{:S(2)}) collective-permute-start(bf16[128,3584]{1,0:T(8,128)(2,1)} %get-tuple-element.34), channel_id=1, source_target_pairs={{0,4},{4,0},{8,12},{12,8},{1,5},{5,1},{9,13},{13,9},{2,6},{6,2},{1... | collective-permute-start | bytes 2752520 | tf_op jit(solution)/shard_map/ppermute | solution.py:558
  94.9 5.4 %copy-start.17 = (bf16[256,2048]{1,0:T(8,128)(2,1)}, bf16[256,2048]{1,0:T(8,128)(2,1)S(1)}, u32[]{:S(2)}) copy-start(bf16[256,2048]{1,0:T(8,128)(2,1)S(1)} %collective-permute-done.12.refs_7_) | copy-start | bytes 3145732
  96.1 4.2 %copy-start.8 = (bf16[128,3584]{1,0:T(8,128)(2,1)}, bf16[128,3584]{1,0:T(8,128)(2,1)S(1)}, u32[]{:S(2)}) copy-start(bf16[128,3584]{1,0:T(8,128)(2,1)S(1)} %collective-permute-done.7.refs_5_) | copy-start | bytes 2752516
  97.4 3.0 %copy-start.9 = (bf16[128,3584]{1,0:T(8,128)(2,1)}, bf16[128,3584]{1,0:T(8,128)(2,1)S(1)}, u32[]{:S(2)}) copy-start(bf16[128,3584]{1,0:T(8,128)(2,1)S(1)} %collective-permute-done.11.refs_1_) | copy-start | bytes 2752516
  100.4 4.3 %copy-start.10 = (bf16[128,3584]{1,0:T(8,128)(2,1)S(1)}, bf16[128,3584]{1,0:T(8,128)(2,1)}, u32[]{:S(2)}) copy-start(bf16[128,3584]{1,0:T(8,128)(2,1)} %add_convert_fusion.refs_6_) | copy-start | bytes 2752516
  104.7 2.7 %collective-permute-start.13 = (bf16[1,128,3584]{2,1,0:T(8,128)(2,1)}, bf16[1,128,3584]{2,1,0:T(8,128)(2,1)S(1)}, u32[]{:S(2)}, u32[]{:S(2)}) collective-permute-start(bf16[1,128,3584]{2,1,0:T(8,128)(2,1)} %shard_map.123.refs_0_.refs_2_), channel_id=1, source_target_pairs={{0,4},{4,0},{8,12},{12,8},{1,5},{5,1},{9,13},{13,9},{2,6},{6,2},{1... | collective-permute-start | bytes 2752520 | tf_op jit(solution)/shard_map/ppermute | solution.py:558
  104.7 22.8 %collective-permute-start.17 = (bf16[128,3584]{1,0:T(8,128)(2,1)S(1)}, bf16[128,3584]{1,0:T(8,128)(2,1)S(1)}, u32[]{:S(2)}, u32[]{:S(2)}) collective-permute-start(bf16[128,3584]{1,0:T(8,128)(2,1)S(1)} %copy-done.10), channel_id=1, source_target_pairs={{0,8},{4,12},{8,0},{12,4},{1,9},{5,13},{9,1},{13,5},{2,10},{6,14},... | collective-permute-start | bytes 2752520 | tf_op jit(solution)/shard_map/ppermute | solution.py:553
  105.6 28.4 %collective-permute-start.19 = (bf16[1,128,3584]{2,1,0:T(8,128)(2,1)}, bf16[1,128,3584]{2,1,0:T(8,128)(2,1)S(1)}, u32[]{:S(2)}, u32[]{:S(2)}) collective-permute-start(bf16[1,128,3584]{2,1,0:T(8,128)(2,1)} %shard_map.123.refs_0_.refs_2_), channel_id=1, source_target_pairs={{0,16},{16,0},{1,17},{17,1},{2,18},{18,2},{3,19},{19,3},{4,20},{20... | collective-permute-start | bytes 2752520 | tf_op jit(solution)/shard_map/ppermute | solution.py:553
  132.7 2.4 %copy-start.29 = (bf16[64,2048]{1,0:T(8,128)(2,1)S(1)}, bf16[64,2048]{1,0:T(8,128)(2,1)}, u32[]{:S(2)}) copy-start(bf16[64,2048]{1,0:T(8,128)(2,1)} %get-tuple-element.37) | copy-start | bytes 786436
  132.7 4.9 %copy-start.28 = (bf16[64,2048]{1,0:T(8,128)(2,1)S(1)}, bf16[64,2048]{1,0:T(8,128)(2,1)}, u32[]{:S(2)}) copy-start(bf16[64,2048]{1,0:T(8,128)(2,1)} %get-tuple-element.38) | copy-start | bytes 786436
  132.7 5.4 %copy-start.27 = (bf16[64,2048]{1,0:T(8,128)(2,1)S(1)}, bf16[64,2048]{1,0:T(8,128)(2,1)}, u32[]{:S(2)}) copy-start(bf16[64,2048]{1,0:T(8,128)(2,1)} %get-tuple-element.39) | copy-start | bytes 786436
  132.7 24.9 %collective-permute-start.18 = (bf16[2,128,3584]{2,1,0:T(8,128)(2,1)}, bf16[2,128,3584]{2,1,0:T(8,128)(2,1)S(1)}, u32[]{:S(2)}, u32[]{:S(2)}) collective-permute-start(bf16[2,128,3584]{2,1,0:T(8,128)(2,1)} %shard_map.126.refs_1_.refs_8_.refs_0_.refs_6_), channel_id=1, source_target_pairs={{0,4},{4,0},{8,12},{12,8},{1,5},{5,1},{9,13},{13,9},{2,6},{6,2},{1... | collective-permute-start | bytes 5505032 | tf_op jit(solution)/shard_map/ppermute | solution.py:558
  132.8 42.6 %collective-permute-start.24 = (bf16[2,128,3584]{2,1,0:T(8,128)(2,1)}, bf16[2,128,3584]{2,1,0:T(8,128)(2,1)S(1)}, u32[]{:S(2)}, u32[]{:S(2)}) collective-permute-start(bf16[2,128,3584]{2,1,0:T(8,128)(2,1)} %shard_map.126.refs_1_.refs_8_.refs_0_.refs_6_), channel_id=1, source_target_pairs={{0,16},{16,0},{1,17},{17,1},{2,18},{18,2},{3,19},{19,3},{4,20},{20... | collective-permute-start | bytes 5505032 | tf_op jit(solution)/shard_map/ppermute | solution.py:553
  134.9 3.2 %collective-permute-start.20 = (bf16[1,128,3584]{2,1,0:T(8,128)(2,1)}, bf16[1,128,3584]{2,1,0:T(8,128)(2,1)S(1)}, u32[]{:S(2)}, u32[]{:S(2)}) collective-permute-start(bf16[1,128,3584]{2,1,0:T(8,128)(2,1)} %shard_map.127.refs_4_), channel_id=1, source_target_pairs={{0,4},{4,0},{8,12},{12,8},{1,5},{5,1},{9,13},{13,9},{2,6},{6,2},{1... | collective-permute-start | bytes 2752520 | tf_op jit(solution)/shard_map/ppermute | solution.py:558
  135.1 37.9 %collective-permute-start.14 = (bf16[64,2048]{1,0:T(8,128)(2,1)S(1)}, bf16[64,2048]{1,0:T(8,128)(2,1)S(1)}, u32[]{:S(2)}, u32[]{:S(2)}) collective-permute-start(bf16[64,2048]{1,0:T(8,128)(2,1)S(1)} %copy-done.29), channel_id=1, source_target_pairs={{0,3},{1,0},{2,1},{3,2},{4,7},{5,4},{6,5},{7,6},{8,11},{9,8},{10,9... | collective-permute-start | bytes 786440 | tf_op jit(solution)/shard_map/ppermute | solution.py:553
  137.6 35.3 %collective-permute-start.15 = (bf16[64,2048]{1,0:T(8,128)(2,1)S(1)}, bf16[64,2048]{1,0:T(8,128)(2,1)S(1)}, u32[]{:S(2)}, u32[]{:S(2)}) collective-permute-start(bf16[64,2048]{1,0:T(8,128)(2,1)S(1)} %copy-done.28), channel_id=1, source_target_pairs={{0,1},{1,2},{2,3},{3,0},{4,5},{5,6},{6,7},{7,4},{8,9},{9,10},{10,1... | collective-permute-start | bytes 786440 | tf_op jit(solution)/shard_map/ppermute | solution.py:553
  138.1 1.9 copy-start.22
  138.1 34.9 %collective-permute-start.16 = (bf16[64,2048]{1,0:T(8,128)(2,1)S(1)}, bf16[64,2048]{1,0:T(8,128)(2,1)S(1)}, u32[]{:S(2)}, u32[]{:S(2)}) collective-permute-start(bf16[64,2048]{1,0:T(8,128)(2,1)S(1)} %copy-done.27), channel_id=1, source_target_pairs={{0,2},{1,3},{2,0},{3,1},{4,6},{5,7},{6,4},{7,5},{8,10},{9,11},{10,... | collective-permute-start | bytes 786440 | tf_op jit(solution)/shard_map/ppermute | solution.py:553
  173.0 2.5 %copy-start.18 = (bf16[64,2048]{1,0:T(8,128)(2,1)}, bf16[64,2048]{1,0:T(8,128)(2,1)S(1)}, u32[]{:S(2)}) copy-start(bf16[64,2048]{1,0:T(8,128)(2,1)S(1)} %collective-permute-done.14.refs_2_.refs_1_) | copy-start | bytes 786436
  173.0 2.5 %copy-start.19 = (bf16[64,2048]{1,0:T(8,128)(2,1)}, bf16[64,2048]{1,0:T(8,128)(2,1)S(1)}, u32[]{:S(2)}) copy-start(bf16[64,2048]{1,0:T(8,128)(2,1)S(1)} %collective-permute-done.15.refs_3_.refs_2_) | copy-start | bytes 786436
  173.0 2.5 %copy-start.20 = (bf16[64,2048]{1,0:T(8,128)(2,1)}, bf16[64,2048]{1,0:T(8,128)(2,1)S(1)}, u32[]{:S(2)}) copy-start(bf16[64,2048]{1,0:T(8,128)(2,1)S(1)} %collective-permute-done.16.refs_4_.refs_3_) | copy-start | bytes 786436
  176.7 3.5 %copy-start.31 = (bf16[64,2048]{1,0:T(8,128)(2,1)S(1)}, bf16[64,2048]{1,0:T(8,128)(2,1)}, u32[]{:S(2)}) copy-start(bf16[64,2048]{1,0:T(8,128)(2,1)} %get-tuple-element.45) | copy-start | bytes 786436
  176.7 3.5 %copy-start.30 = (bf16[64,2048]{1,0:T(8,128)(2,1)S(1)}, bf16[64,2048]{1,0:T(8,128)(2,1)}, u32[]{:S(2)}) copy-start(bf16[64,2048]{1,0:T(8,128)(2,1)} %get-tuple-element.46) | copy-start | bytes 786436
  176.7 5.5 %collective-permute-start.25 = (bf16[2,128,3584]{2,1,0:T(8,128)(2,1)}, bf16[2,128,3584]{2,1,0:T(8,128)(2,1)S(1)}, u32[]{:S(2)}, u32[]{:S(2)}) collective-permute-start(bf16[2,128,3584]{2,1,0:T(8,128)(2,1)} %shard_map.130.refs_8_), channel_id=1, source_target_pairs={{0,4},{4,0},{8,12},{12,8},{1,5},{5,1},{9,13},{13,9},{2,6},{6,2},{1... | collective-permute-start | bytes 5505032 | tf_op jit(solution)/shard_map/ppermute | solution.py:558
  177.6 34.1 %collective-permute-start.21 = (bf16[64,2048]{1,0:T(8,128)(2,1)S(1)}, bf16[64,2048]{1,0:T(8,128)(2,1)S(1)}, u32[]{:S(2)}, u32[]{:S(2)}) collective-permute-start(bf16[64,2048]{1,0:T(8,128)(2,1)S(1)} %copy-done.32), channel_id=1, source_target_pairs={{0,3},{1,0},{2,1},{3,2},{4,7},{5,4},{6,5},{7,6},{8,11},{9,8},{10,9... | collective-permute-start | bytes 786440 | tf_op jit(solution)/shard_map/ppermute | solution.py:553
  180.2 31.6 %collective-permute-start.22 = (bf16[64,2048]{1,0:T(8,128)(2,1)S(1)}, bf16[64,2048]{1,0:T(8,128)(2,1)S(1)}, u32[]{:S(2)}, u32[]{:S(2)}) collective-permute-start(bf16[64,2048]{1,0:T(8,128)(2,1)S(1)} %copy-done.31), channel_id=1, source_target_pairs={{0,1},{1,2},{2,3},{3,0},{4,5},{5,6},{6,7},{7,4},{8,9},{9,10},{10,1... | collective-permute-start | bytes 786440 | tf_op jit(solution)/shard_map/ppermute | solution.py:553
  180.2 31.6 %collective-permute-start.23 = (bf16[64,2048]{1,0:T(8,128)(2,1)S(1)}, bf16[64,2048]{1,0:T(8,128)(2,1)S(1)}, u32[]{:S(2)}, u32[]{:S(2)}) collective-permute-start(bf16[64,2048]{1,0:T(8,128)(2,1)S(1)} %copy-done.30), channel_id=1, source_target_pairs={{0,2},{1,3},{2,0},{3,1},{4,6},{5,7},{6,4},{7,5},{8,10},{9,11},{10,... | collective-permute-start | bytes 786440 | tf_op jit(solution)/shard_map/ppermute | solution.py:553
  182.2 1.3 copy-start.15
  (11 other events, 10.4 us)

commit v6 on v5

--- a/solution.py
+++ b/solution.py
@@ -462,7 +462,7 @@
 
     left_loads = loads(rows_of(lefts, 0), left, left_sem)
     right_loads = [loads(rows_of(rights, m), right.at[m], in_sem.at[m]) for m in range(mats)]
-    for load in left_loads:
+    for load in left_loads + right_loads[0]:
         load.start()
 
     def clear(slot, carry, m):
@@ -473,8 +473,6 @@
         lax.fori_loop(counts[m][0], slots, functools.partial(clear, m=m), 0)
     for load in left_loads:
         load.wait()
-    for load in right_loads[0]:
-        load.start()
     for a in range(length // tall):
         span = slice(a * tall, (a + 1) * tall)
         turned[span, :] = left[:, span].T
@@ -667,7 +665,8 @@
     )
     in_cut = back(core, grad_pieces, [w_gate, w_up], n_col, True, down_grad)
     out_kept = scatter(out_cut)
-    grads_far = [hold(far, in_cut[0], *out_kept[1:]) for far in grads_far]
+    (output,) = sum_chunks([out_kept], in_cut[0])
+    grads_far = [hold(far, output) for far in grads_far]
     gate_grad, up_grad = block_grads(
         core,
         (gate_table, up_table),
@@ -677,7 +676,7 @@
         slots,
         scale,
     )
-    output, input_grad = sum_chunks([out_kept, scatter(in_cut)], gate_grad)
+    (input_grad,) = sum_chunks([scatter(in_cut)], gate_grad)
     shape = gate_blocks.shape
     return (
         output,

time: 216 us -> 215 us (level)
  waiting for transfers between devices: 25.5 us -> 23.1 us
    ppermute x19, waiting for transfers between devices: 24.3 us -> 21.9 us  [shift(): return lax.ppermute(x, axis, [(i, (i + by) % n) for i in range(n)])]
  transfers between devices with their start and end apart: 26 -> 26, of which waited for: 7 -> 6; matrix products, arithmetic and copies ran while one was open for 5% -> 5% of each run, Pallas kernels for 53% -> 54%
where the time goes in v6:
time: 215 us; the launch traced here: 214 us
  Pallas kernels  130 us (60%)
  starting transfers between devices  31.9 us (15%)
  waiting for transfers between devices  23.1 us (11%)
  local copies, waits for them, and re-layouts  13.7 us (6%)
  other arithmetic  10.8 us (5%)
  between operations  4.43 us (2%)
    pallas_call x2, Pallas kernels, block_grads(): pl.pallas_call(functools.partial(block_grad_kernel, mats, len(lefts), len...  44.6 us
    ppermute x19, starting transfers between devices, shift(): return lax.ppermute(x, axis, [(i, (i + by) % n) for i in range(n)])  31.4 us
    pallas_call x2, Pallas kernels, project_blocks(): pl.pallas_call(functools.partial(project_blocks_kernel, transposed, rows,...  25.6 us
    pallas_call x2, Pallas kernels, back(): pl.pallas_call(functools.partial(back_kernel, transposed, n_pieces, mats,...  22.5 us
    ppermute x19, waiting for transfers between devices, shift(): return lax.ppermute(x, axis, [(i, (i + by) % n) for i in range(n)])  21.9 us
    unnamed x72, local copies, waits for them, and re-layouts  10.9 us
    pallas_call x1, Pallas kernels, densify(): pl.pallas_call(functools.partial(densify_kernel, mats, rows, cols, panels...  10.8 us
    pallas_call x2, Pallas kernels, pointwise(): pl.pallas_call(functools.partial(kernel, len(gates)), out_shape=tuple((sh...  9.21 us
  transfers between devices with their start and end apart: 26, of which 6 were waited for; matrix products, arithmetic and copies ran while one was open for 5% of the time, Pallas kernels for 54%

profile of v6, /device:TPU:0, one launch (start us, length us, event | category | flops | bytes accessed | tf_op | source)
XLA Modules:
  0.0 213.9 jit_solution(3629985437915883265)
XLA Ops:
  0.6 3.1 %collective-permute-start = (bf16[64,2048]{1,0:T(8,128)(2,1)}, bf16[64,2048]{1,0:T(8,128)(2,1)S(1)}, u32[]{:S(2)}, u32[]{:S(2)}) collective-permute-start(bf16[64,2048]{1,0:T(8,128)(2,1)} %param.8), channel_id=1, source_target_pairs={{0,1},{1,2},{2,3},{3,0},{4,5},{5,6},{6,7},{7,4},{8,9},{9,10},{10,1... | collective-permute-start | bytes 786440 | tf_op jit(solution)/shard_map/ppermute | solution.py:551
  3.7 2.6 %collective-permute-start.1 = (bf16[64,2048]{1,0:T(8,128)(2,1)}, bf16[64,2048]{1,0:T(8,128)(2,1)S(1)}, u32[]{:S(2)}, u32[]{:S(2)}) collective-permute-start(bf16[64,2048]{1,0:T(8,128)(2,1)} %param.8), channel_id=1, source_target_pairs={{0,2},{1,3},{2,0},{3,1},{4,6},{5,7},{6,4},{7,5},{8,10},{9,11},{10,... | collective-permute-start | bytes 786440 | tf_op jit(solution)/shard_map/ppermute | solution.py:551
  6.3 1.3 collective-permute-start.2
  7.6 1.0 constant_dynamic-update-slice_fusion.3
  8.6 0.8 fusion.2
  9.4 0.8 fusion
  11.1 10.8 %shard_map.119.weight.refs_2_ = bf16[2048,3584]{1,0:T(8,128)(2,1)} custom-call(s32[448]{0:T(512)} %broadcast_subtract_fusion.2.refs_0_, bf16[336,128,128]{2,1,0:T(8,128)(2,1)} %bitcast.16), custom_call_target="tpu_custom_call" | custom-call | bytes 25 | tf_op jit(solution)/shard_map/pallas_call | solution.py:104
  22.0 1.6 collective-permute-done.1
  23.7 1.0 copy-done.1
  24.6 8.9 %shard_map.120 = (f32[128,3584]{1,0:T(8,128)}, bf16[128,3584]{1,0:T(8,128)(2,1)}) custom-call(s32[1]{0:T(128)} %bitcast.core_ref, bf16[256,2048]{1,0:T(8,128)(2,1)} %copy-done.1, bf16[2048,3584]{1,0:T(8,128)(2,1)} %shard_map.119.weight.refs_2_), custom_call_target="tpu_custom_call" | custom-call | flops 3758 | bytes 14 | tf_op jit(solution)/shard_map/pallas_call | solution.py:165
  34.2 1.5 collective-permute-start.6
  35.7 6.1 %collective-permute-start.8 = (bf16[64,2048]{1,0:T(8,128)(2,1)S(1)}, bf16[64,2048]{1,0:T(8,128)(2,1)S(1)}, u32[]{:S(2)}, u32[]{:S(2)}) collective-permute-start(bf16[64,2048]{1,0:T(8,128)(2,1)S(1)} %copy-done.23), channel_id=1, source_target_pairs={{0,1},{1,2},{2,3},{3,0},{4,5},{5,6},{6,7},{7,4},{8,9},{9,10},{10,1... | collective-permute-start | bytes 786440 | tf_op jit(solution)/shard_map/ppermute | solution.py:551
  41.7 1.6 collective-permute-start.9
  43.4 2.0 add_convert_fusion.2.refs_0_
  45.4 1.6 collective-permute-start.4
  47.0 12.7 %shard_map.121 = (f32[128,3584]{1,0:T(8,128)}, bf16[128,3584]{1,0:T(8,128)(2,1)}, bf16[2048,3584]{1,0:T(8,128)(2,1)}) custom-call(s32[1]{0:T(128)} %bitcast.core_ref, s32[448]{0:T(512)} %broadcast_subtract_fusion.1.table.refs_1_, bf16[256,2048]{1,0:T(8,128)(2,1)} %copy-done.1, bf16[336,128,128]{2,1,0:T(8,128)(2,1)} %bitcast.18, bf16[128,3584]{1,0:T(8,128)(2,1)} %copy-done.11), custom_call_target="tpu_custom_call" | custom-call | flops 3758 | bytes 29 | tf_op jit(solution)/shard_map/pallas_call | solution.py:230
  61.0 1.0 collective-permute-start.10
  62.1 7.9 %collective-permute-done.10 = bf16[64,2048]{1,0:T(8,128)(2,1)S(1)} collective-permute-done((bf16[64,2048]{1,0:T(8,128)(2,1)S(1)}, bf16[64,2048]{1,0:T(8,128)(2,1)S(1)}, u32[]{:S(2)}, u32[]{:S(2)}) %collective-permute-start.10) | collective-permute-done | bytes 262176 | tf_op jit(solution)/shard_map/ppermute | solution.py:551
  73.3 0.7 copy-done.3
  74.0 0.8 collective-permute-start.7
  75.4 12.9 %shard_map.122 = (f32[128,3584]{1,0:T(8,128)}, bf16[128,3584]{1,0:T(8,128)(2,1)}, bf16[3584,2048]{1,0:T(8,128)(2,1)}) custom-call(s32[1]{0:T(128)} %bitcast.core_ref, s32[448]{0:T(512)} %broadcast_subtract_fusion.table.refs_0_, bf16[256,2048]{1,0:T(8,128)(2,1)} %copy-done.6, bf16[336,128,128]{2,1,0:T(8,128)(2,1)} %bitcast.19, bf16[128,3584]{1,0:T(8,128)(2,1)} %copy-done.14), custom_call_target="tpu_custom_call" | custom-call | flops 3758 | bytes 29 | tf_op jit(solution)/shard_map/pallas_call | solution.py:230
  88.4 6.4 %collective-permute-done.12.refs_7_ = bf16[256,2048]{1,0:T(8,128)(2,1)S(1)} collective-permute-done((bf16[256,2048]{1,0:T(8,128)(2,1)S(1)}, bf16[256,2048]{1,0:T(8,128)(2,1)S(1)}, u32[]{:S(2)}, u32[]{:S(2)}) %collective-permute-start.12) | collective-permute-done | bytes 1048608 | tf_op jit(solution)/shard_map/ppermute | solution.py:551
  97.3 3.0 %add_convert_fusion.refs_6_ = bf16[128,3584]{1,0:T(8,128)(2,1)} fusion(f32[128,3584]{1,0:T(8,128)} %get-tuple-element.31.refs_0_, bf16[128,3584]{1,0:T(8,128)(2,1)S(1)} %collective-permute-done.11.refs_1_, f32[]{:T(128)} %bitcast.8), kind=kLoop, calls=%fused_computation | loop fusion | flops 1835008 | bytes 3670020 | tf_op jit(solution)/shard_map/convert_element_type | solution.py:319
  100.3 4.3 %shard_map.123.refs_0_.refs_2_ = bf16[1,128,3584]{2,1,0:T(8,128)(2,1)} custom-call(f32[128,3584]{1,0:T(8,128)} %get-tuple-element.26.refs_0_, bf16[128,3584]{1,0:T(8,128)(2,1)} %copy-done.2, bf16[128,3584]{1,0:T(8,128)(2,1)} %copy-done.7, f32[128,3584]{1,0:T(8,128)} %get-tuple-element.28.refs_3_, bf16[128,3584]{1,0:T(8,128)(2,1)} %copy-done.3, ...), custom_call_target="tpu_custom_call" | custom-call | bytes 13 | tf_op jit(solution)/shard_map/pallas_call | solution.py:386
  104.6 0.9 collective-permute-start.17
  105.5 1.1 collective-permute-start.19
  106.6 0.7 collective-permute-done.13.refs_1_.refs_3_
  107.3 0.9 copy-done.13
  108.2 8.3 %shard_map.124 = (f32[64,2048]{1,0:T(8,128)}, bf16[64,2048]{1,0:T(8,128)(2,1)}, bf16[64,2048]{1,0:T(8,128)(2,1)}, bf16[64,2048]{1,0:T(8,128)(2,1)}) custom-call(s32[1]{0:T(128)} %bitcast.core_ref, bf16[1,128,3584]{2,1,0:T(8,128)(2,1)} %shard_map.123.refs_0_.refs_2_, bf16[1,128,3584]{2,1,0:T(8,128)(2,1)} %copy-done.13, ...), custom_call_target="tpu_custom_call" | custom-call | flops 3758 | bytes 14 | tf_op jit(solution)/shard_map/pallas_call | solution.py:297
  116.6 4.9 %shard_map.125 = (f32[128,3584]{1,0:T(8,128)}, f32[128,3584]{1,0:T(8,128)}) custom-call(f32[128,3584]{1,0:T(8,128)} %get-tuple-element.26.refs_0_, bf16[128,3584]{1,0:T(8,128)(2,1)} %copy-done.2, bf16[128,3584]{1,0:T(8,128)(2,1)} %copy-done.7, f32[128,3584]{1,0:T(8,128)} %get-tuple-element.28.refs_3_, bf16[128,3584]{1,0:T(8,128)(2,1)} %copy-done.3, ...), custom_call_target="tpu_custom_call" | custom-call | bytes 13 | tf_op jit(solution)/shard_map/pallas_call | solution.py:386
  121.4 5.9 %collective-permute-done.17.refs_2_ = bf16[128,3584]{1,0:T(8,128)(2,1)S(1)} collective-permute-done((bf16[128,3584]{1,0:T(8,128)(2,1)S(1)}, bf16[128,3584]{1,0:T(8,128)(2,1)S(1)}, u32[]{:S(2)}, u32[]{:S(2)}) %collective-permute-start.17) | collective-permute-done | bytes 917536 | tf_op jit(solution)/shard_map/ppermute | solution.py:551
  127.4 0.9 copy-done.18
  128.3 4.3 %shard_map.126.refs_1_.refs_8_.refs_0_.refs_6_ = bf16[2,128,3584]{2,1,0:T(8,128)(2,1)} custom-call(f32[128,3584]{1,0:T(8,128)} %get-tuple-element.31.refs_0_, bf16[128,3584]{1,0:T(8,128)(2,1)} %copy-done.9, bf16[128,3584]{1,0:T(8,128)(2,1)} %copy-done.18, f32[128,3584]{1,0:T(8,128)} %get-tuple-element.38.refs_3_, f32[128,3584]{1,0:T(8,128)} %get-tuple-element.39.refs_4_), custom_call_target="tpu_custom_call" | custom-call | bytes 9 | tf_op jit(solution)/shard_map/pallas_call | solution.py:420
  132.7 1.2 collective-permute-start.24
  133.9 0.9 copy-done.12
  135.0 2.5 %collective-permute-start.14 = (bf16[64,2048]{1,0:T(8,128)(2,1)S(1)}, bf16[64,2048]{1,0:T(8,128)(2,1)S(1)}, u32[]{:S(2)}, u32[]{:S(2)}) collective-permute-start(bf16[64,2048]{1,0:T(8,128)(2,1)S(1)} %copy-done.29), channel_id=1, source_target_pairs={{0,3},{1,0},{2,1},{3,2},{4,7},{5,4},{6,5},{7,6},{8,11},{9,8},{10,9... | collective-permute-start | bytes 786440 | tf_op jit(solution)/shard_map/ppermute | solution.py:551
  138.0 1.3 collective-permute-start.16
  140.0 17.5 %shard_map.128.refs_4_ = bf16[336,128,128]{2,1,0:T(8,128)(2,1)} custom-call(s32[1]{0:T(128)} %bitcast.core_ref, s32[448]{0:T(512)} %broadcast_subtract_fusion.table.refs_0_, s32[1]{0:T(128)} %bitcast.9.refs_1_, bf16[1,128,3584]{2,1,0:T(8,128)(2,1)} %shard_map.123.refs_0_.refs_2_, bf16[1,128,3584]{2,1,0:T(8,128)(2,1)} %copy-done.13, ...), custom_call_target="tpu_custom_call" | custom-call | flops 7516 | bytes 11 | tf_op jit(solution)/shard_map/pallas_call | solution.py:521
  157.5 1.2 copy-done.5
  158.7 14.1 %shard_map.129 = (f32[64,2048]{1,0:T(8,128)}, bf16[64,2048]{1,0:T(8,128)(2,1)}, bf16[64,2048]{1,0:T(8,128)(2,1)}, bf16[64,2048]{1,0:T(8,128)(2,1)}) custom-call(s32[1]{0:T(128)} %bitcast.core_ref, bf16[2,128,3584]{2,1,0:T(8,128)(2,1)} %shard_map.126.refs_1_.refs_8_.refs_0_.refs_6_, bf16[2,128,3584]{2,1,0:T(8,128)(2,1)} %copy-done.5, ...), custom_call_target="tpu_custom_call" | custom-call | flops 7516 | bytes 29 | tf_op jit(solution)/shard_map/pallas_call | solution.py:297
  173.7 2.1 shard_map.130.refs_1_
  175.8 1.2 copy-done.4
  177.1 2.3 %collective-permute-start.21 = (bf16[64,2048]{1,0:T(8,128)(2,1)S(1)}, bf16[64,2048]{1,0:T(8,128)(2,1)S(1)}, u32[]{:S(2)}, u32[]{:S(2)}) collective-permute-start(bf16[64,2048]{1,0:T(8,128)(2,1)S(1)} %copy-done.32), channel_id=1, source_target_pairs={{0,3},{1,0},{2,1},{3,2},{4,7},{5,4},{6,5},{7,6},{8,11},{9,8},{10,9... | collective-permute-start | bytes 786440 | tf_op jit(solution)/shard_map/ppermute | solution.py:551
  179.8 1.5 collective-permute-start.23
  181.9 0.7 convert_reduce_fusion
  182.6 1.3 copy-done.15
  183.8 27.1 %shard_map.132 = (bf16[336,128,128]{2,1,0:T(8,128)(2,1)}, bf16[336,128,128]{2,1,0:T(8,128)(2,1)}) custom-call(s32[1]{0:T(128)} %bitcast.core_ref, s32[448]{0:T(512)} %broadcast_subtract_fusion.2.refs_0_, s32[448]{0:T(512)} %broadcast_subtract_fusion.1.table.refs_1_, s32[1]{0:T(128)} %bitcast.10.refs_2_, s32[1]{0:T(128)} %bitcast.11.refs_3_, ...), custom_call_target="tpu_custom_call" | custom-call | flops 15032 | bytes 22 | tf_op jit(solution)/shard_map/pallas_call | solution.py:521
  211.8 2.1 shard_map.133
  (111 shorter events, 10.2 us)
Async XLA Ops:
  0.6 21.3 %collective-permute-start = (bf16[64,2048]{1,0:T(8,128)(2,1)}, bf16[64,2048]{1,0:T(8,128)(2,1)S(1)}, u32[]{:S(2)}, u32[]{:S(2)}) collective-permute-start(bf16[64,2048]{1,0:T(8,128)(2,1)} %param.8), channel_id=1, source_target_pairs={{0,1},{1,2},{2,3},{3,0},{4,5},{5,6},{6,7},{7,4},{8,9},{9,10},{10,1... | collective-permute-start | bytes 786440 | tf_op jit(solution)/shard_map/ppermute | solution.py:551
  3.7 19.9 %collective-permute-start.1 = (bf16[64,2048]{1,0:T(8,128)(2,1)}, bf16[64,2048]{1,0:T(8,128)(2,1)S(1)}, u32[]{:S(2)}, u32[]{:S(2)}) collective-permute-start(bf16[64,2048]{1,0:T(8,128)(2,1)} %param.8), channel_id=1, source_target_pairs={{0,2},{1,3},{2,0},{3,1},{4,6},{5,7},{6,4},{7,5},{8,10},{9,11},{10,... | collective-permute-start | bytes 786440 | tf_op jit(solution)/shard_map/ppermute | solution.py:551
  6.3 17.4 %collective-permute-start.2 = (bf16[64,2048]{1,0:T(8,128)(2,1)}, bf16[64,2048]{1,0:T(8,128)(2,1)S(1)}, u32[]{:S(2)}, u32[]{:S(2)}) collective-permute-start(bf16[64,2048]{1,0:T(8,128)(2,1)} %param.8), channel_id=1, source_target_pairs={{0,3},{1,0},{2,1},{3,2},{4,7},{5,4},{6,5},{7,6},{8,11},{9,8},{10,9... | collective-permute-start | bytes 786440 | tf_op jit(solution)/shard_map/ppermute | solution.py:551
  24.6 11.0 %copy-start.23 = (bf16[64,2048]{1,0:T(8,128)(2,1)S(1)}, bf16[64,2048]{1,0:T(8,128)(2,1)}, u32[]{:S(2)}) copy-start(bf16[64,2048]{1,0:T(8,128)(2,1)} %param.9) | copy-start | bytes 786436
  33.5 9.8 %collective-permute-start.3 = (bf16[128,3584]{1,0:T(8,128)(2,1)}, bf16[128,3584]{1,0:T(8,128)(2,1)S(1)}, u32[]{:S(2)}, u32[]{:S(2)}) collective-permute-start(bf16[128,3584]{1,0:T(8,128)(2,1)} %get-tuple-element.27), channel_id=1, source_target_pairs={{0,4},{4,0},{8,12},{12,8},{1,5},{5,1},{9,13},{13,9},{2,6},{6,2},{1... | collective-permute-start | bytes 2752520 | tf_op jit(solution)/shard_map/ppermute | solution.py:556
  34.2 36.4 %collective-permute-start.6 = (bf16[256,2048]{1,0:T(8,128)(2,1)}, bf16[256,2048]{1,0:T(8,128)(2,1)S(1)}, u32[]{:S(2)}, u32[]{:S(2)}) collective-permute-start(bf16[256,2048]{1,0:T(8,128)(2,1)} %copy-done.1), channel_id=1, source_target_pairs={{0,16},{16,0},{1,17},{17,1},{2,18},{18,2},{3,19},{19,3},{4,20},{20... | collective-permute-start | bytes 3145736 | tf_op jit(solution)/shard_map/ppermute | solution.py:551
  35.7 25.3 %collective-permute-start.8 = (bf16[64,2048]{1,0:T(8,128)(2,1)S(1)}, bf16[64,2048]{1,0:T(8,128)(2,1)S(1)}, u32[]{:S(2)}, u32[]{:S(2)}) collective-permute-start(bf16[64,2048]{1,0:T(8,128)(2,1)S(1)} %copy-done.23), channel_id=1, source_target_pairs={{0,1},{1,2},{2,3},{3,0},{4,5},{5,6},{6,7},{7,4},{8,9},{9,10},{10,1... | collective-permute-start | bytes 786440 | tf_op jit(solution)/shard_map/ppermute | solution.py:551
  41.7 20.3 %collective-permute-start.9 = (bf16[64,2048]{1,0:T(8,128)(2,1)S(1)}, bf16[64,2048]{1,0:T(8,128)(2,1)S(1)}, u32[]{:S(2)}, u32[]{:S(2)}) collective-permute-start(bf16[64,2048]{1,0:T(8,128)(2,1)S(1)} %copy-done.23), channel_id=1, source_target_pairs={{0,2},{1,3},{2,0},{3,1},{4,6},{5,7},{6,4},{7,5},{8,10},{9,11},{10,... | collective-permute-start | bytes 786440 | tf_op jit(solution)/shard_map/ppermute | solution.py:551
  43.4 2.0 copy-start.2
  45.4 1.6 copy-start.11
  45.4 26.4 %collective-permute-start.4 = (bf16[128,3584]{1,0:T(8,128)(2,1)S(1)}, bf16[128,3584]{1,0:T(8,128)(2,1)S(1)}, u32[]{:S(2)}, u32[]{:S(2)}) collective-permute-start(bf16[128,3584]{1,0:T(8,128)(2,1)S(1)} %add_convert_fusion.2.refs_0_), channel_id=1, source_target_pairs={{0,8},{4,12},{8,0},{12,4},{1,9},{5,13},{9,1},{13,5},{2,10},{6,14},... | collective-permute-start | bytes 2752520 | tf_op jit(solution)/shard_map/ppermute | solution.py:551
  59.7 13.3 %copy-start = (f32[128,3584]{1,0:T(8,128)S(1)}, f32[128,3584]{1,0:T(8,128)}, u32[]{:S(2)}) copy-start(f32[128,3584]{1,0:T(8,128)} %get-tuple-element.28.refs_3_) | copy-start | bytes 5505028
  59.7 13.3 %collective-permute-start.5 = (bf16[128,3584]{1,0:T(8,128)(2,1)}, bf16[128,3584]{1,0:T(8,128)(2,1)S(1)}, u32[]{:S(2)}, u32[]{:S(2)}) collective-permute-start(bf16[128,3584]{1,0:T(8,128)(2,1)} %get-tuple-element.29), channel_id=1, source_target_pairs={{0,4},{4,0},{8,12},{12,8},{1,5},{5,1},{9,13},{13,9},{2,6},{6,2},{1... | collective-permute-start | bytes 2752520 | tf_op jit(solution)/shard_map/ppermute | solution.py:556
  61.0 8.9 %collective-permute-start.10 = (bf16[64,2048]{1,0:T(8,128)(2,1)S(1)}, bf16[64,2048]{1,0:T(8,128)(2,1)S(1)}, u32[]{:S(2)}, u32[]{:S(2)}) collective-permute-start(bf16[64,2048]{1,0:T(8,128)(2,1)S(1)} %copy-done.23), channel_id=1, source_target_pairs={{0,3},{1,0},{2,1},{3,2},{4,7},{5,4},{6,5},{7,6},{8,11},{9,8},{10,9... | collective-permute-start | bytes 786440 | tf_op jit(solution)/shard_map/ppermute | solution.py:551
  70.0 3.3 %copy-start.6 = (bf16[256,2048]{1,0:T(8,128)(2,1)}, bf16[256,2048]{1,0:T(8,128)(2,1)S(1)}, u32[]{:S(2)}) copy-start(bf16[256,2048]{1,0:T(8,128)(2,1)S(1)} %constant_dynamic-update-slice_fusion.4.panel.refs_6_) | copy-start | bytes 3145732
  70.0 24.8 %collective-permute-start.12 = (bf16[256,2048]{1,0:T(8,128)(2,1)S(1)}, bf16[256,2048]{1,0:T(8,128)(2,1)S(1)}, u32[]{:S(2)}, u32[]{:S(2)}) collective-permute-start(bf16[256,2048]{1,0:T(8,128)(2,1)S(1)} %constant_dynamic-update-slice_fusion.4.panel.refs_6_), channel_id=1, source_target_pairs={{0,16},{16,0},{1,17},{17,1},{2,18},{18,2},{3,19},{19,3},{4,20},{20... | collective-permute-start | bytes 3145736 | tf_op jit(solution)/shard_map/ppermute | solution.py:551
  70.6 17.7 %copy-start.16 = (bf16[256,2048]{1,0:T(8,128)(2,1)}, bf16[256,2048]{1,0:T(8,128)(2,1)S(1)}, u32[]{:S(2)}) copy-start(bf16[256,2048]{1,0:T(8,128)(2,1)S(1)} %collective-permute-done.6.refs_5_) | copy-start | bytes 3145732
  71.8 1.5 copy-start.7
  74.0 1.4 copy-start.14
  74.0 22.0 %collective-permute-start.7 = (bf16[128,3584]{1,0:T(8,128)(2,1)S(1)}, bf16[128,3584]{1,0:T(8,128)(2,1)S(1)}, u32[]{:S(2)}, u32[]{:S(2)}) collective-permute-start(bf16[128,3584]{1,0:T(8,128)(2,1)S(1)} %add_convert_fusion.1.refs_0_), channel_id=1, source_target_pairs={{0,8},{4,12},{8,0},{12,4},{1,9},{5,13},{9,1},{13,5},{2,10},{6,14},... | collective-permute-start | bytes 2752520 | tf_op jit(solution)/shard_map/ppermute | solution.py:551
  88.3 8.9 %collective-permute-start.11 = (bf16[128,3584]{1,0:T(8,128)(2,1)}, bf16[128,3584]{1,0:T(8,128)(2,1)S(1)}, u32[]{:S(2)}, u32[]{:S(2)}) collective-permute-start(bf16[128,3584]{1,0:T(8,128)(2,1)} %get-tuple-element.32), channel_id=1, source_target_pairs={{0,4},{4,0},{8,12},{12,8},{1,5},{5,1},{9,13},{13,9},{2,6},{6,2},{1... | collective-permute-start | bytes 2752520 | tf_op jit(solution)/shard_map/ppermute | solution.py:556
  94.8 5.4 %copy-start.17 = (bf16[256,2048]{1,0:T(8,128)(2,1)}, bf16[256,2048]{1,0:T(8,128)(2,1)S(1)}, u32[]{:S(2)}) copy-start(bf16[256,2048]{1,0:T(8,128)(2,1)S(1)} %collective-permute-done.12.refs_7_) | copy-start | bytes 3145732
  96.0 4.2 %copy-start.8 = (bf16[128,3584]{1,0:T(8,128)(2,1)}, bf16[128,3584]{1,0:T(8,128)(2,1)S(1)}, u32[]{:S(2)}) copy-start(bf16[128,3584]{1,0:T(8,128)(2,1)S(1)} %collective-permute-done.7.refs_5_) | copy-start | bytes 2752516
  97.3 3.0 %copy-start.9 = (bf16[128,3584]{1,0:T(8,128)(2,1)}, bf16[128,3584]{1,0:T(8,128)(2,1)S(1)}, u32[]{:S(2)}) copy-start(bf16[128,3584]{1,0:T(8,128)(2,1)S(1)} %collective-permute-done.11.refs_1_) | copy-start | bytes 2752516
  100.3 4.3 %copy-start.10 = (bf16[128,3584]{1,0:T(8,128)(2,1)S(1)}, bf16[128,3584]{1,0:T(8,128)(2,1)}, u32[]{:S(2)}) copy-start(bf16[128,3584]{1,0:T(8,128)(2,1)} %add_convert_fusion.refs_6_) | copy-start | bytes 2752516
  104.6 2.7 %collective-permute-start.13 = (bf16[1,128,3584]{2,1,0:T(8,128)(2,1)}, bf16[1,128,3584]{2,1,0:T(8,128)(2,1)S(1)}, u32[]{:S(2)}, u32[]{:S(2)}) collective-permute-start(bf16[1,128,3584]{2,1,0:T(8,128)(2,1)} %shard_map.123.refs_0_.refs_2_), channel_id=1, source_target_pairs={{0,4},{4,0},{8,12},{12,8},{1,5},{5,1},{9,13},{13,9},{2,6},{6,2},{1... | collective-permute-start | bytes 2752520 | tf_op jit(solution)/shard_map/ppermute | solution.py:556
  104.6 22.8 %collective-permute-start.17 = (bf16[128,3584]{1,0:T(8,128)(2,1)S(1)}, bf16[128,3584]{1,0:T(8,128)(2,1)S(1)}, u32[]{:S(2)}, u32[]{:S(2)}) collective-permute-start(bf16[128,3584]{1,0:T(8,128)(2,1)S(1)} %copy-done.10), channel_id=1, source_target_pairs={{0,8},{4,12},{8,0},{12,4},{1,9},{5,13},{9,1},{13,5},{2,10},{6,14},... | collective-permute-start | bytes 2752520 | tf_op jit(solution)/shard_map/ppermute | solution.py:551
  105.5 28.4 %collective-permute-start.19 = (bf16[1,128,3584]{2,1,0:T(8,128)(2,1)}, bf16[1,128,3584]{2,1,0:T(8,128)(2,1)S(1)}, u32[]{:S(2)}, u32[]{:S(2)}) collective-permute-start(bf16[1,128,3584]{2,1,0:T(8,128)(2,1)} %shard_map.123.refs_0_.refs_2_), channel_id=1, source_target_pairs={{0,16},{16,0},{1,17},{17,1},{2,18},{18,2},{3,19},{19,3},{4,20},{20... | collective-permute-start | bytes 2752520 | tf_op jit(solution)/shard_map/ppermute | solution.py:551
  132.6 2.4 %copy-start.29 = (bf16[64,2048]{1,0:T(8,128)(2,1)S(1)}, bf16[64,2048]{1,0:T(8,128)(2,1)}, u32[]{:S(2)}) copy-start(bf16[64,2048]{1,0:T(8,128)(2,1)} %get-tuple-element.35) | copy-start | bytes 786436
  132.6 4.9 %copy-start.28 = (bf16[64,2048]{1,0:T(8,128)(2,1)S(1)}, bf16[64,2048]{1,0:T(8,128)(2,1)}, u32[]{:S(2)}) copy-start(bf16[64,2048]{1,0:T(8,128)(2,1)} %get-tuple-element.36) | copy-start | bytes 786436
  132.6 5.4 %copy-start.27 = (bf16[64,2048]{1,0:T(8,128)(2,1)S(1)}, bf16[64,2048]{1,0:T(8,128)(2,1)}, u32[]{:S(2)}) copy-start(bf16[64,2048]{1,0:T(8,128)(2,1)} %get-tuple-element.37) | copy-start | bytes 786436
  132.6 24.8 %collective-permute-start.18 = (bf16[2,128,3584]{2,1,0:T(8,128)(2,1)}, bf16[2,128,3584]{2,1,0:T(8,128)(2,1)S(1)}, u32[]{:S(2)}, u32[]{:S(2)}) collective-permute-start(bf16[2,128,3584]{2,1,0:T(8,128)(2,1)} %shard_map.126.refs_1_.refs_8_.refs_0_.refs_6_), channel_id=1, source_target_pairs={{0,4},{4,0},{8,12},{12,8},{1,5},{5,1},{9,13},{13,9},{2,6},{6,2},{1... | collective-permute-start | bytes 5505032 | tf_op jit(solution)/shard_map/ppermute | solution.py:556
  132.7 43.1 %collective-permute-start.24 = (bf16[2,128,3584]{2,1,0:T(8,128)(2,1)}, bf16[2,128,3584]{2,1,0:T(8,128)(2,1)S(1)}, u32[]{:S(2)}, u32[]{:S(2)}) collective-permute-start(bf16[2,128,3584]{2,1,0:T(8,128)(2,1)} %shard_map.126.refs_1_.refs_8_.refs_0_.refs_6_), channel_id=1, source_target_pairs={{0,16},{16,0},{1,17},{17,1},{2,18},{18,2},{3,19},{19,3},{4,20},{20... | collective-permute-start | bytes 5505032 | tf_op jit(solution)/shard_map/ppermute | solution.py:551
  134.8 3.2 %collective-permute-start.20 = (bf16[1,128,3584]{2,1,0:T(8,128)(2,1)}, bf16[1,128,3584]{2,1,0:T(8,128)(2,1)S(1)}, u32[]{:S(2)}, u32[]{:S(2)}) collective-permute-start(bf16[1,128,3584]{2,1,0:T(8,128)(2,1)} %shard_map.127.refs_4_), channel_id=1, source_target_pairs={{0,4},{4,0},{8,12},{12,8},{1,5},{5,1},{9,13},{13,9},{2,6},{6,2},{1... | collective-permute-start | bytes 2752520 | tf_op jit(solution)/shard_map/ppermute | solution.py:556
  135.0 37.9 %collective-permute-start.14 = (bf16[64,2048]{1,0:T(8,128)(2,1)S(1)}, bf16[64,2048]{1,0:T(8,128)(2,1)S(1)}, u32[]{:S(2)}, u32[]{:S(2)}) collective-permute-start(bf16[64,2048]{1,0:T(8,128)(2,1)S(1)} %copy-done.29), channel_id=1, source_target_pairs={{0,3},{1,0},{2,1},{3,2},{4,7},{5,4},{6,5},{7,6},{8,11},{9,8},{10,9... | collective-permute-start | bytes 786440 | tf_op jit(solution)/shard_map/ppermute | solution.py:551
  137.5 35.3 %collective-permute-start.15 = (bf16[64,2048]{1,0:T(8,128)(2,1)S(1)}, bf16[64,2048]{1,0:T(8,128)(2,1)S(1)}, u32[]{:S(2)}, u32[]{:S(2)}) collective-permute-start(bf16[64,2048]{1,0:T(8,128)(2,1)S(1)} %copy-done.28), channel_id=1, source_target_pairs={{0,1},{1,2},{2,3},{3,0},{4,5},{5,6},{6,7},{7,4},{8,9},{9,10},{10,1... | collective-permute-start | bytes 786440 | tf_op jit(solution)/shard_map/ppermute | solution.py:551
  138.0 1.9 copy-start.19
  138.0 34.9 %collective-permute-start.16 = (bf16[64,2048]{1,0:T(8,128)(2,1)S(1)}, bf16[64,2048]{1,0:T(8,128)(2,1)S(1)}, u32[]{:S(2)}, u32[]{:S(2)}) collective-permute-start(bf16[64,2048]{1,0:T(8,128)(2,1)S(1)} %copy-done.27), channel_id=1, source_target_pairs={{0,2},{1,3},{2,0},{3,1},{4,6},{5,7},{6,4},{7,5},{8,10},{9,11},{10,... | collective-permute-start | bytes 786440 | tf_op jit(solution)/shard_map/ppermute | solution.py:551
  157.5 1.2 copy-start.5
  175.8 1.3 copy-start.32
  175.8 3.6 %copy-start.31 = (bf16[64,2048]{1,0:T(8,128)(2,1)S(1)}, bf16[64,2048]{1,0:T(8,128)(2,1)}, u32[]{:S(2)}) copy-start(bf16[64,2048]{1,0:T(8,128)(2,1)} %get-tuple-element.43) | copy-start | bytes 786436
  175.8 4.0 %copy-start.30 = (bf16[64,2048]{1,0:T(8,128)(2,1)S(1)}, bf16[64,2048]{1,0:T(8,128)(2,1)}, u32[]{:S(2)}) copy-start(bf16[64,2048]{1,0:T(8,128)(2,1)} %get-tuple-element.44) | copy-start | bytes 786436
  175.8 1.2 copy-start.4
  177.1 5.5 %collective-permute-start.25 = (bf16[2,128,3584]{2,1,0:T(8,128)(2,1)}, bf16[2,128,3584]{2,1,0:T(8,128)(2,1)S(1)}, u32[]{:S(2)}, u32[]{:S(2)}) collective-permute-start(bf16[2,128,3584]{2,1,0:T(8,128)(2,1)} %shard_map.131.refs_8_), channel_id=1, source_target_pairs={{0,4},{4,0},{8,12},{12,8},{1,5},{5,1},{9,13},{13,9},{2,6},{6,2},{1... | collective-permute-start | bytes 5505032 | tf_op jit(solution)/shard_map/ppermute | solution.py:556
  177.1 33.9 %collective-permute-start.21 = (bf16[64,2048]{1,0:T(8,128)(2,1)S(1)}, bf16[64,2048]{1,0:T(8,128)(2,1)S(1)}, u32[]{:S(2)}, u32[]{:S(2)}) collective-permute-start(bf16[64,2048]{1,0:T(8,128)(2,1)S(1)} %copy-done.32), channel_id=1, source_target_pairs={{0,3},{1,0},{2,1},{3,2},{4,7},{5,4},{6,5},{7,6},{8,11},{9,8},{10,9... | collective-permute-start | bytes 786440 | tf_op jit(solution)/shard_map/ppermute | solution.py:551
  179.4 31.6 %collective-permute-start.22 = (bf16[64,2048]{1,0:T(8,128)(2,1)S(1)}, bf16[64,2048]{1,0:T(8,128)(2,1)S(1)}, u32[]{:S(2)}, u32[]{:S(2)}) collective-permute-start(bf16[64,2048]{1,0:T(8,128)(2,1)S(1)} %copy-done.31), channel_id=1, source_target_pairs={{0,1},{1,2},{2,3},{3,0},{4,5},{5,6},{6,7},{7,4},{8,9},{9,10},{10,1... | collective-permute-start | bytes 786440 | tf_op jit(solution)/shard_map/ppermute | solution.py:551
  179.8 31.2 %collective-permute-start.23 = (bf16[64,2048]{1,0:T(8,128)(2,1)S(1)}, bf16[64,2048]{1,0:T(8,128)(2,1)S(1)}, u32[]{:S(2)}, u32[]{:S(2)}) collective-permute-start(bf16[64,2048]{1,0:T(8,128)(2,1)S(1)} %copy-done.30), channel_id=1, source_target_pairs={{0,2},{1,3},{2,0},{3,1},{4,6},{5,7},{6,4},{7,5},{8,10},{9,11},{10,... | collective-permute-start | bytes 786440 | tf_op jit(solution)/shard_map/ppermute | solution.py:551
  182.6 1.3 copy-start.15
  (11 other events, 9.3 us)

commit v7 on v6

--- a/solution.py
+++ b/solution.py
@@ -358,8 +358,8 @@
 def mark(*earlier):
     total = 0.0
     for x in earlier:
-        corner = lax.slice(x, (0,) * x.ndim, (1,) * x.ndim).reshape(())
-        total = total + jnp.abs(corner.astype(jnp.float32))
+        corner = x[(0,) * (x.ndim - 2)][:16, :BLK]
+        total = total + jnp.sum(jnp.abs(corner.astype(jnp.float32)))
     return lax.optimization_barrier(jnp.minimum(total, 0.0))
 
 

time: 215 us -> 219 us (1.019)
  other arithmetic: 10.8 us -> 16.4 us
  local copies, waits for them, and re-layouts: 13.7 us -> 11.5 us
    reduce_sum x0 -> x5, other arithmetic: none -> 3.89 us  [mark(): total = total + jnp.sum(jnp.abs(corner.astype(jnp.float32)))]
    slice x5 -> x0, local copies, waits for them, and re-layouts: 2.69 us -> none  [mark(): corner = lax.slice(x, (0,) * x.ndim, (1,) * x.ndim).reshape(())]
    unnamed x72 -> x68, local copies, waits for them, and re-layouts: 10.9 us -> 11.4 us
  transfers between devices with their start and end apart: 26 -> 26, of which waited for: 6 -> 6; matrix products, arithmetic and copies ran while one was open for 5% -> 7% of each run, Pallas kernels for 54% -> 53%
where the time goes in v7:
time: 219 us; the launch traced here: 218 us
  Pallas kernels  130 us (59%)
  starting transfers between devices  33.5 us (15%)
  waiting for transfers between devices  22.2 us (10%)
  other arithmetic  16.4 us (7%)
  local copies, waits for them, and re-layouts  11.5 us (5%)
  between operations  4.34 us (2%)
    pallas_call x2, Pallas kernels, block_grads(): pl.pallas_call(functools.partial(block_grad_kernel, mats, len(lefts), len...  44.5 us
    ppermute x19, starting transfers between devices, shift(): return lax.ppermute(x, axis, [(i, (i + by) % n) for i in range(n)])  33 us
    pallas_call x2, Pallas kernels, project_blocks(): pl.pallas_call(functools.partial(project_blocks_kernel, transposed, rows,...  25.7 us
    pallas_call x2, Pallas kernels, back(): pl.pallas_call(functools.partial(back_kernel, transposed, n_pieces, mats,...  22.5 us
    ppermute x19, waiting for transfers between devices, shift(): return lax.ppermute(x, axis, [(i, (i + by) % n) for i in range(n)])  21.5 us
    unnamed x68, local copies, waits for them, and re-layouts  11.4 us
    pallas_call x1, Pallas kernels, densify(): pl.pallas_call(functools.partial(densify_kernel, mats, rows, cols, panels...  10.8 us
    pallas_call x2, Pallas kernels, pointwise(): pl.pallas_call(functools.partial(kernel, len(gates)), out_shape=tuple((sh...  9.14 us
  transfers between devices with their start and end apart: 26, of which 6 were waited for; matrix products, arithmetic and copies ran while one was open for 7% of the time, Pallas kernels for 53%

profile of v7, /device:TPU:0, one launch (start us, length us, event | category | flops | bytes accessed | tf_op | source)
XLA Modules:
  0.0 217.9 jit_solution(10981123554952356504)
XLA Ops:
  0.6 3.1 %collective-permute-start = (bf16[64,2048]{1,0:T(8,128)(2,1)}, bf16[64,2048]{1,0:T(8,128)(2,1)S(1)}, u32[]{:S(2)}, u32[]{:S(2)}) collective-permute-start(bf16[64,2048]{1,0:T(8,128)(2,1)} %param.8), channel_id=1, source_target_pairs={{0,1},{1,2},{2,3},{3,0},{4,5},{5,6},{6,7},{7,4},{8,9},{9,10},{10,1... | collective-permute-start | bytes 786440 | tf_op jit(solution)/shard_map/ppermute | solution.py:551
  3.7 2.6 %collective-permute-start.1 = (bf16[64,2048]{1,0:T(8,128)(2,1)}, bf16[64,2048]{1,0:T(8,128)(2,1)S(1)}, u32[]{:S(2)}, u32[]{:S(2)}) collective-permute-start(bf16[64,2048]{1,0:T(8,128)(2,1)} %param.8), channel_id=1, source_target_pairs={{0,2},{1,3},{2,0},{3,1},{4,6},{5,7},{6,4},{7,5},{8,10},{9,11},{10,... | collective-permute-start | bytes 786440 | tf_op jit(solution)/shard_map/ppermute | solution.py:551
  6.3 1.3 collective-permute-start.2
  7.6 1.0 constant_dynamic-update-slice_fusion.3
  8.6 0.8 fusion.2
  9.4 0.8 fusion
  11.1 10.8 %shard_map.119.weight.refs_2_ = bf16[2048,3584]{1,0:T(8,128)(2,1)} custom-call(s32[448]{0:T(512)} %broadcast_subtract_fusion.2.refs_0_, bf16[336,128,128]{2,1,0:T(8,128)(2,1)} %bitcast.14), custom_call_target="tpu_custom_call" | custom-call | bytes 25 | tf_op jit(solution)/shard_map/pallas_call | solution.py:104
  22.0 1.6 collective-permute-done.1
  23.7 1.0 copy-done
  24.7 8.9 %shard_map.120 = (f32[128,3584]{1,0:T(8,128)}, bf16[128,3584]{1,0:T(8,128)(2,1)}) custom-call(s32[1]{0:T(128)} %bitcast.core_ref, bf16[256,2048]{1,0:T(8,128)(2,1)} %copy-done, bf16[2048,3584]{1,0:T(8,128)(2,1)} %shard_map.119.weight.refs_2_), custom_call_target="tpu_custom_call" | custom-call | flops 3758 | bytes 14 | tf_op jit(solution)/shard_map/pallas_call | solution.py:165
  34.1 1.5 collective-permute-start.6
  35.6 6.1 %collective-permute-start.8 = (bf16[64,2048]{1,0:T(8,128)(2,1)S(1)}, bf16[64,2048]{1,0:T(8,128)(2,1)S(1)}, u32[]{:S(2)}, u32[]{:S(2)}) collective-permute-start(bf16[64,2048]{1,0:T(8,128)(2,1)S(1)} %copy-done.18), channel_id=1, source_target_pairs={{0,1},{1,2},{2,3},{3,0},{4,5},{5,6},{6,7},{7,4},{8,9},{9,10},{10,1... | collective-permute-start | bytes 786440 | tf_op jit(solution)/shard_map/ppermute | solution.py:551
  41.7 2.0 add_convert_fusion.2.refs_0_
  43.7 1.6 collective-permute-start.4
  45.3 1.7 collective-permute-start.9
  47.0 12.9 %shard_map.121 = (f32[128,3584]{1,0:T(8,128)}, bf16[128,3584]{1,0:T(8,128)(2,1)}, bf16[2048,3584]{1,0:T(8,128)(2,1)}) custom-call(s32[1]{0:T(128)} %bitcast.core_ref, s32[448]{0:T(512)} %broadcast_subtract_fusion.1.table.refs_1_, bf16[256,2048]{1,0:T(8,128)(2,1)} %copy-done, bf16[336,128,128]{2,1,0:T(8,128)(2,1)} %bitcast.16, bf16[128,3584]{1,0:T(8,128)(2,1)} %copy-done.10), custom_call_target="tpu_custom_call" | custom-call | flops 3758 | bytes 29 | tf_op jit(solution)/shard_map/pallas_call | solution.py:230
  60.6 1.4 collective-permute-start.10
  62.0 7.3 %collective-permute-done.10 = bf16[64,2048]{1,0:T(8,128)(2,1)S(1)} collective-permute-done((bf16[64,2048]{1,0:T(8,128)(2,1)S(1)}, bf16[64,2048]{1,0:T(8,128)(2,1)S(1)}, u32[]{:S(2)}, u32[]{:S(2)}) %collective-permute-start.10) | collective-permute-done | bytes 262176 | tf_op jit(solution)/shard_map/ppermute | solution.py:551
  69.9 0.7 abs_reduce_fusion.2
  73.5 2.0 add_convert_fusion.1.refs_0_
  76.7 12.8 %shard_map.122 = (f32[128,3584]{1,0:T(8,128)}, bf16[128,3584]{1,0:T(8,128)(2,1)}, bf16[3584,2048]{1,0:T(8,128)(2,1)}) custom-call(s32[1]{0:T(128)} %bitcast.core_ref, s32[448]{0:T(512)} %broadcast_subtract_fusion.table.refs_0_, bf16[256,2048]{1,0:T(8,128)(2,1)} %copy-done.5, bf16[336,128,128]{2,1,0:T(8,128)(2,1)} %bitcast.17, bf16[128,3584]{1,0:T(8,128)(2,1)} %copy-done.13), custom_call_target="tpu_custom_call" | custom-call | flops 3758 | bytes 29 | tf_op jit(solution)/shard_map/pallas_call | solution.py:230
  89.6 4.6 %collective-permute-done.12.refs_7_ = bf16[256,2048]{1,0:T(8,128)(2,1)} collective-permute-done((bf16[256,2048]{1,0:T(8,128)(2,1)S(1)}, bf16[256,2048]{1,0:T(8,128)(2,1)}, u32[]{:S(2)}, u32[]{:S(2)}) %collective-permute-start.12) | collective-permute-done | bytes 1048608 | tf_op jit(solution)/shard_map/ppermute | solution.py:551
  94.3 1.3 abs_reduce_fusion
  95.6 1.9 collective-permute-done.7.refs_5_
  97.5 0.9 copy-done.7
  100.3 3.0 %add_convert_fusion.refs_6_ = bf16[128,3584]{1,0:T(8,128)(2,1)} fusion(f32[128,3584]{1,0:T(8,128)} %get-tuple-element.31.refs_0_, bf16[128,3584]{1,0:T(8,128)(2,1)S(1)} %collective-permute-done.11.refs_1_, f32[]{:T(128)S(6)} %min.7), kind=kLoop, calls=%fused_computation | loop fusion | flops 1835008 | bytes 3670020 | tf_op jit(solution)/shard_map/convert_element_type | solution.py:319
  103.3 4.3 %shard_map.123.refs_0_.refs_2_ = bf16[1,128,3584]{2,1,0:T(8,128)(2,1)} custom-call(f32[128,3584]{1,0:T(8,128)} %get-tuple-element.26.refs_0_, bf16[128,3584]{1,0:T(8,128)(2,1)} %copy-done.1, bf16[128,3584]{1,0:T(8,128)(2,1)} %copy-done.6, f32[128,3584]{1,0:T(8,128)} %get-tuple-element.28.refs_3_, bf16[128,3584]{1,0:T(8,128)(2,1)} %copy-done.2, ...), custom_call_target="tpu_custom_call" | custom-call | bytes 13 | tf_op jit(solution)/shard_map/pallas_call | solution.py:386
  108.2 1.4 collective-permute-start.19
  110.3 0.9 copy-done.12
  111.3 8.3 %shard_map.124 = (f32[64,2048]{1,0:T(8,128)}, bf16[64,2048]{1,0:T(8,128)(2,1)}, bf16[64,2048]{1,0:T(8,128)(2,1)}, bf16[64,2048]{1,0:T(8,128)(2,1)}) custom-call(s32[1]{0:T(128)} %bitcast.core_ref, bf16[1,128,3584]{2,1,0:T(8,128)(2,1)} %shard_map.123.refs_0_.refs_2_, bf16[1,128,3584]{2,1,0:T(8,128)(2,1)} %copy-done.12, ...), custom_call_target="tpu_custom_call" | custom-call | flops 3758 | bytes 14 | tf_op jit(solution)/shard_map/pallas_call | solution.py:297
  119.6 4.8 %shard_map.125 = (f32[128,3584]{1,0:T(8,128)}, f32[128,3584]{1,0:T(8,128)}) custom-call(f32[128,3584]{1,0:T(8,128)} %get-tuple-element.26.refs_0_, bf16[128,3584]{1,0:T(8,128)(2,1)} %copy-done.1, bf16[128,3584]{1,0:T(8,128)(2,1)} %copy-done.6, f32[128,3584]{1,0:T(8,128)} %get-tuple-element.28.refs_3_, bf16[128,3584]{1,0:T(8,128)(2,1)} %copy-done.2, ...), custom_call_target="tpu_custom_call" | custom-call | bytes 13 | tf_op jit(solution)/shard_map/pallas_call | solution.py:386
  124.4 6.0 %collective-permute-done.17.refs_2_ = bf16[128,3584]{1,0:T(8,128)(2,1)S(1)} collective-permute-done((bf16[128,3584]{1,0:T(8,128)(2,1)S(1)}, bf16[128,3584]{1,0:T(8,128)(2,1)S(1)}, u32[]{:S(2)}, u32[]{:S(2)}) %collective-permute-start.17) | collective-permute-done | bytes 917536 | tf_op jit(solution)/shard_map/ppermute | solution.py:551
  130.4 0.9 copy-done.16
  131.3 4.3 %shard_map.126.refs_1_.refs_8_.refs_0_.refs_6_ = bf16[2,128,3584]{2,1,0:T(8,128)(2,1)} custom-call(f32[128,3584]{1,0:T(8,128)} %get-tuple-element.31.refs_0_, bf16[128,3584]{1,0:T(8,128)(2,1)} %copy-done.8, bf16[128,3584]{1,0:T(8,128)(2,1)} %copy-done.16, f32[128,3584]{1,0:T(8,128)} %get-tuple-element.38.refs_3_, f32[128,3584]{1,0:T(8,128)} %get-tuple-element.39.refs_4_), custom_call_target="tpu_custom_call" | custom-call | bytes 9 | tf_op jit(solution)/shard_map/pallas_call | solution.py:420
  135.8 1.5 collective-permute-start.24
  137.2 0.9 copy-done.11
  138.3 3.3 %collective-permute-start.14 = (bf16[64,2048]{1,0:T(8,128)(2,1)S(1)}, bf16[64,2048]{1,0:T(8,128)(2,1)S(1)}, u32[]{:S(2)}, u32[]{:S(2)}) collective-permute-start(bf16[64,2048]{1,0:T(8,128)(2,1)S(1)} %copy-done.27), channel_id=1, source_target_pairs={{0,3},{1,0},{2,1},{3,2},{4,7},{5,4},{6,5},{7,6},{8,11},{9,8},{10,9... | collective-permute-start | bytes 786440 | tf_op jit(solution)/shard_map/ppermute | solution.py:551
  141.6 0.7 collective-permute-start.16
  143.0 17.5 %shard_map.128.refs_4_ = bf16[336,128,128]{2,1,0:T(8,128)(2,1)} custom-call(s32[1]{0:T(128)} %bitcast.core_ref, s32[448]{0:T(512)} %broadcast_subtract_fusion.table.refs_0_, s32[1]{0:T(128)} %bitcast.7.refs_1_, bf16[1,128,3584]{2,1,0:T(8,128)(2,1)} %shard_map.123.refs_0_.refs_2_, bf16[1,128,3584]{2,1,0:T(8,128)(2,1)} %copy-done.12, ...), custom_call_target="tpu_custom_call" | custom-call | flops 7516 | bytes 11 | tf_op jit(solution)/shard_map/pallas_call | solution.py:521
  160.6 1.2 copy-done.4
  161.8 14.2 %shard_map.129 = (f32[64,2048]{1,0:T(8,128)}, bf16[64,2048]{1,0:T(8,128)(2,1)}, bf16[64,2048]{1,0:T(8,128)(2,1)}, bf16[64,2048]{1,0:T(8,128)(2,1)}) custom-call(s32[1]{0:T(128)} %bitcast.core_ref, bf16[2,128,3584]{2,1,0:T(8,128)(2,1)} %shard_map.126.refs_1_.refs_8_.refs_0_.refs_6_, bf16[2,128,3584]{2,1,0:T(8,128)(2,1)} %copy-done.4, ...), custom_call_target="tpu_custom_call" | custom-call | flops 7516 | bytes 29 | tf_op jit(solution)/shard_map/pallas_call | solution.py:297
  176.8 2.1 shard_map.130.refs_1_
  178.9 1.2 copy-done.3
  180.2 3.5 %collective-permute-start.21 = (bf16[64,2048]{1,0:T(8,128)(2,1)S(1)}, bf16[64,2048]{1,0:T(8,128)(2,1)S(1)}, u32[]{:S(2)}, u32[]{:S(2)}) collective-permute-start(bf16[64,2048]{1,0:T(8,128)(2,1)S(1)} %copy-done.30), channel_id=1, source_target_pairs={{0,3},{1,0},{2,1},{3,2},{4,7},{5,4},{6,5},{7,6},{8,11},{9,8},{10,9... | collective-permute-start | bytes 786440 | tf_op jit(solution)/shard_map/ppermute | solution.py:551
  183.9 1.4 collective-permute-start.23
  186.6 1.3 copy-done.14
  187.9 27.0 %shard_map.132 = (bf16[336,128,128]{2,1,0:T(8,128)(2,1)}, bf16[336,128,128]{2,1,0:T(8,128)(2,1)}) custom-call(s32[1]{0:T(128)} %bitcast.core_ref, s32[448]{0:T(512)} %broadcast_subtract_fusion.2.refs_0_, s32[448]{0:T(512)} %broadcast_subtract_fusion.1.table.refs_1_, s32[1]{0:T(128)} %bitcast.8.refs_2_, s32[1]{0:T(128)} %bitcast.9.refs_3_, ...), custom_call_target="tpu_custom_call" | custom-call | flops 15032 | bytes 22 | tf_op jit(solution)/shard_map/pallas_call | solution.py:521
  215.8 2.1 shard_map.133
  (107 shorter events, 11.1 us)
Async XLA Ops:
  0.6 21.3 %collective-permute-start = (bf16[64,2048]{1,0:T(8,128)(2,1)}, bf16[64,2048]{1,0:T(8,128)(2,1)S(1)}, u32[]{:S(2)}, u32[]{:S(2)}) collective-permute-start(bf16[64,2048]{1,0:T(8,128)(2,1)} %param.8), channel_id=1, source_target_pairs={{0,1},{1,2},{2,3},{3,0},{4,5},{5,6},{6,7},{7,4},{8,9},{9,10},{10,1... | collective-permute-start | bytes 786440 | tf_op jit(solution)/shard_map/ppermute | solution.py:551
  3.7 19.9 %collective-permute-start.1 = (bf16[64,2048]{1,0:T(8,128)(2,1)}, bf16[64,2048]{1,0:T(8,128)(2,1)S(1)}, u32[]{:S(2)}, u32[]{:S(2)}) collective-permute-start(bf16[64,2048]{1,0:T(8,128)(2,1)} %param.8), channel_id=1, source_target_pairs={{0,2},{1,3},{2,0},{3,1},{4,6},{5,7},{6,4},{7,5},{8,10},{9,11},{10,... | collective-permute-start | bytes 786440 | tf_op jit(solution)/shard_map/ppermute | solution.py:551
  6.3 17.4 %collective-permute-start.2 = (bf16[64,2048]{1,0:T(8,128)(2,1)}, bf16[64,2048]{1,0:T(8,128)(2,1)S(1)}, u32[]{:S(2)}, u32[]{:S(2)}) collective-permute-start(bf16[64,2048]{1,0:T(8,128)(2,1)} %param.8), channel_id=1, source_target_pairs={{0,3},{1,0},{2,1},{3,2},{4,7},{5,4},{6,5},{7,6},{8,11},{9,8},{10,9... | collective-permute-start | bytes 786440 | tf_op jit(solution)/shard_map/ppermute | solution.py:551
  23.7 1.0 copy-start
  24.6 11.0 %copy-start.18 = (bf16[64,2048]{1,0:T(8,128)(2,1)S(1)}, bf16[64,2048]{1,0:T(8,128)(2,1)}, u32[]{:S(2)}) copy-start(bf16[64,2048]{1,0:T(8,128)(2,1)} %param.9) | copy-start | bytes 786436
  33.5 8.2 %collective-permute-start.3 = (bf16[128,3584]{1,0:T(8,128)(2,1)}, bf16[128,3584]{1,0:T(8,128)(2,1)S(1)}, u32[]{:S(2)}, u32[]{:S(2)}) collective-permute-start(bf16[128,3584]{1,0:T(8,128)(2,1)} %get-tuple-element.27), channel_id=1, source_target_pairs={{0,4},{4,0},{8,12},{12,8},{1,5},{5,1},{9,13},{13,9},{2,6},{6,2},{1... | collective-permute-start | bytes 2752520 | tf_op jit(solution)/shard_map/ppermute | solution.py:556
  34.1 35.8 %collective-permute-start.6 = (bf16[256,2048]{1,0:T(8,128)(2,1)}, bf16[256,2048]{1,0:T(8,128)(2,1)S(1)}, u32[]{:S(2)}, u32[]{:S(2)}) collective-permute-start(bf16[256,2048]{1,0:T(8,128)(2,1)} %copy-done), channel_id=1, source_target_pairs={{0,16},{16,0},{1,17},{17,1},{2,18},{18,2},{3,19},{19,3},{4,20},{20... | collective-permute-start | bytes 3145736 | tf_op jit(solution)/shard_map/ppermute | solution.py:551
  35.6 24.9 %collective-permute-start.8 = (bf16[64,2048]{1,0:T(8,128)(2,1)S(1)}, bf16[64,2048]{1,0:T(8,128)(2,1)S(1)}, u32[]{:S(2)}, u32[]{:S(2)}) collective-permute-start(bf16[64,2048]{1,0:T(8,128)(2,1)S(1)} %copy-done.18), channel_id=1, source_target_pairs={{0,1},{1,2},{2,3},{3,0},{4,5},{5,6},{6,7},{7,4},{8,9},{9,10},{10,1... | collective-permute-start | bytes 786440 | tf_op jit(solution)/shard_map/ppermute | solution.py:551
  41.7 2.0 copy-start.1
  43.7 3.3 %copy-start.10 = (bf16[128,3584]{1,0:T(8,128)(2,1)}, bf16[128,3584]{1,0:T(8,128)(2,1)S(1)}, u32[]{:S(2)}) copy-start(bf16[128,3584]{1,0:T(8,128)(2,1)S(1)} %add_convert_fusion.2.refs_0_) | copy-start | bytes 2752516
  43.7 26.9 %collective-permute-start.4 = (bf16[128,3584]{1,0:T(8,128)(2,1)S(1)}, bf16[128,3584]{1,0:T(8,128)(2,1)S(1)}, u32[]{:S(2)}, u32[]{:S(2)}) collective-permute-start(bf16[128,3584]{1,0:T(8,128)(2,1)S(1)} %add_convert_fusion.2.refs_0_), channel_id=1, source_target_pairs={{0,8},{4,12},{8,0},{12,4},{1,9},{5,13},{9,1},{13,5},{2,10},{6,14},... | collective-permute-start | bytes 2752520 | tf_op jit(solution)/shard_map/ppermute | solution.py:551
  45.3 16.7 %collective-permute-start.9 = (bf16[64,2048]{1,0:T(8,128)(2,1)S(1)}, bf16[64,2048]{1,0:T(8,128)(2,1)S(1)}, u32[]{:S(2)}, u32[]{:S(2)}) collective-permute-start(bf16[64,2048]{1,0:T(8,128)(2,1)S(1)} %copy-done.18), channel_id=1, source_target_pairs={{0,2},{1,3},{2,0},{3,1},{4,6},{5,7},{6,4},{7,5},{8,10},{9,11},{10,... | collective-permute-start | bytes 786440 | tf_op jit(solution)/shard_map/ppermute | solution.py:551
  59.9 13.6 %collective-permute-start.5 = (bf16[128,3584]{1,0:T(8,128)(2,1)}, bf16[128,3584]{1,0:T(8,128)(2,1)S(1)}, u32[]{:S(2)}, u32[]{:S(2)}) collective-permute-start(bf16[128,3584]{1,0:T(8,128)(2,1)} %get-tuple-element.29), channel_id=1, source_target_pairs={{0,4},{4,0},{8,12},{12,8},{1,5},{5,1},{9,13},{13,9},{2,6},{6,2},{1... | collective-permute-start | bytes 2752520 | tf_op jit(solution)/shard_map/ppermute | solution.py:556
  60.6 8.7 %collective-permute-start.10 = (bf16[64,2048]{1,0:T(8,128)(2,1)S(1)}, bf16[64,2048]{1,0:T(8,128)(2,1)S(1)}, u32[]{:S(2)}, u32[]{:S(2)}) collective-permute-start(bf16[64,2048]{1,0:T(8,128)(2,1)S(1)} %copy-done.18), channel_id=1, source_target_pairs={{0,3},{1,0},{2,1},{3,2},{4,7},{5,4},{6,5},{7,6},{8,11},{9,8},{10,9... | collective-permute-start | bytes 786440 | tf_op jit(solution)/shard_map/ppermute | solution.py:551
  69.3 6.3 %copy-start.5 = (bf16[256,2048]{1,0:T(8,128)(2,1)}, bf16[256,2048]{1,0:T(8,128)(2,1)S(1)}, u32[]{:S(2)}) copy-start(bf16[256,2048]{1,0:T(8,128)(2,1)S(1)} %constant_dynamic-update-slice_fusion.4.panel.refs_6_) | copy-start | bytes 3145732
  69.3 24.9 %collective-permute-start.12 = (bf16[256,2048]{1,0:T(8,128)(2,1)S(1)}, bf16[256,2048]{1,0:T(8,128)(2,1)}, u32[]{:S(2)}, u32[]{:S(2)}) collective-permute-start(bf16[256,2048]{1,0:T(8,128)(2,1)S(1)} %constant_dynamic-update-slice_fusion.4.panel.refs_6_), channel_id=1, source_target_pairs={{0,16},{16,0},{1,17},{17,1},{2,18},{18,2},{3,19},{19,3},{4,20},{20... | collective-permute-start | bytes 3145736 | tf_op jit(solution)/shard_map/ppermute | solution.py:551
  69.9 1.0 copy-start.15
  70.9 4.7 %copy-start.6 = (bf16[128,3584]{1,0:T(8,128)(2,1)}, bf16[128,3584]{1,0:T(8,128)(2,1)S(1)}, u32[]{:S(2)}) copy-start(bf16[128,3584]{1,0:T(8,128)(2,1)S(1)} %collective-permute-done.4.refs_2_) | copy-start | bytes 2752516
  73.5 2.1 copy-start.2
  75.6 1.1 copy-start.13
  75.6 21.9 %collective-permute-start.7 = (bf16[128,3584]{1,0:T(8,128)(2,1)S(1)}, bf16[128,3584]{1,0:T(8,128)(2,1)S(1)}, u32[]{:S(2)}, u32[]{:S(2)}) collective-permute-start(bf16[128,3584]{1,0:T(8,128)(2,1)S(1)} %add_convert_fusion.1.refs_0_), channel_id=1, source_target_pairs={{0,8},{4,12},{8,0},{12,4},{1,9},{5,13},{9,1},{13,5},{2,10},{6,14},... | collective-permute-start | bytes 2752520 | tf_op jit(solution)/shard_map/ppermute | solution.py:551
  89.6 10.7 %collective-permute-start.11 = (bf16[128,3584]{1,0:T(8,128)(2,1)}, bf16[128,3584]{1,0:T(8,128)(2,1)S(1)}, u32[]{:S(2)}, u32[]{:S(2)}) collective-permute-start(bf16[128,3584]{1,0:T(8,128)(2,1)} %get-tuple-element.32), channel_id=1, source_target_pairs={{0,4},{4,0},{8,12},{12,8},{1,5},{5,1},{9,13},{13,9},{2,6},{6,2},{1... | collective-permute-start | bytes 2752520 | tf_op jit(solution)/shard_map/ppermute | solution.py:556
  100.3 3.0 %copy-start.8 = (bf16[128,3584]{1,0:T(8,128)(2,1)}, bf16[128,3584]{1,0:T(8,128)(2,1)S(1)}, u32[]{:S(2)}) copy-start(bf16[128,3584]{1,0:T(8,128)(2,1)S(1)} %collective-permute-done.11.refs_1_) | copy-start | bytes 2752516
  103.3 4.4 %copy-start.9 = (bf16[128,3584]{1,0:T(8,128)(2,1)S(1)}, bf16[128,3584]{1,0:T(8,128)(2,1)}, u32[]{:S(2)}) copy-start(bf16[128,3584]{1,0:T(8,128)(2,1)} %add_convert_fusion.refs_6_) | copy-start | bytes 2752516
  107.7 2.7 %collective-permute-start.13 = (bf16[1,128,3584]{2,1,0:T(8,128)(2,1)}, bf16[1,128,3584]{2,1,0:T(8,128)(2,1)S(1)}, u32[]{:S(2)}, u32[]{:S(2)}) collective-permute-start(bf16[1,128,3584]{2,1,0:T(8,128)(2,1)} %shard_map.123.refs_0_.refs_2_), channel_id=1, source_target_pairs={{0,4},{4,0},{8,12},{12,8},{1,5},{5,1},{9,13},{13,9},{2,6},{6,2},{1... | collective-permute-start | bytes 2752520 | tf_op jit(solution)/shard_map/ppermute | solution.py:556
  107.7 22.8 %collective-permute-start.17 = (bf16[128,3584]{1,0:T(8,128)(2,1)S(1)}, bf16[128,3584]{1,0:T(8,128)(2,1)S(1)}, u32[]{:S(2)}, u32[]{:S(2)}) collective-permute-start(bf16[128,3584]{1,0:T(8,128)(2,1)S(1)} %copy-done.9), channel_id=1, source_target_pairs={{0,8},{4,12},{8,0},{12,4},{1,9},{5,13},{9,1},{13,5},{2,10},{6,14},... | collective-permute-start | bytes 2752520 | tf_op jit(solution)/shard_map/ppermute | solution.py:551
  108.2 29.0 %collective-permute-start.19 = (bf16[1,128,3584]{2,1,0:T(8,128)(2,1)}, bf16[1,128,3584]{2,1,0:T(8,128)(2,1)S(1)}, u32[]{:S(2)}, u32[]{:S(2)}) collective-permute-start(bf16[1,128,3584]{2,1,0:T(8,128)(2,1)} %shard_map.123.refs_0_.refs_2_), channel_id=1, source_target_pairs={{0,16},{16,0},{1,17},{17,1},{2,18},{18,2},{3,19},{19,3},{4,20},{20... | collective-permute-start | bytes 2752520 | tf_op jit(solution)/shard_map/ppermute | solution.py:551
  110.3 0.9 copy-start.12
  135.7 2.6 %copy-start.27 = (bf16[64,2048]{1,0:T(8,128)(2,1)S(1)}, bf16[64,2048]{1,0:T(8,128)(2,1)}, u32[]{:S(2)}) copy-start(bf16[64,2048]{1,0:T(8,128)(2,1)} %get-tuple-element.35) | copy-start | bytes 786436
  135.7 5.9 %copy-start.26 = (bf16[64,2048]{1,0:T(8,128)(2,1)S(1)}, bf16[64,2048]{1,0:T(8,128)(2,1)}, u32[]{:S(2)}) copy-start(bf16[64,2048]{1,0:T(8,128)(2,1)} %get-tuple-element.36) | copy-start | bytes 786436
  135.7 5.9 %copy-start.25 = (bf16[64,2048]{1,0:T(8,128)(2,1)S(1)}, bf16[64,2048]{1,0:T(8,128)(2,1)}, u32[]{:S(2)}) copy-start(bf16[64,2048]{1,0:T(8,128)(2,1)} %get-tuple-element.37) | copy-start | bytes 786436
  135.7 24.8 %collective-permute-start.18 = (bf16[2,128,3584]{2,1,0:T(8,128)(2,1)}, bf16[2,128,3584]{2,1,0:T(8,128)(2,1)S(1)}, u32[]{:S(2)}, u32[]{:S(2)}) collective-permute-start(bf16[2,128,3584]{2,1,0:T(8,128)(2,1)} %shard_map.126.refs_1_.refs_8_.refs_0_.refs_6_), channel_id=1, source_target_pairs={{0,4},{4,0},{8,12},{12,8},{1,5},{5,1},{9,13},{13,9},{2,6},{6,2},{1... | collective-permute-start | bytes 5505032 | tf_op jit(solution)/shard_map/ppermute | solution.py:556
  135.8 43.1 %collective-permute-start.24 = (bf16[2,128,3584]{2,1,0:T(8,128)(2,1)}, bf16[2,128,3584]{2,1,0:T(8,128)(2,1)S(1)}, u32[]{:S(2)}, u32[]{:S(2)}) collective-permute-start(bf16[2,128,3584]{2,1,0:T(8,128)(2,1)} %shard_map.126.refs_1_.refs_8_.refs_0_.refs_6_), channel_id=1, source_target_pairs={{0,16},{16,0},{1,17},{17,1},{2,18},{18,2},{3,19},{19,3},{4,20},{20... | collective-permute-start | bytes 5505032 | tf_op jit(solution)/shard_map/ppermute | solution.py:551
  138.2 3.4 %collective-permute-start.20 = (bf16[1,128,3584]{2,1,0:T(8,128)(2,1)}, bf16[1,128,3584]{2,1,0:T(8,128)(2,1)S(1)}, u32[]{:S(2)}, u32[]{:S(2)}) collective-permute-start(bf16[1,128,3584]{2,1,0:T(8,128)(2,1)} %shard_map.127.refs_4_), channel_id=1, source_target_pairs={{0,4},{4,0},{8,12},{12,8},{1,5},{5,1},{9,13},{13,9},{2,6},{6,2},{1... | collective-permute-start | bytes 2752520 | tf_op jit(solution)/shard_map/ppermute | solution.py:556
  138.3 37.6 %collective-permute-start.14 = (bf16[64,2048]{1,0:T(8,128)(2,1)S(1)}, bf16[64,2048]{1,0:T(8,128)(2,1)S(1)}, u32[]{:S(2)}, u32[]{:S(2)}) collective-permute-start(bf16[64,2048]{1,0:T(8,128)(2,1)S(1)} %copy-done.27), channel_id=1, source_target_pairs={{0,3},{1,0},{2,1},{3,2},{4,7},{5,4},{6,5},{7,6},{8,11},{9,8},{10,9... | collective-permute-start | bytes 786440 | tf_op jit(solution)/shard_map/ppermute | solution.py:551
  141.6 34.3 %collective-permute-start.15 = (bf16[64,2048]{1,0:T(8,128)(2,1)S(1)}, bf16[64,2048]{1,0:T(8,128)(2,1)S(1)}, u32[]{:S(2)}, u32[]{:S(2)}) collective-permute-start(bf16[64,2048]{1,0:T(8,128)(2,1)S(1)} %copy-done.26), channel_id=1, source_target_pairs={{0,1},{1,2},{2,3},{3,0},{4,5},{5,6},{6,7},{7,4},{8,9},{9,10},{10,1... | collective-permute-start | bytes 786440 | tf_op jit(solution)/shard_map/ppermute | solution.py:551
  141.6 1.4 copy-start.17
  141.6 34.3 %collective-permute-start.16 = (bf16[64,2048]{1,0:T(8,128)(2,1)S(1)}, bf16[64,2048]{1,0:T(8,128)(2,1)S(1)}, u32[]{:S(2)}, u32[]{:S(2)}) collective-permute-start(bf16[64,2048]{1,0:T(8,128)(2,1)S(1)} %copy-done.25), channel_id=1, source_target_pairs={{0,2},{1,3},{2,0},{3,1},{4,6},{5,7},{6,4},{7,5},{8,10},{9,11},{10,... | collective-permute-start | bytes 786440 | tf_op jit(solution)/shard_map/ppermute | solution.py:551
  160.5 1.2 copy-start.4
  178.9 1.3 copy-start.30
  178.9 4.8 %copy-start.29 = (bf16[64,2048]{1,0:T(8,128)(2,1)S(1)}, bf16[64,2048]{1,0:T(8,128)(2,1)}, u32[]{:S(2)}) copy-start(bf16[64,2048]{1,0:T(8,128)(2,1)} %get-tuple-element.43) | copy-start | bytes 786436
  178.9 5.0 %copy-start.28 = (bf16[64,2048]{1,0:T(8,128)(2,1)S(1)}, bf16[64,2048]{1,0:T(8,128)(2,1)}, u32[]{:S(2)}) copy-start(bf16[64,2048]{1,0:T(8,128)(2,1)} %get-tuple-element.44) | copy-start | bytes 786436
  178.9 1.2 copy-start.3
  180.1 6.5 %collective-permute-start.25 = (bf16[2,128,3584]{2,1,0:T(8,128)(2,1)}, bf16[2,128,3584]{2,1,0:T(8,128)(2,1)S(1)}, u32[]{:S(2)}, u32[]{:S(2)}) collective-permute-start(bf16[2,128,3584]{2,1,0:T(8,128)(2,1)} %shard_map.131.refs_8_), channel_id=1, source_target_pairs={{0,4},{4,0},{8,12},{12,8},{1,5},{5,1},{9,13},{13,9},{2,6},{6,2},{1... | collective-permute-start | bytes 5505032 | tf_op jit(solution)/shard_map/ppermute | solution.py:556
  180.2 34.8 %collective-permute-start.21 = (bf16[64,2048]{1,0:T(8,128)(2,1)S(1)}, bf16[64,2048]{1,0:T(8,128)(2,1)S(1)}, u32[]{:S(2)}, u32[]{:S(2)}) collective-permute-start(bf16[64,2048]{1,0:T(8,128)(2,1)S(1)} %copy-done.30), channel_id=1, source_target_pairs={{0,3},{1,0},{2,1},{3,2},{4,7},{5,4},{6,5},{7,6},{8,11},{9,8},{10,9... | collective-permute-start | bytes 786440 | tf_op jit(solution)/shard_map/ppermute | solution.py:551
  183.7 31.3 %collective-permute-start.22 = (bf16[64,2048]{1,0:T(8,128)(2,1)S(1)}, bf16[64,2048]{1,0:T(8,128)(2,1)S(1)}, u32[]{:S(2)}, u32[]{:S(2)}) collective-permute-start(bf16[64,2048]{1,0:T(8,128)(2,1)S(1)} %copy-done.29), channel_id=1, source_target_pairs={{0,1},{1,2},{2,3},{3,0},{4,5},{5,6},{6,7},{7,4},{8,9},{9,10},{10,1... | collective-permute-start | bytes 786440 | tf_op jit(solution)/shard_map/ppermute | solution.py:551
  183.9 31.1 %collective-permute-start.23 = (bf16[64,2048]{1,0:T(8,128)(2,1)S(1)}, bf16[64,2048]{1,0:T(8,128)(2,1)S(1)}, u32[]{:S(2)}, u32[]{:S(2)}) collective-permute-start(bf16[64,2048]{1,0:T(8,128)(2,1)S(1)} %copy-done.28), channel_id=1, source_target_pairs={{0,2},{1,3},{2,0},{3,1},{4,6},{5,7},{6,4},{7,5},{8,10},{9,11},{10,... | collective-permute-start | bytes 786440 | tf_op jit(solution)/shard_map/ppermute | solution.py:551
  186.6 1.3 copy-start.14
  (9 other events, 7.4 us)
